TPU v7x, 32 devices: a whole 2x2x4 slice. The times are simulated.
32 devices in a mesh: section: 2 (over x), gx: 2 (over core), gy: 2 (over y), dp: 4 (over z).
Axes of the slice: x: 2, y: 2, z: 4, core: 2. Of those that a mesh axis runs over, the one named last changes fastest.
Arguments:
- x_input: bfloat16 [2, 4, 2048, 640], P(None, 'dp', ('gx', 'gy')), may hold values from -6 to 6
- doc_lengths: int32 [2, 4, 8], P(None, 'dp'), may hold values from 0 to 2048, as said below
- cotangent: bfloat16 [2, 4, 2048, 640], P(None, 'dp', ('gx', 'gy')), may hold values from -6 to 6
- gain_attn: float32 [2, 640], P('section'), may hold values from 0.25 to 1.75
- w_query: bfloat16 [2, 640, 1024], P('section', None, 'gy'), may hold values from -0.25 to 0.25
- w_key: bfloat16 [2, 640, 256], P('section'), may hold values from -0.25 to 0.25
- w_value: bfloat16 [2, 640, 256], P('section'), may hold values from -0.25 to 0.25
- w_out: bfloat16 [2, 1024, 640], P('section', 'gy'), may hold values from -1.5 to 1.5
- gain_ff: float32 [2, 640], P('section'), may hold values from 0.25 to 1.75
- w_gate: bfloat16 [2, 640, 2048], P('section', None, 'gy'), may hold values from -0.25 to 0.25
- w_up: bfloat16 [2, 640, 2048], P('section', None, 'gy'), may hold values from -0.25 to 0.25
- w_down: bfloat16 [2, 2048, 640], P('section', 'gy'), may hold values from -0.125 to 0.125
Outputs:
- hidden_states: bfloat16 [2, 2, 4, 2048, 640], P('section', None, 'dp', ('gx', 'gy'))
- input_grads: bfloat16 [2, 2, 4, 2048, 640], P('section', None, 'dp', ('gx', 'gy'))
- gain_attn_grad: float32 [2, 640], P('section')
- query_grad: float32 [2, 640, 1024], P('section', None, 'gy')
- key_grad: float32 [2, 640, 256], P('section')
- value_grad: float32 [2, 640, 256], P('section')
- out_grad: float32 [2, 1024, 640], P('section', 'gy')
- gain_ff_grad: float32 [2, 640], P('section')
- gate_grad: float32 [2, 640, 2048], P('section', None, 'gy')
- up_grad: float32 [2, 640, 2048], P('section', None, 'gy')
- down_grad: float32 [2, 2048, 640], P('section', 'gy')
Inputs may be any that keep to these rules, and one draw needn't show every extreme that they name: `doc_lengths`: each slot's lengths sum to at most 2048; zero lengths occur.
All inputs are finite; a program needn't handle non-finite values.
Results may differ from a plain program's by a relative error of at most 0.028.
Values may be sent and summed in bfloat16 or wider, within the bound.
No kernel may reach another device: no remote copies, remote signals or barrier semaphores. Data moves between devices by JAX's collectives and lax.ppermute only.
A program may use at most 192 MiB of HBM per device.

v0:
```python
import math

import jax
import jax.numpy as jnp
from jax import lax
from jax.sharding import PartitionSpec as P

HD = 256
WINDOW = 512
MICRO = 2


def from_behind(value, axis, steps):
    count = lax.axis_size(axis)
    leading, last = (max(0, -steps), min(count, count - steps))
    return lax.ppermute(value, axis, [(source, source + steps) for source in range(leading, last)])


def rms_scale(value, gain):
    return value * lax.rsqrt(jnp.mean(value * value, axis=-1, keepdims=True) + 1e-06) * gain


def rotate(value, cosine_part, sine_part):
    half_width = value.shape[-1] // 2
    first_half = value[..., :half_width]
    second_half = value[..., half_width:]
    return jnp.concatenate(
        [
            first_half * cosine_part - second_half * sine_part,
            second_half * cosine_part + first_half * sine_part,
        ],
        axis=-1,
    )


def unrotate(grad_value, cosine_part, sine_part):
    half_width = grad_value.shape[-1] // 2
    first_half = grad_value[..., :half_width]
    second_half = grad_value[..., half_width:]
    return jnp.concatenate(
        [
            first_half * cosine_part + second_half * sine_part,
            second_half * cosine_part - first_half * sine_part,
        ],
        axis=-1,
    )


def doc_layout(lengths, slot_rows):
    doc_count = lengths.shape[0]
    doc_ends = jnp.cumsum(lengths)
    starts = doc_ends - lengths
    row_place = jnp.arange(slot_rows, dtype=jnp.int32)
    doc_number = jnp.sum((row_place[:, None] >= doc_ends[None, :]).astype(jnp.int32), axis=1)
    valid_rows = doc_number < doc_count
    doc_begin = jnp.sum(
        jnp.where(
            doc_number[:, None] == jnp.arange(doc_count, dtype=jnp.int32)[None, :],
            starts[None, :],
            0,
        ),
        axis=1,
    )
    where_in = jnp.where(valid_rows, row_place - doc_begin, 0)
    segment = jnp.where(valid_rows, doc_number, doc_count + row_place)
    return (segment, where_in, valid_rows)


def rope_tables(where_in):
    half_width = HD // 2
    frequency = jnp.exp(jnp.arange(half_width, dtype=jnp.float32) * (-2.0 * math.log(10000.0) / HD))
    angles = where_in.astype(jnp.float32)[:, None] * frequency[None, :]
    return (jnp.cos(angles), jnp.sin(angles))


def spread_rows(normed):
    return lax.all_gather(normed, "gy", axis=0, tiled=True)


def spread_grad(grad_rows):
    return lax.all_gather(grad_rows, "gy", axis=0, tiled=True)


def project_back(left, weight):
    return lax.psum_scatter(
        jnp.dot(left, weight, preferred_element_type=jnp.float32).astype(jnp.bfloat16),
        "gy",
        scatter_dimension=0,
        tiled=True,
    ).astype(jnp.float32)


def local_back(pairs):
    summed = None
    for left, weight in pairs:
        piece = jnp.einsum("rc,dc->rd", left, weight, preferred_element_type=jnp.float32)
        summed = piece if summed is None else summed + piece
    return summed


def gather_back(pairs):
    return lax.psum_scatter(
        local_back([(left, weight) for left, weight in pairs]).astype(jnp.bfloat16),
        "gy",
        scatter_dimension=0,
        tiled=True,
    ).astype(jnp.float32)


def block_mask(seg_query, seg_key, block_rows):
    distance = (
        jnp.arange(block_rows, dtype=jnp.int32)[:, None]
        + WINDOW
        - jnp.arange(WINDOW + block_rows, dtype=jnp.int32)[None, :]
    )
    return (distance >= 0) & (distance < WINDOW) & (seg_query[:, None] == seg_key[None, :])


def padded(key_rows, value_rows, segment):
    pad_keys = jnp.concatenate(
        [jnp.zeros((WINDOW, key_rows.shape[1]), key_rows.dtype), key_rows], axis=0
    )
    pad_values = jnp.concatenate(
        [jnp.zeros((WINDOW, value_rows.shape[1]), value_rows.dtype), value_rows], axis=0
    )
    pad_segment = jnp.concatenate([jnp.full((WINDOW,), -1, jnp.int32), segment])
    return (pad_keys, pad_values, pad_segment)


def attend(queries, key_rows, value_rows, segment, seg_query, base_row):
    group_rows = queries.shape[0]
    block_rows = min(512, group_rows)
    pad_keys, pad_values, pad_segment = padded(key_rows, value_rows, segment)

    def one_block(number):
        offset = number * block_rows
        at_row = base_row + offset
        q_block = lax.dynamic_slice_in_dim(queries, offset, block_rows, 0)
        k_block = lax.dynamic_slice_in_dim(pad_keys, at_row, WINDOW + block_rows, 0)
        v_block = lax.dynamic_slice_in_dim(pad_values, at_row, WINDOW + block_rows, 0)
        allowed = block_mask(
            lax.dynamic_slice_in_dim(seg_query, offset, block_rows, 0),
            lax.dynamic_slice_in_dim(pad_segment, at_row, WINDOW + block_rows, 0),
            block_rows,
        )
        scores = jnp.einsum("qhd,kd->hqk", q_block, k_block, preferred_element_type=jnp.float32)
        scores = jnp.where(allowed[None], scores, -1e30)
        row_max = jnp.max(scores, axis=-1, keepdims=True)
        weights = jnp.exp(scores - row_max)
        summed = jnp.sum(weights, axis=-1, keepdims=True)
        probability = (weights / summed).astype(jnp.bfloat16)
        mixed_heads = jnp.einsum(
            "hqk,kd->qhd", probability, v_block, preferred_element_type=jnp.float32
        )
        return (mixed_heads.astype(jnp.bfloat16), (row_max + jnp.log(summed))[..., 0])

    mixed_heads, log_total = lax.map(
        one_block, jnp.arange(group_rows // block_rows, dtype=jnp.int32)
    )
    return (mixed_heads.reshape(group_rows, -1), log_total)


def attend_back(grad_mixed, queries, key_rows, value_rows, log_total, segment, seg_query, base_row):
    group_rows, heads_here, _ = queries.shape
    block_rows = min(512, group_rows)
    grad_mixed = grad_mixed.reshape(group_rows, heads_here, HD)
    pad_keys, pad_values, pad_segment = padded(key_rows, value_rows, segment)

    def one_block(carry, slot_item):
        pad_grad_keys, pad_grad_values = carry
        number, log_block = slot_item
        offset = number * block_rows
        at_row = base_row + offset
        q_block = lax.dynamic_slice_in_dim(queries, offset, block_rows, 0)
        g_block = lax.dynamic_slice_in_dim(grad_mixed, offset, block_rows, 0)
        k_block = lax.dynamic_slice_in_dim(pad_keys, at_row, WINDOW + block_rows, 0)
        v_block = lax.dynamic_slice_in_dim(pad_values, at_row, WINDOW + block_rows, 0)
        allowed = block_mask(
            lax.dynamic_slice_in_dim(seg_query, offset, block_rows, 0),
            lax.dynamic_slice_in_dim(pad_segment, at_row, WINDOW + block_rows, 0),
            block_rows,
        )
        scores = jnp.einsum("qhd,kd->hqk", q_block, k_block, preferred_element_type=jnp.float32)
        scores = jnp.where(allowed[None], scores, -1e30)
        probability = jnp.exp(scores - log_block[..., None])
        grad_prob = jnp.einsum("qhd,kd->hqk", g_block, v_block, preferred_element_type=jnp.float32)
        grad_scores = (
            probability * (grad_prob - jnp.sum(probability * grad_prob, axis=-1, keepdims=True))
        ).astype(jnp.bfloat16)
        grad_queries = jnp.einsum(
            "hqk,kd->qhd", grad_scores, k_block, preferred_element_type=jnp.float32
        )
        grad_keys = jnp.einsum(
            "hqk,qhd->kd", grad_scores, q_block, preferred_element_type=jnp.float32
        )
        grad_values = jnp.einsum(
            "hqk,qhd->kd",
            probability.astype(jnp.bfloat16),
            g_block,
            preferred_element_type=jnp.float32,
        )
        pad_grad_keys = lax.dynamic_update_slice_in_dim(
            pad_grad_keys,
            lax.dynamic_slice_in_dim(pad_grad_keys, at_row, WINDOW + block_rows, 0) + grad_keys,
            at_row,
            0,
        )
        pad_grad_values = lax.dynamic_update_slice_in_dim(
            pad_grad_values,
            lax.dynamic_slice_in_dim(pad_grad_values, at_row, WINDOW + block_rows, 0) + grad_values,
            at_row,
            0,
        )
        return ((pad_grad_keys, pad_grad_values), grad_queries)

    slot_rows = key_rows.shape[0]
    start_grads = (
        jnp.zeros((WINDOW + slot_rows, HD), jnp.float32),
        jnp.zeros((WINDOW + slot_rows, HD), jnp.float32),
    )
    numbers = jnp.arange(group_rows // block_rows, dtype=jnp.int32)
    (pad_grad_keys, pad_grad_values), grad_queries = lax.scan(
        one_block, start_grads, (numbers, log_total)
    )
    return (
        grad_queries.reshape(group_rows, heads_here, HD),
        pad_grad_keys[WINDOW:],
        pad_grad_values[WINDOW:],
    )


def forward_layer(inputs, lengths, weights, quarter, half_index):
    gain_attn, w_query, w_key, w_value, w_out, gain_ff, w_gate, w_up, w_down = weights
    own_rows = inputs.shape[0]
    group_rows = own_rows * lax.axis_size("gy")
    slot_rows = group_rows * lax.axis_size("gx")
    segment, where_in, valid_rows = doc_layout(lengths, slot_rows)
    cosine_part, sine_part = rope_tables(where_in)
    own_start = quarter * own_rows
    query_start = half_index * group_rows
    cos_query = lax.dynamic_slice_in_dim(cosine_part, query_start, group_rows, 0)
    sin_query = lax.dynamic_slice_in_dim(sine_part, query_start, group_rows, 0)
    cos_key = lax.dynamic_slice_in_dim(cosine_part, own_start, own_rows, 0)
    sin_key = lax.dynamic_slice_in_dim(sine_part, own_start, own_rows, 0)
    seg_query = lax.dynamic_slice_in_dim(segment, query_start, group_rows, 0)
    valid_own = lax.dynamic_slice_in_dim(valid_rows, own_start, own_rows, 0).astype(jnp.float32)
    normed = rms_scale(inputs, gain_attn).astype(jnp.bfloat16)
    gathered = spread_rows(normed)
    heads_here = w_query.shape[1] // HD
    q_raw = jnp.dot(gathered, w_query, preferred_element_type=jnp.float32).reshape(
        group_rows, heads_here, HD
    )
    queries = (rotate(q_raw, cos_query[:, None, :], sin_query[:, None, :]) * HD ** (-0.5)).astype(
        jnp.bfloat16
    )
    key_part = rotate(
        jnp.dot(normed, w_key, preferred_element_type=jnp.float32), cos_key, sin_key
    ).astype(jnp.bfloat16)
    value_part = jnp.dot(normed, w_value, preferred_element_type=jnp.float32).astype(jnp.bfloat16)
    key_rows, value_rows = (
        lax.all_gather(key_part, ("gx", "gy"), axis=0, tiled=True),
        lax.all_gather(value_part, ("gx", "gy"), axis=0, tiled=True),
    )
    mixed_heads, log_total = attend(queries, key_rows, value_rows, segment, seg_query, query_start)
    hidden = inputs + project_back(mixed_heads, w_out)
    normed_ff = rms_scale(hidden, gain_ff).astype(jnp.bfloat16)
    gathered_ff = spread_rows(normed_ff)
    gate_value = jnp.dot(gathered_ff, w_gate, preferred_element_type=jnp.float32)
    up_value = jnp.dot(gathered_ff, w_up, preferred_element_type=jnp.float32)
    activated = (jax.nn.gelu(gate_value, approximate=True) * up_value).astype(jnp.bfloat16)
    output = hidden + project_back(activated, w_down)
    kept = {
        "inputs": inputs,
        "hidden": hidden,
        "normed": normed,
        "gathered": gathered,
        "queries": queries,
        "key_rows": key_rows,
        "value_rows": value_rows,
        "mixed_heads": mixed_heads,
        "log_total": log_total,
        "gathered_ff": gathered_ff,
        "gate_value": gate_value,
        "up_value": up_value,
        "activated": activated,
        "segment": segment,
        "seg_query": seg_query,
        "cos_query": cos_query,
        "sin_query": sin_query,
        "cos_key": cos_key,
        "sin_key": sin_key,
        "group_start": query_start,
        "valid_rows": valid_own,
    }
    return (output, kept)


def backward_layer(grad_out, kept, weights):
    gain_attn, w_query, w_key, w_value, w_out, gain_ff, w_gate, w_up, w_down = weights
    grad_branch = spread_grad(grad_out.astype(jnp.bfloat16))
    grad_w_down = jnp.einsum(
        "rf,rd->fd", kept["activated"], grad_branch, preferred_element_type=jnp.float32
    )
    grad_act = jnp.einsum("rd,fd->rf", grad_branch, w_down, preferred_element_type=jnp.float32)
    _, pullback = jax.vjp(
        lambda a, b: jax.nn.gelu(a, approximate=True) * b, kept["gate_value"], kept["up_value"]
    )
    grad_gate, grad_up = pullback(grad_act)
    grad_gate = grad_gate.astype(jnp.bfloat16)
    grad_up = grad_up.astype(jnp.bfloat16)
    grad_w_gate = jnp.einsum(
        "rd,rf->df", kept["gathered_ff"], grad_gate, preferred_element_type=jnp.float32
    )
    grad_w_up = jnp.einsum(
        "rd,rf->df", kept["gathered_ff"], grad_up, preferred_element_type=jnp.float32
    )
    grad_normed_ff = gather_back([(grad_gate, w_gate), (grad_up, w_up)])
    _, pullback = jax.vjp(rms_scale, kept["hidden"], gain_ff)
    grad_hidden_norm, grad_gain_ff = pullback(grad_normed_ff)
    grad_hidden = grad_out + grad_hidden_norm
    grad_attn = spread_grad(grad_hidden.astype(jnp.bfloat16))
    grad_w_out = jnp.einsum(
        "rc,rd->cd", kept["mixed_heads"], grad_attn, preferred_element_type=jnp.float32
    )
    grad_mixed = jnp.einsum(
        "rd,cd->rc", grad_attn, w_out, preferred_element_type=jnp.float32
    ).astype(jnp.bfloat16)
    grad_queries, grad_keys, grad_values = attend_back(
        grad_mixed,
        kept["queries"],
        kept["key_rows"],
        kept["value_rows"],
        kept["log_total"],
        kept["segment"],
        kept["seg_query"],
        kept["group_start"],
    )
    query_rows = grad_queries.shape[0]
    grad_q_raw = (
        (
            unrotate(grad_queries, kept["cos_query"][:, None, :], kept["sin_query"][:, None, :])
            * HD ** (-0.5)
        )
        .astype(jnp.bfloat16)
        .reshape(query_rows, -1)
    )
    grad_w_query = jnp.einsum(
        "rd,rc->dc", kept["gathered"], grad_q_raw, preferred_element_type=jnp.float32
    )
    own_keys, own_values = (
        lax.psum_scatter(
            grad_keys.astype(jnp.bfloat16), ("gx", "gy"), scatter_dimension=0, tiled=True
        ).astype(jnp.float32),
        lax.psum_scatter(
            grad_values.astype(jnp.bfloat16), ("gx", "gy"), scatter_dimension=0, tiled=True
        ).astype(jnp.float32),
    )
    grad_k_raw = unrotate(own_keys, kept["cos_key"], kept["sin_key"]).astype(jnp.bfloat16)
    grad_v_raw = own_values.astype(jnp.bfloat16)
    grad_w_key = jnp.einsum(
        "rd,rc->dc", kept["normed"], grad_k_raw, preferred_element_type=jnp.float32
    )
    grad_w_value = jnp.einsum(
        "rd,rc->dc", kept["normed"], grad_v_raw, preferred_element_type=jnp.float32
    )
    query_term = gather_back([(grad_q_raw, w_query)])
    grad_normed = (
        query_term
        + jnp.einsum("rc,dc->rd", grad_k_raw, w_key, preferred_element_type=jnp.float32)
        + jnp.einsum("rc,dc->rd", grad_v_raw, w_value, preferred_element_type=jnp.float32)
    )
    _, pullback = jax.vjp(rms_scale, kept["inputs"], gain_attn)
    grad_input_norm, grad_gain_attn = pullback(grad_normed)
    grad_inputs = grad_hidden + grad_input_norm
    return (
        grad_inputs,
        (
            grad_gain_attn,
            grad_w_query,
            grad_w_key,
            grad_w_value,
            grad_w_out,
            grad_gain_ff,
            grad_w_gate,
            grad_w_up,
            grad_w_down,
        ),
    )


def local(
    x_input,
    doc_lengths,
    cotangent,
    gain_attn,
    w_query,
    w_key,
    w_value,
    w_out,
    gain_ff,
    w_gate,
    w_up,
    w_down,
):
    weights = tuple(
        (a[0] for a in (gain_attn, w_query, w_key, w_value, w_out, gain_ff, w_gate, w_up, w_down))
    )
    section_first = lax.axis_index("section") == 0
    half_index = lax.axis_index("gx")
    quarter = half_index * lax.axis_size("gy") + lax.axis_index("gy")
    own_rows = x_input.shape[2]
    width_here = x_input.shape[3]
    blank = jnp.zeros((own_rows, width_here), jnp.bfloat16)
    received = blank
    kept_all = []
    outputs = []
    for moment in range(MICRO + 1):
        lengths = jnp.where(
            section_first,
            doc_lengths[min(moment, MICRO - 1), 0],
            doc_lengths[max(moment - 1, 0), 0],
        )
        fresh = x_input[moment, 0] if moment < MICRO else blank
        inputs = jnp.where(section_first, fresh, received).astype(jnp.float32)
        output, kept = forward_layer(inputs, lengths, weights, quarter, half_index)
        sent = output.astype(jnp.bfloat16)
        outputs.append(sent)
        kept_all.append(kept)
        if moment < MICRO:
            received = from_behind(sent, "section", 1)
    returned = blank
    back_list = []
    grid_total = None
    shared_total = None
    for reverse_step in range(MICRO + 1):
        kept = kept_all[MICRO - reverse_step]
        if reverse_step < MICRO:
            fresh_grad = (
                cotangent[MICRO - 1 - reverse_step, 0].astype(jnp.float32)
                * kept["valid_rows"][:, None]
            )
        else:
            fresh_grad = jnp.zeros((own_rows, width_here), jnp.float32)
        grad_out = jnp.where(section_first, returned.astype(jnp.float32), fresh_grad)
        grad_inputs, grads = backward_layer(grad_out, kept, weights)
        sent_grad = grad_inputs.astype(jnp.bfloat16)
        back_list.append(sent_grad)
        if reverse_step < MICRO:
            returned = from_behind(sent_grad, "section", -1)
        grid_part = (grads[1], grads[6], grads[7], grads[4], grads[8])
        shared_part = (grads[0], grads[2], grads[3], grads[5])
        grid_total = (
            grid_part
            if grid_total is None
            else tuple((a + b for a, b in zip(grid_total, grid_part)))
        )
        shared_total = (
            shared_part
            if shared_total is None
            else tuple((a + b for a, b in zip(shared_total, shared_part)))
        )
    grid_total = lax.psum(
        (grid_total[0], grid_total[1], grid_total[2], grid_total[3], grid_total[4]), ("gx", "dp")
    )
    shared_total = lax.psum(
        (shared_total[0], shared_total[1], shared_total[2], shared_total[3]), ("gx", "gy", "dp")
    )
    scale = 1.0 / lax.axis_size("dp")
    hidden_states = jnp.where(section_first, jnp.stack(outputs[:MICRO]), jnp.stack(outputs[1:]))[
        None, :, None
    ]
    later_grads = jnp.stack([back_list[MICRO - 1 - k] for k in range(MICRO)])
    earlier_grads = jnp.stack([back_list[MICRO - k] for k in range(MICRO)])
    input_grads = jnp.where(section_first, earlier_grads, later_grads)[None, :, None]
    return (
        hidden_states,
        input_grads,
        (shared_total[0] * scale)[None],
        (grid_total[0] * scale)[None],
        (shared_total[1] * scale)[None],
        (shared_total[2] * scale)[None],
        (grid_total[3] * scale)[None],
        (shared_total[3] * scale)[None],
        (grid_total[1] * scale)[None],
        (grid_total[2] * scale)[None],
        (grid_total[4] * scale)[None],
    )


def solution(mesh):
    return jax.shard_map(
        local,
        mesh=mesh,
        in_specs=(
            P(None, "dp", ("gx", "gy"), None),
            P(None, "dp", None),
            P(None, "dp", ("gx", "gy"), None),
            P("section", None),
            P("section", None, "gy"),
            P("section", None, None),
            P("section", None, None),
            P("section", "gy", None),
            P("section", None),
            P("section", None, "gy"),
            P("section", None, "gy"),
            P("section", "gy", None),
        ),
        out_specs=(
            P("section", None, "dp", ("gx", "gy"), None),
            P("section", None, "dp", ("gx", "gy"), None),
            P("section", None),
            P("section", None, "gy"),
            P("section", None, None),
            P("section", None, None),
            P("section", "gy", None),
            P("section", None),
            P("section", None, "gy"),
            P("section", None, "gy"),
            P("section", "gy", None),
        ),
        check_vma=False,
    )
```

profile of v0, /device:TPU:0, one launch (start us, length us, event | category | flops | bytes accessed | tf_op | source)
XLA Modules:
  0.0 1808.4 jit_solution(11891280993728470318)
XLA Ops:
  81.1 24.3 %while.78 = (s32[]{:T(128)}, bf16[2,512,2,256]{3,2,1,0:T(2,128)(2,1)}, f32[2,2,512]{2,1,0:T(2,128)}, s32[2]{0:T(128)S(1)}, s32[]{:T(128)}, /*index=5*/bf16[2560,...) while((s32[]{:T(128)}, ...), condition=%wide.region_7.8_spmd, body=%wide.region_4.7_spmd.sunk | while | flops 1086586368 | bytes 18930952 | solution.py:157
  137.0 24.4 %all-gather.25.cloned.1.call-done = bf16[1024,640]{1,0:T(8,128)(2,1)} async-done(((bf16[512,640]{1,0:T(8,128)(2,1)}), bf16[1024,640]{1,0:T(8,128)(2,1)}) %all-gather.25.cloned.1.call-update) | async-done | bytes 1310736 | tf_op jit(solution)/shard_map/all_gather | solution.py:77
  173.4 23.3 %reduce-scatter.21.cloned.1.call-done = bf16[512,640]{1,0:T(8,128)(2,1)} async-done(((bf16[1024,640]{1,0:T(8,128)(2,1)}), bf16[512,640]{1,0:T(8,128)(2,1)}) %reduce-scatter.21.cloned.1.call-update) | async-done | bytes 655376 | tf_op jit(solution)/shard_map/reduce_scatter | solution.py:85
  307.0 23.3 %reduce-scatter.23.cloned.1.call-done = bf16[512,640]{1,0:T(8,128)(2,1)} async-done(((bf16[1024,640]{1,0:T(8,128)(2,1)}), bf16[512,640]{1,0:T(8,128)(2,1)}) %reduce-scatter.23.cloned.1.call-update) | async-done | bytes 655376 | tf_op jit(solution)/shard_map/reduce_scatter | solution.py:85
  334.4 23.9 %all-gather.33.cloned.1.call-done = bf16[1024,640]{1,0:T(8,128)(2,1)} async-done(((bf16[512,640]{1,0:T(8,128)(2,1)}), bf16[1024,640]{1,0:T(8,128)(2,1)}) %all-gather.33.cloned.1.call-update) | async-done | bytes 1310736 | tf_op jit(solution)/shard_map/all_gather | solution.py:77
  369.9 23.3 %reduce-scatter.25.cloned.1.call-done = bf16[512,640]{1,0:T(8,128)(2,1)} async-done(((bf16[1024,640]{1,0:T(8,128)(2,1)}), bf16[512,640]{1,0:T(8,128)(2,1)}) %reduce-scatter.25.cloned.1.call-update) | async-done | bytes 655376 | tf_op jit(solution)/shard_map/reduce_scatter | solution.py:85
  480.1 24.0 %while.80 = (s32[]{:T(128)}, bf16[2,512,2,256]{3,2,1,0:T(2,128)(2,1)}, f32[2,2,512]{2,1,0:T(2,128)}, s32[2]{0:T(128)S(1)}, s32[]{:T(128)}, /*index=5*/bf16[2560,...) while((s32[]{:T(128)}, ...), condition=%wide.region_29.30_spmd, body=%wide.region_26.29_spmd.sunk | while | flops 1086586368 | bytes 18930952 | solution.py:157
  599.9 23.3 %reduce-scatter.31.cloned.1.call-done = bf16[512,640]{1,0:T(8,128)(2,1)} async-done(((bf16[1024,640]{1,0:T(8,128)(2,1)}), bf16[512,640]{1,0:T(8,128)(2,1)}) %reduce-scatter.31.cloned.1.call-update) | async-done | bytes 655376 | tf_op jit(solution)/shard_map/reduce_scatter | solution.py:102
  629.6 24.0 %all-gather.45.cloned.1.call-done = bf16[1024,640]{1,0:T(8,128)(2,1)} async-done(((bf16[512,640]{1,0:T(8,128)(2,1)}), bf16[1024,640]{1,0:T(8,128)(2,1)}) %all-gather.45.cloned.1.call-update) | async-done | bytes 1310736 | tf_op jit(solution)/shard_map/all_gather | solution.py:81
  662.9 99.9 %while.81 = (s32[]{:T(128)}, f32[2560,256]{0,1:T(8,128)}, f32[2560,256]{1,0:T(8,128)}, f32[2,512,2,256]{1,0,3,2:T(2,128)}, s32[2]{0:T(128)}, /*index=5*/s32[]{:T...) while((s32[]{:T(128)}, f32[2560,256]{0,1:T(8,128)}, ...), condition=%wide.region_37.38_spmd, body=%wide.region_35.37_spmd.sunk | while | flops 2700606976 | bytes 84462016 | solution.py:222
  793.1 23.9 %reduce-scatter.33.cloned.1.call-done = bf16[512,640]{1,0:T(8,128)(2,1)} async-done(((bf16[1024,640]{1,0:T(8,128)(2,1)}), bf16[512,640]{1,0:T(8,128)(2,1)}) %reduce-scatter.33.cloned.1.call-update) | async-done | bytes 655376 | tf_op jit(solution)/shard_map/reduce_scatter | solution.py:102
  819.5 25.4 %reduce-scatter.37.cloned.1.call-done = bf16[512,256]{1,0:T(8,128)(2,1)} async-done(((bf16[2048,256]{1,0:T(8,128)(2,1)}), bf16[512,256]{1,0:T(8,128)(2,1)}) %reduce-scatter.37.cloned.1.call-update) | async-done | bytes 262160 | tf_op jit(solution)/shard_map/reduce_scatter | solution.py:354
  893.7 23.5 %all-gather.47.cloned.1.call-done = bf16[1024,640]{1,0:T(8,128)(2,1)} async-done(((bf16[512,640]{1,0:T(8,128)(2,1)}), bf16[1024,640]{1,0:T(8,128)(2,1)}) %all-gather.47.cloned.1.call-update) | async-done | bytes 1310736 | tf_op jit(solution)/shard_map/all_gather | solution.py:81
  930.2 23.1 %reduce-scatter.39.cloned.1.call-done = bf16[512,640]{1,0:T(8,128)(2,1)} async-done(((bf16[1024,640]{1,0:T(8,128)(2,1)}), bf16[512,640]{1,0:T(8,128)(2,1)}) %reduce-scatter.39.cloned.1.call-update) | async-done | bytes 655376 | tf_op jit(solution)/shard_map/reduce_scatter | solution.py:102
  957.8 24.4 %all-gather.49.cloned.1.call-done = bf16[1024,640]{1,0:T(8,128)(2,1)} async-done(((bf16[512,640]{1,0:T(8,128)(2,1)}), bf16[1024,640]{1,0:T(8,128)(2,1)}) %all-gather.49.cloned.1.call-update) | async-done | bytes 1310736 | tf_op jit(solution)/shard_map/all_gather | solution.py:81
  990.9 97.6 %while.82 = (s32[]{:T(128)}, f32[2560,256]{0,1:T(8,128)}, f32[2560,256]{1,0:T(8,128)}, f32[2,512,2,256]{1,0,3,2:T(2,128)}, s32[2]{0:T(128)S(1)}, /*index=5*/s32[...) while((s32[]{:T(128)}, f32[2560,256]{0,1:T(8,128)}, ...), condition=%wide.region_46.47_spmd, body=%wide.region_44.46_spmd.sunk | while | flops 2700606976 | bytes 76073368 | solution.py:222
  1118.7 23.8 %reduce-scatter.41.cloned.1.call-done = bf16[512,640]{1,0:T(8,128)(2,1)} async-done(((bf16[1024,640]{1,0:T(8,128)(2,1)}), bf16[512,640]{1,0:T(8,128)(2,1)}) %reduce-scatter.41.cloned.1.call-update) | async-done | bytes 655376 | tf_op jit(solution)/shard_map/reduce_scatter | solution.py:102
  1145.1 25.5 %reduce-scatter.45.cloned.1.call-done = bf16[512,256]{1,0:T(8,128)(2,1)} async-done(((bf16[2048,256]{1,0:T(8,128)(2,1)}), bf16[512,256]{1,0:T(8,128)(2,1)}) %reduce-scatter.45.cloned.1.call-update) | async-done | bytes 262160 | tf_op jit(solution)/shard_map/reduce_scatter | solution.py:354
  1193.9 23.5 %all-gather.51.cloned.1.call-done = bf16[1024,640]{1,0:T(8,128)(2,1)} async-done(((bf16[512,640]{1,0:T(8,128)(2,1)}), bf16[1024,640]{1,0:T(8,128)(2,1)}) %all-gather.51.cloned.1.call-update) | async-done | bytes 1310736 | tf_op jit(solution)/shard_map/all_gather | solution.py:81
  1230.2 23.3 %reduce-scatter.47.cloned.1.call-done = bf16[512,640]{1,0:T(8,128)(2,1)} async-done(((bf16[1024,640]{1,0:T(8,128)(2,1)}), bf16[512,640]{1,0:T(8,128)(2,1)}) %reduce-scatter.47.cloned.1.call-update) | async-done | bytes 655376 | tf_op jit(solution)/shard_map/reduce_scatter | solution.py:102
  1291.0 99.6 %while.83 = (s32[]{:T(128)}, f32[2560,256]{0,1:T(8,128)}, f32[2560,256]{1,0:T(8,128)}, f32[2,512,2,256]{1,0,3,2:T(2,128)}, s32[2]{0:T(128)}, /*index=5*/s32[]{:T...) while((s32[]{:T(128)}, f32[2560,256]{0,1:T(8,128)}, ...), condition=%wide.region_55.56_spmd, body=%wide.region_53.55_spmd.sunk | while | flops 2700606976 | bytes 76073368 | solution.py:222
  1476.7 35.1 %all-reduce.9 = (f32[640]{0:T(1024)S(1)}, f32[640]{0:T(1024)S(1)}) all-reduce(f32[640]{0:T(1024)S(1)} %add_add_fusion.10, f32[640]{0:T(1024)} %add_add_fusion.9), channel_id=1, replica_groups=mesh['section'=2,'gx'=2,'gy'=2,'dp'=4] {'gx','gy','dp'}, use_global_device_ids=true, to_apply=%region_63.64 | all-reduce | flops 1280 | bytes 10240 | tf_op jit(solution)/shard_map/psum | solution.py:465
  1517.7 52.6 %all-reduce.15.cloned.1.call-done = (f32[640,256]{1,0:T(8,128)}, f32[640,256]{1,0:T(8,128)}) async-done(((f32[640,256]{1,0:T(8,128)}, f32[640,256]{1,0:T(8,128)}), (f32[640,256]{1,0:T(8,128)}, f32[640,256]{1,0:T(8,128)})) %all-reduce.15.cloned.1.call-update) | async-done | bytes 1310736 | tf_op jit(solution)/shard_map/psum | solution.py:465
  1574.2 216.5 %all-reduce.17.cloned.1.call-done = (f32[640,512]{1,0:T(8,128)}, f32[512,640]{1,0:T(8,128)}, f32[640,1024]{1,0:T(8,128)}, f32[640,1024]{1,0:T(8,128)}, f32[1024,640]{1,0:T(8,128)}) async-done(((f32[640,512]{1,0:T(8,128)}, f32[512,640]{1,0:T(8,128)}, f32[640,1024]{1,0:T(8,128)}, f32[640,1024]{1,0:T(8,128)}, f32[1024,640]{1,0:T(8,128)}), (f32[640,512]{1,0:T(8,128)}, f32[512,640]{1,0:T(8,128)}, ...) | async-done | bytes 10485776 | tf_op jit(solution)/shard_map/psum | solution.py:462
  (915 shorter events, 1115.9 us)
Async XLA Ops:
  30.3 103.0 %reduce-scatter.19.cloned.1.call-start = ((), (), s32[]{:S(2)}) async-start(), calls=%async_computation.21 | async-start | bytes 1966080 | tf_op jit(solution)/shard_map/reduce_scatter | solution.py:85
  136.9 59.8 %reduce-scatter.21.cloned.1.call-start = ((), (), s32[]{:S(2)}) async-start(), calls=%async_computation.23 | async-start | bytes 1966080 | tf_op jit(solution)/shard_map/reduce_scatter | solution.py:85
  173.4 69.0 %all-gather.31.cloned.1.call-start = ((), (), s32[]{:S(2)}) async-start(), calls=%async_computation.26 | async-start | bytes 1966080 | tf_op jit(solution)/shard_map/all_gather | solution.py:77
  220.5 59.6 %all-gather.27.cloned.1.call-start = ((), (), s32[]{:S(2)}) async-start(), calls=%async_computation.24 | async-start | bytes 1310720 | tf_op jit(solution)/shard_map/all_gather | solution.py:262
  222.7 107.6 %reduce-scatter.23.cloned.1.call-start = ((), (), s32[]{:S(2)}) async-start(), calls=%async_computation.27 | async-start | bytes 1966080 | tf_op jit(solution)/shard_map/reduce_scatter | solution.py:85
  333.9 59.3 %reduce-scatter.25.cloned.1.call-start = ((), (), s32[]{:S(2)}) async-start(), calls=%async_computation.29 | async-start | bytes 1966080 | tf_op jit(solution)/shard_map/reduce_scatter | solution.py:85
  369.9 68.8 %all-gather.39.cloned.1.call-start = ((), (), s32[]{:S(2)}) async-start(), calls=%async_computation.32 | async-start | bytes 1966080 | tf_op jit(solution)/shard_map/all_gather | solution.py:77
  416.9 58.8 %all-gather.35.cloned.1.call-start = ((), (), s32[]{:S(2)}) async-start(), calls=%async_computation.30 | async-start | bytes 1310720 | tf_op jit(solution)/shard_map/all_gather | solution.py:262
  418.1 114.0 %reduce-scatter.27.cloned.1.call-start = ((), (), s32[]{:S(2)}) async-start(), calls=%async_computation.33 | async-start | bytes 1966080 | tf_op jit(solution)/shard_map/reduce_scatter | solution.py:85
  511.6 73.0 %all-gather.41.cloned.1.call-start = ((), (), s32[]{:S(2)}) async-start(), calls=%async_computation.34 | async-start | bytes 1966080 | tf_op jit(solution)/shard_map/all_gather | solution.py:77
  535.7 87.4 %reduce-scatter.31.cloned.1.call-start = ((), (), s32[]{:S(2)}) async-start(), calls=%async_computation.37 | async-start | bytes 1966080 | tf_op jit(solution)/shard_map/reduce_scatter | solution.py:102
  629.1 161.7 %reduce-scatter.35.cloned.1.call-start = ((), (), s32[]{:S(2)}) async-start(), calls=%async_computation.40 | async-start | bytes 1310720 | tf_op jit(solution)/shard_map/reduce_scatter | solution.py:351
  774.4 70.6 %reduce-scatter.37.cloned.1.call-start = ((), (), s32[]{:S(2)}) async-start(), calls=%async_computation.41 | async-start | bytes 1310720 | tf_op jit(solution)/shard_map/reduce_scatter | solution.py:354
  777.2 93.7 %reduce-scatter.29.cloned.1.call-start = ((), (), s32[]{:S(2)}) async-start(), calls=%async_computation.35 | async-start | bytes 1966080 | tf_op jit(solution)/shard_map/reduce_scatter | solution.py:85
  780.2 137.0 %all-gather.47.cloned.1.call-start = ((), (), s32[]{:S(2)}) async-start(), calls=%async_computation.42 | async-start | bytes 1966080 | tf_op jit(solution)/shard_map/all_gather | solution.py:81
  893.7 59.6 %reduce-scatter.39.cloned.1.call-start = ((), (), s32[]{:S(2)}) async-start(), calls=%async_computation.43 | async-start | bytes 1966080 | tf_op jit(solution)/shard_map/reduce_scatter | solution.py:102
  957.8 158.7 %reduce-scatter.43.cloned.1.call-start = ((), (), s32[]{:S(2)}) async-start(), calls=%async_computation.46 | async-start | bytes 1310720 | tf_op jit(solution)/shard_map/reduce_scatter | solution.py:351
  1100.2 70.3 %reduce-scatter.45.cloned.1.call-start = ((), (), s32[]{:S(2)}) async-start(), calls=%async_computation.47 | async-start | bytes 1310720 | tf_op jit(solution)/shard_map/reduce_scatter | solution.py:354
  1103.0 114.4 %all-gather.51.cloned.1.call-start = ((), (), s32[]{:S(2)}) async-start(), calls=%async_computation.48 | async-start | bytes 1966080 | tf_op jit(solution)/shard_map/all_gather | solution.py:81
  1193.9 59.6 %reduce-scatter.47.cloned.1.call-start = ((), (), s32[]{:S(2)}) async-start(), calls=%async_computation.49 | async-start | bytes 1966080 | tf_op jit(solution)/shard_map/reduce_scatter | solution.py:102
  1257.5 190.9 %reduce-scatter.51.cloned.1.call-start = ((), (), s32[]{:S(2)}) async-start(), calls=%async_computation.52 | async-start | bytes 1310720 | tf_op jit(solution)/shard_map/reduce_scatter | solution.py:351
  1393.4 59.3 %reduce-scatter.53.cloned.1.call-start = ((), (), s32[]{:S(2)}) async-start(), calls=%async_computation.53 | async-start | bytes 1310720 | tf_op jit(solution)/shard_map/reduce_scatter | solution.py:354
  1433.7 136.6 %all-reduce.15.cloned.1.call-start = ((), (), s32[]{:S(2)}) async-start(), calls=%async_computation.54 | async-start | bytes 2621440 | tf_op jit(solution)/shard_map/psum | solution.py:465
  1458.1 332.6 %all-reduce.17.cloned.1.call-start = ((), (), s32[]{:S(2)}) async-start(), calls=%async_computation.55 | async-start | bytes 20971520 | tf_op jit(solution)/shard_map/psum | solution.py:462
  (227 other events, 4084.5 us)
Sparse Core Ops, SparseCore 0:
  11.8 26.9 all-gather.22
  137.0 24.2 all-gather.24
  217.0 25.2 all-gather.30
  334.0 24.2 all-gather.32
  370.0 23.1 reduce-scatter.24
  413.4 25.2 all-gather.38
  508.8 23.2 reduce-scatter.26
  534.1 24.2 all-gather.42
  560.4 24.2 all-gather.40
  629.2 24.2 all-gather.44
  765.8 24.8 reduce-scatter.34
  793.7 23.1 reduce-scatter.32
  820.0 24.8 reduce-scatter.36
  847.7 23.1 reduce-scatter.28
  893.8 23.3 all-gather.46
  957.9 24.2 all-gather.48
  1091.5 24.8 reduce-scatter.42
  1145.6 24.8 reduce-scatter.44
  1194.0 23.3 all-gather.50
  1257.6 24.2 all-gather.52
  1393.6 24.8 reduce-scatter.50
  1421.0 24.8 reduce-scatter.52
  1475.8 94.3 all-reduce.14
  1574.2 216.5 all-reduce.16
  (14 shorter events, 285.0 us)
where the time goes:
time: 1830 us; the launch traced here: 1810 us
  waiting for transfers between devices  987 us (54%)
  local copies, waits for them, and re-layouts  325 us (18%)
  matrix products  296 us (16%)
  other arithmetic  126 us (7%)
  blocking collectives  35.1 us (2%)
    psum x1, waiting for transfers between devices, local(): lax.psum((grid_total[0], grid_total[1], grid_total[2], grid_total[3], gri...  217 us
    all_gather x6, waiting for transfers between devices, spread_grad(): return lax.all_gather(grad_rows, 'gy', axis=0, tiled=True)  136 us
    reduce_scatter x6, waiting for transfers between devices, project_back(): lax.psum_scatter(jnp.dot(left, weight, preferred_element_type=jnp.float32...  136 us
    dynamic_update_slice x12, local copies, waits for them, and re-layouts, attend_back(): lax.scan(one_block, start_grads, (numbers, log_total))  124 us
    reduce_scatter x6, waiting for transfers between devices, gather_back(): lax.psum_scatter(local_back([(left, weight) for left, weight in pairs]).a...  120 us
    all_gather x6, waiting for transfers between devices, spread_rows(): return lax.all_gather(normed, 'gy', axis=0, tiled=True)  105 us
    ppermute x4, waiting for transfers between devices, from_behind(): lax.ppermute(value, axis, [(source, source + steps) for source in range(l...  61.2 us
    psum x1, waiting for transfers between devices, local(): lax.psum((shared_total[0], shared_total[1], shared_total[2], shared_total...  52.6 us
  transfers between devices with their start and end apart: 42, of which 40 were waited for; matrix products, arithmetic and copies ran while one was open for 11% of the time, Pallas kernels for 0%

commit v1 on v0

v1 whole, which is shorter than its diff:
```python
import math

import jax
import jax.numpy as jnp
from jax import lax
from jax.sharding import PartitionSpec as P

HD = 256
WINDOW = 512
F32 = jnp.float32
BF16 = jnp.bfloat16


def swap(value, axis):
    return lax.ppermute(value, axis, [(0, 1), (1, 0)])


def mm(a, b):
    return jnp.dot(a, b, preferred_element_type=F32)


def mm_t(a, b):
    return lax.dot_general(a, b, (((1,), (1,)), ((), ())), preferred_element_type=F32)


def t_mm(a, b):
    return lax.dot_general(a, b, (((0,), (0,)), ((), ())), preferred_element_type=F32)


def inverse_rms(value):
    return lax.rsqrt(jnp.mean(value * value, axis=-1, keepdims=True) + 1e-06)


def norm_back(value, gain, grad):
    s = inverse_rms(value)
    scaled = grad * gain
    to_value = s * scaled - value * (s * s * s) * jnp.mean(value * scaled, axis=-1, keepdims=True)
    return to_value, jnp.sum(grad * value * s, axis=0)


def rotate(value, cos, sin):
    half = value.shape[-1] // 2
    a, b = value[..., :half], value[..., half:]
    return jnp.concatenate([a * cos - b * sin, b * cos + a * sin], axis=-1)


def unrotate(value, cos, sin):
    half = value.shape[-1] // 2
    c, e = value[..., :half], value[..., half:]
    return jnp.concatenate([c * cos + e * sin, e * cos - c * sin], axis=-1)


def gelu_parts(v):
    c = math.sqrt(2.0 / math.pi)
    t = jnp.tanh(c * (v + 0.044715 * v * v * v))
    value = 0.5 * v * (1.0 + t)
    slope = 0.5 * (1.0 + t) + 0.5 * v * (1.0 - t * t) * (c * (1.0 + 3 * 0.044715 * v * v))
    return value, slope


def layout(lengths, rows):
    docs = lengths.shape[0]
    ends = jnp.cumsum(lengths)
    number = jnp.sum((rows[:, None] >= ends[None, :]).astype(jnp.int32), axis=1)
    valid = number < docs
    begin = jnp.sum(
        jnp.where(number[:, None] == jnp.arange(docs)[None, :], (ends - lengths)[None, :], 0), axis=1
    )
    place = jnp.where(valid, rows - begin, 0)
    segment = jnp.where(rows < 0, -1, jnp.where(valid, number, docs + rows))
    return segment, place, valid


def spread(shard, axis, section):
    half = shard.shape[axis] // 2
    mine = lax.dynamic_slice_in_dim(shard, lax.axis_index("gx") * half, half, axis)
    received = swap(mine, "section")
    layers = []
    for layer in range(2):
        own = jnp.where(section == layer, mine, received)
        beside = swap(own, "gy")
        other = swap(jnp.stack([own, beside]), "gx")
        layers.append([own, beside, other[0], other[1]])
    return layers


def spread_shared(shard, section):
    half = shard.shape[0] // 2
    gx = lax.axis_index("gx")
    mine = lax.dynamic_slice_in_dim(shard, gx * half, half, 0)
    received = swap(mine, "section")
    other = swap(received, "gx")
    low, high = jnp.where(gx == 0, received, other), jnp.where(gx == 0, other, received)
    whole = jnp.concatenate([low, high])
    return [jnp.where(section == layer, shard, whole) for layer in range(2)]


def from_before(value):
    return lax.ppermute(value, ("gx", "gy"), [(0, 1), (1, 2), (2, 3)])


def to_before(value):
    return lax.ppermute(value, ("gx", "gy"), [(1, 0), (2, 1), (3, 2)])


def attend(queries, keys, values, allowed):
    heads, rows, _ = queries.shape
    scores = mm_t(queries.reshape(heads * rows, HD), keys).reshape(heads, rows, -1)
    scores = jnp.where(allowed[None], scores, -1e30)
    top = jnp.max(scores, axis=-1, keepdims=True)
    weights = jnp.exp(scores - top)
    total = jnp.sum(weights, axis=-1, keepdims=True)
    probs = (weights / total).astype(BF16)
    mixed = mm(probs.reshape(heads * rows, -1), values).astype(BF16)
    return mixed.reshape(heads, rows, HD), top + jnp.log(total)


def attend_back(grad_mixed, queries, keys, values, log_total, allowed):
    heads, rows, _ = queries.shape
    flat_q = queries.reshape(heads * rows, HD)
    flat_g = grad_mixed.reshape(heads * rows, HD)
    scores = mm_t(flat_q, keys).reshape(heads, rows, -1)
    probs = jnp.exp(jnp.where(allowed[None], scores, -1e30) - log_total)
    grad_probs = mm_t(flat_g, values).reshape(heads, rows, -1)
    inner = jnp.sum(probs * grad_probs, axis=-1, keepdims=True)
    grad_scores = (probs * (grad_probs - inner)).astype(BF16).reshape(heads * rows, -1)
    probs_low = probs.astype(BF16).reshape(heads * rows, -1)
    grad_queries = mm(grad_scores, keys).reshape(heads, rows, HD)
    return grad_queries, t_mm(grad_scores, flat_q), t_mm(probs_low, flat_g)


def forward_layer(x, w, place):
    cos, sin, allowed = place
    normed = (x * inverse_rms(x) * w["gain_attn"]).astype(BF16)
    keys = rotate(mm(normed, w["key"]), cos, sin).astype(BF16)
    values = mm(normed, w["value"]).astype(BF16)
    before = from_before(jnp.concatenate([keys, values], axis=1))
    queries = jnp.stack(
        [(rotate(mm(normed, p), cos, sin) * HD**-0.5).astype(BF16) for p in w["query"]]
    )
    keys = jnp.concatenate([before[:, :HD], keys])
    values = jnp.concatenate([before[:, HD:], values])
    mixed, log_total = attend(queries, keys, values, allowed)
    hidden = x
    for j, p in enumerate(w["out"]):
        hidden = hidden + mm(mixed[j], p)
    normed_ff = (hidden * inverse_rms(hidden) * w["gain_ff"]).astype(BF16)
    out = hidden
    gates, ups, acts = [], [], []
    for p_gate, p_up, p_down in zip(w["gate"], w["up"], w["down"]):
        gate, up = mm(normed_ff, p_gate), mm(normed_ff, p_up)
        act = (jax.nn.gelu(gate, approximate=True) * up).astype(BF16)
        out = out + mm(act, p_down)
        gates.append(gate)
        ups.append(up)
        acts.append(act)
    kept = (x, normed, queries, keys, values, mixed, log_total, hidden, normed_ff, gates, ups, acts)
    return out, kept


def backward_layer(grad_out, kept, w, place):
    cos, sin, allowed = place
    x, normed, queries, keys, values, mixed, log_total, hidden, normed_ff, gates, ups, acts = kept
    grads = {"gate": [], "up": [], "down": []}
    g_ff = grad_out.astype(BF16)
    grad_normed = 0.0
    for j in range(4):
        d_act = mm_t(g_ff, w["down"][j])
        value, slope = gelu_parts(gates[j])
        d_gate = (d_act * ups[j] * slope).astype(BF16)
        d_up = (d_act * value).astype(BF16)
        grad_normed = grad_normed + mm_t(d_gate, w["gate"][j]) + mm_t(d_up, w["up"][j])
        grads["down"].append(t_mm(acts[j], g_ff))
        grads["gate"].append(t_mm(normed_ff, d_gate))
        grads["up"].append(t_mm(normed_ff, d_up))
    to_hidden, gain_ff = norm_back(hidden, w["gain_ff"], grad_normed)
    grad_hidden = grad_out + to_hidden
    g_attn = grad_hidden.astype(BF16)
    grads["out"] = [t_mm(mixed[j], g_attn) for j in range(4)]
    grad_mixed = jnp.stack([mm_t(g_attn, p).astype(BF16) for p in w["out"]])
    d_queries, d_keys, d_values = attend_back(
        grad_mixed, queries, keys, values, log_total, allowed
    )
    d_both = jnp.concatenate([d_keys, d_values], axis=1)
    behind = to_before(d_both[:WINDOW].astype(BF16))
    grad_normed = 0.0
    grads["query"] = []
    for j in range(4):
        d_q = (unrotate(d_queries[j], cos, sin) * HD**-0.5).astype(BF16)
        grads["query"].append(t_mm(normed, d_q))
        grad_normed = grad_normed + mm_t(d_q, w["query"][j])
    d_both = d_both[WINDOW:] + behind.astype(F32)
    d_k = unrotate(d_both[:, :HD], cos, sin).astype(BF16)
    d_v = d_both[:, HD:].astype(BF16)
    grad_normed = grad_normed + mm_t(d_k, w["key"]) + mm_t(d_v, w["value"])
    grads["shared"] = t_mm(jnp.concatenate([d_k, d_v], axis=1), normed)
    to_x, gain_attn = norm_back(x, w["gain_attn"], grad_normed)
    grads["gains"] = jnp.stack([gain_attn, gain_ff])
    return grad_hidden + to_x, grads


def reduce_pieces(pieces, section, layer):
    pieces = [p.astype(BF16) for p in pieces]
    got = swap(jnp.stack([pieces[2], pieces[3]]), "gx")
    near = pieces[0] + got[0]
    far = pieces[1] + got[1]
    near = near + swap(far, "gy")
    half = near.shape[0] // 2
    keep = lax.dynamic_slice_in_dim(near, section * half, half, 0)
    send = lax.dynamic_slice_in_dim(near, (1 - section) * half, half, 0)
    total = lax.psum(keep + swap(send, "section"), "dp")
    return total, lax.ppermute(total, "section", [(1 - layer, layer)])


def joined(parts, section):
    (own_0, got_0), (own_1, got_1) = parts
    own, got = jnp.where(section == 0, own_0, own_1), jnp.where(section == 0, got_0, got_1)
    return jnp.where(section == 0, jnp.concatenate([own, got]), jnp.concatenate([got, own]))


def both_cores(piece, axis, scale):
    other = swap(piece, "gx")
    first = lax.axis_index("gx") == 0
    low, high = jnp.where(first, piece, other), jnp.where(first, other, piece)
    return jnp.concatenate([low, high], axis=axis).astype(F32) * scale


def local(
    x_input,
    doc_lengths,
    cotangent,
    gain_attn,
    w_query,
    w_key,
    w_value,
    w_out,
    gain_ff,
    w_gate,
    w_up,
    w_down,
):
    section = lax.axis_index("section")
    gx, gy = lax.axis_index("gx"), lax.axis_index("gy")
    own_rows = x_input.shape[2]
    scale = 1.0 / lax.axis_size("dp")

    weights = [{}, {}]

    def put(name, layers):
        for layer in range(2):
            weights[layer][name] = layers[layer]

    gains = jnp.concatenate([gain_attn, gain_ff])
    other_gains = swap(gains, "section")
    for layer in range(2):
        here = jnp.where(section == layer, gains, other_gains)
        weights[layer]["gain_attn"], weights[layer]["gain_ff"] = here[:1], here[1:]
    put("key", spread_shared(w_key[0], section))
    put("value", spread_shared(w_value[0], section))
    put("query", spread(w_query[0], 1, section))
    put("out", spread(w_out[0], 0, section))
    put("gate", spread(w_gate[0], 1, section))
    put("up", spread(w_up[0], 1, section))
    put("down", spread(w_down[0], 0, section))

    lengths = lax.dynamic_index_in_dim(doc_lengths[:, 0], section, 0, keepdims=False)
    x = lax.dynamic_index_in_dim(x_input[:, 0], section, 0, keepdims=False).astype(F32)
    cot = lax.dynamic_index_in_dim(cotangent[:, 0], section, 0, keepdims=False).astype(F32)
    start = (gx * lax.axis_size("gy") + gy) * own_rows
    rows = start - WINDOW + jnp.arange(WINDOW + own_rows, dtype=jnp.int32)
    segment, place, valid = layout(lengths, rows)
    frequency = jnp.exp(jnp.arange(HD // 2, dtype=F32) * (-2.0 * math.log(10000.0) / HD))
    angles = place[WINDOW:].astype(F32)[:, None] * frequency[None, :]
    distance = rows[WINDOW:, None] - rows[None, :]
    allowed = (
        (distance >= 0) & (distance < WINDOW) & (segment[WINDOW:, None] == segment[None, :])
    )
    where = (jnp.cos(angles), jnp.sin(angles), allowed)

    out_0, kept_0 = forward_layer(x, weights[0], where)
    out_0 = out_0.astype(BF16)
    out_1, kept_1 = forward_layer(out_0.astype(F32), weights[1], where)
    out_1 = out_1.astype(BF16)
    states = jnp.where(section == 0, out_0, out_1)
    other_states = swap(jnp.where(section == 0, out_1, out_0), "section")

    grad_1, grads_1 = backward_layer(
        cot * valid[WINDOW:, None].astype(F32), kept_1, weights[1], where
    )
    grad_1 = grad_1.astype(BF16)
    grad_0, grads_0 = backward_layer(grad_1.astype(F32), kept_0, weights[0], where)
    grad_0 = grad_0.astype(BF16)
    in_grads = jnp.where(section == 0, grad_0, grad_1)
    other_grads = swap(jnp.where(section == 0, grad_1, grad_0), "section")

    def by_micro(own, other):
        first = section == 0
        return jnp.stack([jnp.where(first, own, other), jnp.where(first, other, own)])[
            None, :, None
        ]

    def summed(name):
        return joined(
            [reduce_pieces(grads[name], section, i) for i, grads in enumerate((grads_0, grads_1))],
            section,
        )

    def shared_pieces(grads):
        count = grads["shared"].shape[0] // 4
        parts = [grads["shared"][j * count : (j + 1) * count] for j in range(4)]
        index = 2 * gx + gy
        stacked = jnp.stack(parts)
        return [
            lax.dynamic_index_in_dim(stacked, jnp.bitwise_xor(index, flip), 0, keepdims=False)
            for flip in (0, 1, 2, 3)
        ]

    down = summed("down")
    gate = summed("gate")
    up = summed("up")
    out = summed("out")
    query = summed("query")
    shared = joined(
        [reduce_pieces(shared_pieces(g), section, i) for i, g in enumerate((grads_0, grads_1))],
        section,
    )
    shared = lax.all_gather(shared, ("gx", "gy"), axis=0, tiled=True).astype(F32).T * scale
    gain_sums = lax.psum(
        jnp.stack([grads_0["gains"], grads_1["gains"]]), ("section", "gx", "gy", "dp")
    )
    gain_sums = jnp.where(section == 0, gain_sums[0], gain_sums[1]) * scale

    return (
        by_micro(states, other_states),
        by_micro(in_grads, other_grads),
        gain_sums[:1],
        both_cores(query, 1, scale)[None],
        shared[None, :, :HD],
        shared[None, :, HD:],
        both_cores(out, 0, scale)[None],
        gain_sums[1:],
        both_cores(gate, 1, scale)[None],
        both_cores(up, 1, scale)[None],
        both_cores(down, 0, scale)[None],
    )


def solution(mesh):
    rows = P(None, "dp", ("gx", "gy"), None)
    columns = P("section", None, "gy")
    depth = P("section", "gy", None)
    whole = P("section", None, None)
    gain = P("section", None)
    by_layer = P("section", None, "dp", ("gx", "gy"), None)
    return jax.shard_map(
        local,
        mesh=mesh,
        in_specs=(
            rows,
            P(None, "dp", None),
            rows,
            gain,
            columns,
            whole,
            whole,
            depth,
            gain,
            columns,
            columns,
            depth,
        ),
        out_specs=(
            by_layer,
            by_layer,
            gain,
            columns,
            whole,
            whole,
            depth,
            gain,
            columns,
            columns,
            depth,
        ),
        check_vma=False,
    )
```

time: 1830 us -> 778 us (0.43)
  waiting for transfers between devices: 987 us -> 281 us
  local copies, waits for them, and re-layouts: 325 us -> 38.8 us
  matrix products: 296 us -> 158 us
  starting transfers between devices: 14.2 us -> 117 us
  other arithmetic: 126 us -> 92.4 us
  blocking collectives: 35.1 us -> 62.6 us
    reduce_scatter x18 -> x0, waiting for transfers between devices: 331 us -> none  [the longest x6 136 us: project_back(): lax.psum_scatter(jnp.dot(left, weight, preferred_element_type=jnp.float32...]
    all_gather x18 -> x0, waiting for transfers between devices: 325 us -> none  [the longest x6 136 us: spread_grad(): return lax.all_gather(grad_rows, 'gy', axis=0, tiled=True)]
    psum x2 -> x1, waiting for transfers between devices: 269 us -> 56.9 us  [reduce_pieces(): total = lax.psum(keep + swap(send, 'section'), 'dp')]
    dynamic_update_slice x36 -> x0, local copies, waits for them, and re-layouts: 166 us -> none  [the longest x12 124 us: attend_back(): lax.scan(one_block, start_grads, (numbers, log_total))]
    ppermute x4 -> x89, waiting for transfers between devices: 61.2 us -> 224 us  [the longest x73 210 us: swap(): return lax.ppermute(value, axis, [(0, 1), (1, 0)])]
    dot_general x105 -> x142, matrix products: 296 us -> 158 us  [the longest x46 56.2 us: t_mm(): lax.dot_general(a, b, (((0,), (0,)), ((), ())), preferred_element_type=F32)]
    ppermute x4 -> x89, starting transfers between devices: 9.38 us -> 117 us  [the longest x73 66.9 us: swap(): return lax.ppermute(value, axis, [(0, 1), (1, 0)])]
    dynamic_slice x59 -> x19, local copies, waits for them, and re-layouts: 57.4 us -> 8.73 us  [the longest x5 7.06 us: spread(): lax.dynamic_slice_in_dim(shard, lax.axis_index('gx') * half, half, axis)]
  transfers between devices with their start and end apart: 42 -> 90, of which waited for: 40 -> 35; matrix products, arithmetic and copies ran while one was open for 11% -> 27% of each run, Pallas kernels for 0% -> 0%
where the time goes in v1:
time: 778 us; the launch traced here: 768 us
  waiting for transfers between devices  281 us (36%)
  matrix products  158 us (20%)
  starting transfers between devices  117 us (15%)
  other arithmetic  92.4 us (12%)
  blocking collectives  62.6 us (8%)
  local copies, waits for them, and re-layouts  38.8 us (5%)
  between operations  17.9 us (2%)
    ppermute x73, waiting for transfers between devices, swap(): return lax.ppermute(value, axis, [(0, 1), (1, 0)])  210 us
    ppermute x73, starting transfers between devices, swap(): return lax.ppermute(value, axis, [(0, 1), (1, 0)])  66.9 us
    psum x1, waiting for transfers between devices, reduce_pieces(): total = lax.psum(keep + swap(send, 'section'), 'dp')  56.9 us
    dot_general x46, matrix products, t_mm(): lax.dot_general(a, b, (((0,), (0,)), ((), ())), preferred_element_type=F32)  56.2 us
    dot_general x48, matrix products, mm_t(): lax.dot_general(a, b, (((1,), (1,)), ((), ())), preferred_element_type=F32)  53.3 us
    dot_general x48, matrix products, mm(): return jnp.dot(a, b, preferred_element_type=F32)  48.4 us
    psum x1, blocking collectives, local(): lax.psum(jnp.stack([grads_0['gains'], grads_1['gains']]), ('section', 'gx...  48 us
    ppermute x12, starting transfers between devices, reduce_pieces(): return (total, lax.ppermute(total, 'section', [(1 - layer, layer)]))  38.4 us
  transfers between devices with their start and end apart: 90, of which 35 were waited for; matrix products, arithmetic and copies ran while one was open for 27% of the time, Pallas kernels for 0%

profile of v1, /device:TPU:0, one launch (start us, length us, event | category | flops | bytes accessed | tf_op | source)
XLA Modules:
  0.0 767.6 jit_solution(2742733275523743411)
XLA Ops:
  41.8 11.8 %collective-permute-done.10 = bf16[256,640]{1,0:T(8,128)(2,1)S(1)} collective-permute-done((bf16[256,640]{1,0:T(8,128)(2,1)S(1)}, bf16[256,640]{1,0:T(8,128)(2,1)S(1)}, u32[]{:S(2)}, u32[]{:S(2)}) %collective-permute-start.10) | collective-permute-done | bytes 327712 | tf_op jit(solution)/shard_map/ppermute | solution.py:15
  62.6 12.9 %collective-permute-done.14 = bf16[512,640]{1,0:T(8,128)(2,1)S(1)} collective-permute-done((bf16[512,640]{1,0:T(8,128)(2,1)S(1)}, bf16[512,640]{1,0:T(8,128)(2,1)S(1)}, u32[]{:S(2)}, u32[]{:S(2)}) %collective-permute-start.14) | collective-permute-done | bytes 655392 | tf_op jit(solution)/shard_map/ppermute | solution.py:15
  87.7 5.4 collective-permute-done.15
  95.0 12.2 %collective-permute-done.16 = bf16[640,512]{1,0:T(8,128)(2,1)S(1)} collective-permute-done((bf16[640,512]{1,0:T(8,128)(2,1)S(1)}, bf16[640,512]{1,0:T(8,128)(2,1)S(1)}, u32[]{:S(2)}, u32[]{:S(2)}) %collective-permute-start.16) | collective-permute-done | bytes 655392 | tf_op jit(solution)/shard_map/ppermute | solution.py:15
  111.0 24.3 %collective-permute-done.17 = bf16[512,640]{1,0:T(8,128)(2,1)S(1)} collective-permute-done((bf16[512,640]{1,0:T(8,128)(2,1)S(1)}, bf16[512,640]{1,0:T(8,128)(2,1)S(1)}, u32[]{:S(2)}, u32[]{:S(2)}) %collective-permute-start.17) | collective-permute-done | bytes 655392 | tf_op jit(solution)/shard_map/ppermute | solution.py:15
  136.1 13.2 %collective-permute-done.27 = bf16[640,512]{1,0:T(8,128)(2,1)S(1)} collective-permute-done((bf16[640,512]{1,0:T(8,128)(2,1)S(1)}, bf16[640,512]{1,0:T(8,128)(2,1)S(1)}, u32[]{:S(2)}, u32[]{:S(2)}) %collective-permute-start.27) | collective-permute-done | bytes 655392 | tf_op jit(solution)/shard_map/ppermute | solution.py:15
  154.5 8.1 %collective-permute-done.26 = bf16[640,512]{1,0:T(8,128)(2,1)S(1)} collective-permute-done((bf16[640,512]{1,0:T(8,128)(2,1)S(1)}, bf16[640,512]{1,0:T(8,128)(2,1)S(1)}, u32[]{:S(2)}, u32[]{:S(2)}) %collective-permute-start.26) | collective-permute-done | bytes 655392 | tf_op jit(solution)/shard_map/ppermute | solution.py:15
  166.2 5.6 collective-permute-done.8
  282.8 5.8 multiply_convert_fusion.1
  395.7 7.0 collective-permute-done.40
  403.7 5.2 collective-permute-done.57
  441.7 7.0 collective-permute-done.37
  448.8 6.3 collective-permute-done.54
  483.7 11.1 %collective-permute-done.66 = bf16[640,512]{1,0:T(8,128)(2,1)S(1)} collective-permute-done((bf16[640,512]{1,0:T(8,128)(2,1)S(1)}, bf16[640,512]{1,0:T(8,128)(2,1)S(1)}, u32[]{:S(2)}, u32[]{:S(2)}) %collective-permute-start.66) | collective-permute-done | bytes 655392 | tf_op jit(solution)/shard_map/ppermute | solution.py:15
  497.7 11.1 %collective-permute-done.75 = bf16[640,512]{1,0:T(8,128)(2,1)S(1)} collective-permute-done((bf16[640,512]{1,0:T(8,128)(2,1)S(1)}, bf16[640,512]{1,0:T(8,128)(2,1)S(1)}, u32[]{:S(2)}, u32[]{:S(2)}) %collective-permute-start.75) | collective-permute-done | bytes 655392 | tf_op jit(solution)/shard_map/ppermute | solution.py:15
  511.6 11.2 %collective-permute-done.84 = bf16[512,640]{1,0:T(8,128)(2,1)S(1)} collective-permute-done((bf16[512,640]{1,0:T(8,128)(2,1)S(1)}, bf16[512,640]{1,0:T(8,128)(2,1)S(1)}, u32[]{:S(2)}, u32[]{:S(2)}) %collective-permute-start.84) | collective-permute-done | bytes 655392 | tf_op jit(solution)/shard_map/ppermute | solution.py:15
  526.0 6.0 collective-permute-done.76
  539.5 11.4 %collective-permute-done.72 = bf16[640,512]{1,0:T(8,128)(2,1)S(1)} collective-permute-done((bf16[640,512]{1,0:T(8,128)(2,1)S(1)}, bf16[640,512]{1,0:T(8,128)(2,1)S(1)}, u32[]{:S(2)}, u32[]{:S(2)}) %collective-permute-start.72) | collective-permute-done | bytes 655392 | tf_op jit(solution)/shard_map/ppermute | solution.py:15
  552.7 6.3 collective-permute-done.81
  576.5 48.0 %psum.91 = f32[2,2,640]{2,1,0:T(2,128)S(1)} all-reduce(f32[2,2,640]{2,1,0:T(2,128)S(1)} %pad_maximum_fusion.50), channel_id=1, replica_groups=mesh['section'=2,'gx'=2,'gy'=2,'dp'=4] {'section','gx','gy','dp'}, use_global_device_ids=true, to_apply=%region_21.22 | all-reduce | flops 2560 | bytes 20480 | tf_op jit(solution)/shard_map/psum | solution.py:328
  626.4 56.9 %all-reduce.3.cloned.1.call-done = (bf16[320,256]{1,0:T(8,128)(2,1)}, bf16[320,256]{1,0:T(8,128)(2,1)}, bf16[64,640]{1,0:T(8,128)(2,1)}, bf16[64,640]{1,0:T(8,12...) async-done(((bf16[320,256]{1,0:T(8,128)(2,1)}, ...) | async-done | bytes 2785296 | tf_op jit(solution)/shard_map/psum | solution.py:211
  684.7 5.9 collective-permute-start.43
  701.8 5.9 collective-permute-start.60
  709.0 14.6 %all_gather.3 = bf16[512,640]{1,0:T(8,128)(2,1)S(1)} all-gather(bf16[128,640]{1,0:T(8,128)(2,1)S(1)} %maximum_select_fusion.7), channel_id=1, replica_groups=mesh['section'=2,'gx'=2,'gy'=2,'dp'=4] {'gx','gy'}, dimensions={0}, use_global_device_ids=true | all-gather | bytes 819200 | tf_op jit(solution)/shard_map/all_gather | solution.py:327
  (901 shorter events, 436.8 us)
Async XLA Ops:
  7.2 676.1 %all-reduce.3.cloned.1.call-start = ((), (), s32[]{:S(2)}) async-start(), calls=%async_computation | async-start | bytes 5570560 | tf_op jit(solution)/shard_map/psum | solution.py:211
  30.7 44.7 %collective-permute-start.14 = (bf16[512,640]{1,0:T(8,128)(2,1)S(1)}, bf16[512,640]{1,0:T(8,128)(2,1)S(1)}, u32[]{:S(2)}, u32[]{:S(2)}) collective-permute-start(bf16[512,640]{1,0:T(8,128)(2,1)S(1)} %copy-done.94), channel_id=1, source_target_pairs={{0,16},{16,0},{1,17},{17,1},{2,18},{18,2},{3,19},{19,3},{4,20},{20... | collective-permute-start | bytes 1966088 | tf_op jit(solution)/shard_map/ppermute | solution.py:15
  55.8 123.2 %collective-permute-start.11 = (bf16[2,256,640]{2,1,0:T(8,128)(2,1)S(1)}, bf16[2,256,640]{2,1,0:T(8,128)(2,1)S(1)}, u32[]{:S(2)}, u32[]{:S(2)}) collective-permute-start(bf16[2,256,640]{2,1,0:T(8,128)(2,1)S(1)} %pad_maximum_fusion.21), channel_id=1, source_target_pairs={{0,8},{8,0},{1,9},{9,1},{2,10},{10,2},{3,11},{11,3},{4,12},{12,4},... | collective-permute-start | bytes 1966088 | tf_op jit(solution)/shard_map/ppermute | solution.py:15
  78.8 56.6 %collective-permute-start.28 = (bf16[512,640]{1,0:T(8,128)(2,1)S(1)}, bf16[512,640]{1,0:T(8,128)(2,1)S(1)}, u32[]{:S(2)}, u32[]{:S(2)}) collective-permute-start(bf16[512,640]{1,0:T(8,128)(2,1)S(1)} %get-tuple-element.113), channel_id=1, source_target_pairs={{0,4},{4,0},{1,5},{5,1},{2,6},{6,2},{3,7},{7,3},{8,12},{12,8},{9,1... | collective-permute-start | bytes 1966088 | tf_op jit(solution)/shard_map/ppermute | solution.py:15
  84.4 50.9 %collective-permute-start.17 = (bf16[512,640]{1,0:T(8,128)(2,1)S(1)}, bf16[512,640]{1,0:T(8,128)(2,1)S(1)}, u32[]{:S(2)}, u32[]{:S(2)}) collective-permute-start(bf16[512,640]{1,0:T(8,128)(2,1)S(1)} %get-tuple-element.114), channel_id=1, source_target_pairs={{0,4},{4,0},{1,5},{5,1},{2,6},{6,2},{3,7},{7,3},{8,12},{12,8},{9,1... | collective-permute-start | bytes 1966088 | tf_op jit(solution)/shard_map/ppermute | solution.py:15
  93.1 56.2 %collective-permute-start.27 = (bf16[640,512]{1,0:T(8,128)(2,1)S(1)}, bf16[640,512]{1,0:T(8,128)(2,1)S(1)}, u32[]{:S(2)}, u32[]{:S(2)}) collective-permute-start(bf16[640,512]{1,0:T(8,128)(2,1)S(1)} %get-tuple-element.117), channel_id=1, source_target_pairs={{0,4},{4,0},{1,5},{5,1},{2,6},{6,2},{3,7},{7,3},{8,12},{12,8},{9,1... | collective-permute-start | bytes 1966088 | tf_op jit(solution)/shard_map/ppermute | solution.py:15
  107.1 55.5 %collective-permute-start.26 = (bf16[640,512]{1,0:T(8,128)(2,1)S(1)}, bf16[640,512]{1,0:T(8,128)(2,1)S(1)}, u32[]{:S(2)}, u32[]{:S(2)}) collective-permute-start(bf16[640,512]{1,0:T(8,128)(2,1)S(1)} %get-tuple-element.115), channel_id=1, source_target_pairs={{0,4},{4,0},{1,5},{5,1},{2,6},{6,2},{3,7},{7,3},{8,12},{12,8},{9,1... | collective-permute-start | bytes 1966088 | tf_op jit(solution)/shard_map/ppermute | solution.py:15
  135.2 92.4 %collective-permute-start.25 = (bf16[2,256,640]{2,1,0:T(8,128)(2,1)}, bf16[2,256,640]{2,1,0:T(8,128)(2,1)}, u32[]{:S(2)}, u32[]{:S(2)}) collective-permute-start(bf16[2,256,640]{2,1,0:T(8,128)(2,1)} %pad_maximum_fusion.23), channel_id=1, source_target_pairs={{0,8},{8,0},{1,9},{9,1},{2,10},{10,2},{3,11},{11,3},{4,12},{12,4},... | collective-permute-start | bytes 1966088 | tf_op jit(solution)/shard_map/ppermute | solution.py:15
  135.4 62.1 %collective-permute-start.22 = (bf16[2,640,256]{2,1,0:T(8,128)(2,1)}, bf16[2,640,256]{2,1,0:T(8,128)(2,1)}, u32[]{:S(2)}, u32[]{:S(2)}) collective-permute-start(bf16[2,640,256]{2,1,0:T(8,128)(2,1)} %pad_maximum_fusion.22), channel_id=1, source_target_pairs={{0,8},{8,0},{1,9},{9,1},{2,10},{10,2},{3,11},{11,3},{4,12},{12,4},... | collective-permute-start | bytes 1966088 | tf_op jit(solution)/shard_map/ppermute | solution.py:15
  190.1 42.4 %collective-permute-start.30 = (bf16[2,640,512]{2,1,0:T(8,128)(2,1)}, bf16[2,640,512]{2,1,0:T(8,128)(2,1)S(1)}, u32[]{:S(2)}, u32[]{:S(2)}) collective-permute-start(bf16[2,640,512]{2,1,0:T(8,128)(2,1)} %pad_maximum_fusion.4), channel_id=1, source_target_pairs={{0,8},{8,0},{1,9},{9,1},{2,10},{10,2},{3,11},{11,3},{4,12},{12,4},... | collective-permute-start | bytes 3932168 | tf_op jit(solution)/shard_map/ppermute | solution.py:15
  193.7 44.3 %collective-permute-start.29 = (bf16[2,640,512]{2,1,0:T(8,128)(2,1)}, bf16[2,640,512]{2,1,0:T(8,128)(2,1)}, u32[]{:S(2)}, u32[]{:S(2)}) collective-permute-start(bf16[2,640,512]{2,1,0:T(8,128)(2,1)} %pad_maximum_fusion.3), channel_id=1, source_target_pairs={{0,8},{8,0},{1,9},{9,1},{2,10},{10,2},{3,11},{11,3},{4,12},{12,4},... | collective-permute-start | bytes 3932168 | tf_op jit(solution)/shard_map/ppermute | solution.py:15
  300.2 89.1 %collective-permute-start.39 = (bf16[2,640,256]{2,1,0:T(8,128)(2,1)}, bf16[2,640,256]{2,1,0:T(8,128)(2,1)}, u32[]{:S(2)}, u32[]{:S(2)}) collective-permute-start(bf16[2,640,256]{2,1,0:T(8,128)(2,1)} %pad_maximum_fusion.25), channel_id=1, source_target_pairs={{0,8},{8,0},{1,9},{9,1},{2,10},{10,2},{3,11},{11,3},{4,12},{12,4},... | collective-permute-start | bytes 1966088 | tf_op jit(solution)/shard_map/ppermute | solution.py:15
  304.3 87.7 %collective-permute-start.56 = (bf16[2,256,640]{2,1,0:T(8,128)(2,1)}, bf16[2,256,640]{2,1,0:T(8,128)(2,1)}, u32[]{:S(2)}, u32[]{:S(2)}) collective-permute-start(bf16[2,256,640]{2,1,0:T(8,128)(2,1)} %pad_maximum_fusion.27), channel_id=1, source_target_pairs={{0,8},{8,0},{1,9},{9,1},{2,10},{10,2},{3,11},{11,3},{4,12},{12,4},... | collective-permute-start | bytes 1966088 | tf_op jit(solution)/shard_map/ppermute | solution.py:15
  305.5 128.5 %collective-permute-start.65 = (bf16[2,640,512]{2,1,0:T(8,128)(2,1)}, bf16[2,640,512]{2,1,0:T(8,128)(2,1)}, u32[]{:S(2)}, u32[]{:S(2)}) collective-permute-start(bf16[2,640,512]{2,1,0:T(8,128)(2,1)} %pad_maximum_fusion.9), channel_id=1, source_target_pairs={{0,8},{8,0},{1,9},{9,1},{2,10},{10,2},{3,11},{11,3},{4,12},{12,4},... | collective-permute-start | bytes 3932168 | tf_op jit(solution)/shard_map/ppermute | solution.py:15
  307.3 128.8 %collective-permute-start.74 = (bf16[2,640,512]{2,1,0:T(8,128)(2,1)}, bf16[2,640,512]{2,1,0:T(8,128)(2,1)}, u32[]{:S(2)}, u32[]{:S(2)}) collective-permute-start(bf16[2,640,512]{2,1,0:T(8,128)(2,1)} %pad_maximum_fusion.11), channel_id=1, source_target_pairs={{0,8},{8,0},{1,9},{9,1},{2,10},{10,2},{3,11},{11,3},{4,12},{12,4},... | collective-permute-start | bytes 3932168 | tf_op jit(solution)/shard_map/ppermute | solution.py:15
  432.3 135.5 %collective-permute-start.32 = (bf16[512,640]{1,0:T(8,128)(2,1)}, bf16[512,640]{1,0:T(8,128)(2,1)}, u32[]{:S(2)}, u32[]{:S(2)}) collective-permute-start(bf16[512,640]{1,0:T(8,128)(2,1)} %get-tuple-element.213), channel_id=1, source_target_pairs={{0,16},{16,0},{1,17},{17,1},{2,18},{18,2},{3,19},{19,3},{4,20},{20... | collective-permute-start | bytes 1966088 | tf_op jit(solution)/shard_map/ppermute | solution.py:15
  433.3 46.2 %collective-permute-start.62 = (bf16[2,640,512]{2,1,0:T(8,128)(2,1)S(1)}, bf16[2,640,512]{2,1,0:T(8,128)(2,1)S(1)}, u32[]{:S(2)}, u32[]{:S(2)}) collective-permute-start(bf16[2,640,512]{2,1,0:T(8,128)(2,1)S(1)} %pad_maximum_fusion.8), channel_id=1, source_target_pairs={{0,8},{8,0},{1,9},{9,1},{2,10},{10,2},{3,11},{11,3},{4,12},{12,4},... | collective-permute-start | bytes 3932168 | tf_op jit(solution)/shard_map/ppermute | solution.py:15
  434.0 46.4 %collective-permute-start.71 = (bf16[2,640,512]{2,1,0:T(8,128)(2,1)S(1)}, bf16[2,640,512]{2,1,0:T(8,128)(2,1)S(1)}, u32[]{:S(2)}, u32[]{:S(2)}) collective-permute-start(bf16[2,640,512]{2,1,0:T(8,128)(2,1)S(1)} %pad_maximum_fusion.10), channel_id=1, source_target_pairs={{0,8},{8,0},{1,9},{9,1},{2,10},{10,2},{3,11},{11,3},{4,12},{12,4},... | collective-permute-start | bytes 3932168 | tf_op jit(solution)/shard_map/ppermute | solution.py:15
  480.4 42.5 %collective-permute-start.84 = (bf16[512,640]{1,0:T(8,128)(2,1)S(1)}, bf16[512,640]{1,0:T(8,128)(2,1)S(1)}, u32[]{:S(2)}, u32[]{:S(2)}) collective-permute-start(bf16[512,640]{1,0:T(8,128)(2,1)S(1)} %fusion.256), channel_id=1, source_target_pairs={{0,4},{4,0},{1,5},{5,1},{2,6},{6,2},{3,7},{7,3},{8,12},{12,8},{9,1... | collective-permute-start | bytes 1966088 | tf_op jit(solution)/shard_map/ppermute | solution.py:15
  482.7 55.1 %collective-permute-start.63 = (bf16[640,512]{1,0:T(8,128)(2,1)S(1)}, bf16[640,512]{1,0:T(8,128)(2,1)S(1)}, u32[]{:S(2)}, u32[]{:S(2)}) collective-permute-start(bf16[640,512]{1,0:T(8,128)(2,1)S(1)} %fusion.271), channel_id=1, source_target_pairs={{0,4},{4,0},{1,5},{5,1},{2,6},{6,2},{3,7},{7,3},{8,12},{12,8},{9,1... | collective-permute-start | bytes 1966088 | tf_op jit(solution)/shard_map/ppermute | solution.py:15
  494.8 56.2 %collective-permute-start.72 = (bf16[640,512]{1,0:T(8,128)(2,1)S(1)}, bf16[640,512]{1,0:T(8,128)(2,1)S(1)}, u32[]{:S(2)}, u32[]{:S(2)}) collective-permute-start(bf16[640,512]{1,0:T(8,128)(2,1)S(1)} %fusion.265), channel_id=1, source_target_pairs={{0,4},{4,0},{1,5},{5,1},{2,6},{6,2},{3,7},{7,3},{8,12},{12,8},{9,1... | collective-permute-start | bytes 1966088 | tf_op jit(solution)/shard_map/ppermute | solution.py:15
  574.8 50.3 %collective-permute-start.35 = (bf16[512,640]{1,0:T(8,128)(2,1)S(1)}, bf16[512,640]{1,0:T(8,128)(2,1)S(1)}, u32[]{:S(2)}, u32[]{:S(2)}) collective-permute-start(bf16[512,640]{1,0:T(8,128)(2,1)S(1)} %get-tuple-element.57), channel_id=1, source_target_pairs={{0,16},{16,0},{1,17},{17,1},{2,18},{18,2},{3,19},{19,3},{4,20},{20... | collective-permute-start | bytes 1966088 | tf_op jit(solution)/shard_map/ppermute | solution.py:15
  683.3 42.7 %collective-permute-start.42 = (bf16[320,256]{1,0:T(8,128)(2,1)}, bf16[320,256]{1,0:T(8,128)(2,1)}, u32[]{:S(2)}, u32[]{:S(2)}) collective-permute-start(bf16[320,256]{1,0:T(8,128)(2,1)} %get-tuple-element.45), channel_id=1, source_target_pairs={{16,0},{17,1},{18,2},{19,3},{20,4},{21,5},{22,6},{23,7},{24,8},{25... | collective-permute-start | bytes 491528 | tf_op jit(solution)/shard_map/ppermute | solution.py:212
  684.7 46.2 %collective-permute-start.43 = (bf16[320,256]{1,0:T(8,128)(2,1)}, bf16[320,256]{1,0:T(8,128)(2,1)}, u32[]{:S(2)}, u32[]{:S(2)}) collective-permute-start(bf16[320,256]{1,0:T(8,128)(2,1)} %get-tuple-element.46), channel_id=1, source_target_pairs={{0,16},{1,17},{2,18},{3,19},{4,20},{5,21},{6,22},{7,23},{8,24},{9,... | collective-permute-start | bytes 491528 | tf_op jit(solution)/shard_map/ppermute | solution.py:212
  (271 other events, 3804.0 us)
Sparse Core Ops, SparseCore 0:
  567.3 115.9 all-reduce.2

commit v2 on v1

--- a/solution.py
+++ b/solution.py
@@ -7,6 +7,7 @@
 
 HD = 256
 WINDOW = 512
+GAIN_ROWS = 32
 F32 = jnp.float32
 BF16 = jnp.bfloat16
 
@@ -71,28 +72,62 @@
     return segment, place, valid
 
 
-def spread(shard, axis, section):
-    half = shard.shape[axis] // 2
-    mine = lax.dynamic_slice_in_dim(shard, lax.axis_index("gx") * half, half, axis)
-    received = swap(mine, "section")
+def pick(flag, a, b):
+    return jnp.where(flag, a, b)
+
+
+def gather_weights(w_query, w_key, w_value, w_out, w_gate, w_up, w_down, section):
+    gx = lax.axis_index("gx")
+
+    def half(w, axis):
+        size = w.shape[axis] // 2
+        return lax.dynamic_slice_in_dim(w, gx * size, size, axis)
+
+    def two_layers(mine, received):
+        return [pick(section == layer, mine, received) for layer in range(2)]
+
+    heads, hidden = w_query.shape[1] // 2, w_gate.shape[1] // 2
+    first_own = jnp.concatenate([half(w_query, 1), half(w_key, 1), half(w_value, 1)], axis=1)
+    out_own = half(w_out, 0)
+    wide_own = jnp.concatenate([half(w_gate, 1), half(w_up, 1)], axis=1)
+    down_own = half(w_down, 0)
+    first_got = swap(first_own, "section")
+    down_beside = swap(down_own, "gy")
+    out_got = swap(out_own, "section")
+    wide_got = swap(wide_own, "section")
+    down_own = jnp.concatenate([down_own, down_beside])
+    down_got = swap(down_own, "section")
+
+    shared_got = first_got[:, heads:]
+    shared_other = swap(shared_got, "gx")
+    low, high = pick(gx == 0, shared_got, shared_other), pick(gx == 0, shared_other, shared_got)
+    part = low.shape[1] // 2
+    key_got = jnp.concatenate([low[:, :part], high[:, :part]], axis=1)
+    value_got = jnp.concatenate([low[:, part:], high[:, part:]], axis=1)
+    keys, values = two_layers(w_key, key_got), two_layers(w_value, value_got)
+
+    queries = two_layers(first_own[:, :heads], first_got[:, :heads])
+    outs = two_layers(out_own, out_got)
+    wides = two_layers(wide_own, wide_got)
+    downs = two_layers(down_own, down_got)
     layers = []
     for layer in range(2):
-        own = jnp.where(section == layer, mine, received)
-        beside = swap(own, "gy")
-        other = swap(jnp.stack([own, beside]), "gx")
-        layers.append([own, beside, other[0], other[1]])
+        query, out, wide, down = queries[layer], outs[layer], wides[layer], downs[layer]
+        query_beside, out_beside, wide_beside = swap(query, "gy"), swap(out, "gy"), swap(wide, "gy")
+        wide_pieces = [wide, wide_beside, swap(wide, "gx"), swap(wide_beside, "gx")]
+        down_other = swap(down, "gx")
+        layers.append(
+            {
+                "query": [query, query_beside, swap(query, "gx"), swap(query_beside, "gx")],
+                "out": [out, out_beside, swap(out, "gx"), swap(out_beside, "gx")],
+                "gate": [w[:, :hidden] for w in wide_pieces],
+                "up": [w[:, hidden:] for w in wide_pieces],
+                "down": [down[:hidden], down[hidden:], down_other[:hidden], down_other[hidden:]],
+                "key": keys[layer],
+                "value": values[layer],
+            }
+        )
     return layers
-
-
-def spread_shared(shard, section):
-    half = shard.shape[0] // 2
-    gx = lax.axis_index("gx")
-    mine = lax.dynamic_slice_in_dim(shard, gx * half, half, 0)
-    received = swap(mine, "section")
-    other = swap(received, "gx")
-    low, high = jnp.where(gx == 0, received, other), jnp.where(gx == 0, other, received)
-    whole = jnp.concatenate([low, high])
-    return [jnp.where(section == layer, shard, whole) for layer in range(2)]
 
 
 def from_before(value):
@@ -158,25 +193,26 @@
     return out, kept
 
 
-def backward_layer(grad_out, kept, w, place):
-    cos, sin, allowed = place
-    x, normed, queries, keys, values, mixed, log_total, hidden, normed_ff, gates, ups, acts = kept
-    grads = {"gate": [], "up": [], "down": []}
+def ffn_back(grad_out, kept, w):
+    hidden, normed_ff, gates, ups, acts = kept[7:]
     g_ff = grad_out.astype(BF16)
     grad_normed = 0.0
+    pieces = []
     for j in range(4):
         d_act = mm_t(g_ff, w["down"][j])
         value, slope = gelu_parts(gates[j])
         d_gate = (d_act * ups[j] * slope).astype(BF16)
         d_up = (d_act * value).astype(BF16)
         grad_normed = grad_normed + mm_t(d_gate, w["gate"][j]) + mm_t(d_up, w["up"][j])
-        grads["down"].append(t_mm(acts[j], g_ff))
-        grads["gate"].append(t_mm(normed_ff, d_gate))
-        grads["up"].append(t_mm(normed_ff, d_up))
+        pieces += [t_mm(d_gate, normed_ff), t_mm(d_up, normed_ff), t_mm(acts[j], g_ff)]
     to_hidden, gain_ff = norm_back(hidden, w["gain_ff"], grad_normed)
-    grad_hidden = grad_out + to_hidden
+    return grad_out + to_hidden, gain_ff, [p.astype(BF16) for p in pieces]
+
+
+def attn_back(grad_hidden, gain_ff, kept, w, place, order):
+    cos, sin, allowed = place
+    x, normed, queries, keys, values, mixed, log_total = kept[:7]
     g_attn = grad_hidden.astype(BF16)
-    grads["out"] = [t_mm(mixed[j], g_attn) for j in range(4)]
     grad_mixed = jnp.stack([mm_t(g_attn, p).astype(BF16) for p in w["out"]])
     d_queries, d_keys, d_values = attend_back(
         grad_mixed, queries, keys, values, log_total, allowed
@@ -184,45 +220,43 @@
     d_both = jnp.concatenate([d_keys, d_values], axis=1)
     behind = to_before(d_both[:WINDOW].astype(BF16))
     grad_normed = 0.0
-    grads["query"] = []
+    grad_query = []
     for j in range(4):
         d_q = (unrotate(d_queries[j], cos, sin) * HD**-0.5).astype(BF16)
-        grads["query"].append(t_mm(normed, d_q))
+        grad_query.append(t_mm(d_q, normed).astype(BF16))
         grad_normed = grad_normed + mm_t(d_q, w["query"][j])
+    grad_out = [t_mm(mixed[j], g_attn).astype(BF16) for j in range(4)]
     d_both = d_both[WINDOW:] + behind.astype(F32)
     d_k = unrotate(d_both[:, :HD], cos, sin).astype(BF16)
     d_v = d_both[:, HD:].astype(BF16)
     grad_normed = grad_normed + mm_t(d_k, w["key"]) + mm_t(d_v, w["value"])
-    grads["shared"] = t_mm(jnp.concatenate([d_k, d_v], axis=1), normed)
+    shared = t_mm(jnp.concatenate([d_k, d_v], axis=1), normed).astype(BF16)
     to_x, gain_attn = norm_back(x, w["gain_attn"], grad_normed)
-    grads["gains"] = jnp.stack([gain_attn, gain_ff])
-    return grad_hidden + to_x, grads
-
-
-def reduce_pieces(pieces, section, layer):
-    pieces = [p.astype(BF16) for p in pieces]
-    got = swap(jnp.stack([pieces[2], pieces[3]]), "gx")
-    near = pieces[0] + got[0]
-    far = pieces[1] + got[1]
-    near = near + swap(far, "gy")
-    half = near.shape[0] // 2
-    keep = lax.dynamic_slice_in_dim(near, section * half, half, 0)
-    send = lax.dynamic_slice_in_dim(near, (1 - section) * half, half, 0)
-    total = lax.psum(keep + swap(send, "section"), "dp")
-    return total, lax.ppermute(total, "section", [(1 - layer, layer)])
-
-
-def joined(parts, section):
-    (own_0, got_0), (own_1, got_1) = parts
-    own, got = jnp.where(section == 0, own_0, own_1), jnp.where(section == 0, got_0, got_1)
-    return jnp.where(section == 0, jnp.concatenate([own, got]), jnp.concatenate([got, own]))
-
-
-def both_cores(piece, axis, scale):
-    other = swap(piece, "gx")
-    first = lax.axis_index("gx") == 0
-    low, high = jnp.where(first, piece, other), jnp.where(first, other, piece)
-    return jnp.concatenate([low, high], axis=axis).astype(F32) * scale
+    gains = jnp.pad(jnp.stack([gain_attn, gain_ff]), ((0, GAIN_ROWS - 2), (0, 0))).astype(BF16)
+    count = shared.shape[0] // 4
+    pieces = []
+    for j in range(4):
+        quarter = lax.dynamic_slice_in_dim(shared, (order ^ j) * count, count, 0)
+        pieces += [grad_query[j], grad_out[j], quarter, gains]
+    return grad_hidden + to_x, pieces
+
+
+def over_cores(pieces):
+    count = len(pieces) // 4
+    kept = jnp.concatenate(pieces[: 2 * count])
+    kept = kept + swap(jnp.concatenate(pieces[2 * count :]), "gx")
+    half = kept.shape[0] // 2
+    return kept[:half], kept[half:]
+
+
+def over_section(total, section):
+    half = total.shape[0] // 2
+    low, high = total[:half], total[half:]
+    return pick(section == 0, low, high) + swap(pick(section == 0, high, low), "section")
+
+
+def to_owner(value, layer):
+    return lax.ppermute(value, "section", [(1 - layer, layer)])
 
 
 def local(
@@ -244,24 +278,14 @@
     own_rows = x_input.shape[2]
     scale = 1.0 / lax.axis_size("dp")
 
-    weights = [{}, {}]
-
-    def put(name, layers):
-        for layer in range(2):
-            weights[layer][name] = layers[layer]
-
+    weights = gather_weights(
+        w_query[0], w_key[0], w_value[0], w_out[0], w_gate[0], w_up[0], w_down[0], section
+    )
     gains = jnp.concatenate([gain_attn, gain_ff])
     other_gains = swap(gains, "section")
     for layer in range(2):
-        here = jnp.where(section == layer, gains, other_gains)
+        here = pick(section == layer, gains, other_gains)
         weights[layer]["gain_attn"], weights[layer]["gain_ff"] = here[:1], here[1:]
-    put("key", spread_shared(w_key[0], section))
-    put("value", spread_shared(w_value[0], section))
-    put("query", spread(w_query[0], 1, section))
-    put("out", spread(w_out[0], 0, section))
-    put("gate", spread(w_gate[0], 1, section))
-    put("up", spread(w_up[0], 1, section))
-    put("down", spread(w_down[0], 0, section))
 
     lengths = lax.dynamic_index_in_dim(doc_lengths[:, 0], section, 0, keepdims=False)
     x = lax.dynamic_index_in_dim(x_input[:, 0], section, 0, keepdims=False).astype(F32)
@@ -284,14 +308,44 @@
     states = jnp.where(section == 0, out_0, out_1)
     other_states = swap(jnp.where(section == 0, out_1, out_0), "section")
 
-    grad_1, grads_1 = backward_layer(
-        cot * valid[WINDOW:, None].astype(F32), kept_1, weights[1], where
-    )
+    order = 2 * gx + gy
+    grad_out = cot * valid[WINDOW:, None].astype(F32)
+    grad_hidden, gain_ff, pieces = ffn_back(grad_out, kept_1, weights[1])
+    ffn_1, far = over_cores(pieces)
+    ffn_1 = ffn_1 + swap(far, "gy")
+    grad_1, pieces = attn_back(grad_hidden, gain_ff, kept_1, weights[1], where, order)
     grad_1 = grad_1.astype(BF16)
-    grad_0, grads_0 = backward_layer(grad_1.astype(F32), kept_0, weights[0], where)
+    attn_1, far = over_cores(pieces)
+    attn_1 = attn_1 + swap(far, "gy")
+
+    grad_hidden, gain_ff, pieces = ffn_back(grad_1.astype(F32), kept_0, weights[0])
+    ffn_1 = over_section(ffn_1, section)
+    ffn_0, far = over_cores(pieces)
+    grad_hidden, ffn_1, attn_1, ffn_0, far = lax.optimization_barrier(
+        (grad_hidden, ffn_1, attn_1, ffn_0, far)
+    )
+    ffn_0 = ffn_0 + swap(far, "gy")
+    ffn_1 = lax.psum(ffn_1, "dp")
+    attn_1 = over_section(attn_1, section)
+    grad_0, pieces = attn_back(grad_hidden, gain_ff, kept_0, weights[0], where, order)
     grad_0 = grad_0.astype(BF16)
-    in_grads = jnp.where(section == 0, grad_0, grad_1)
-    other_grads = swap(jnp.where(section == 0, grad_1, grad_0), "section")
+    attn_0, far = over_cores(pieces)
+    ffn_1, attn_1, attn_0, far = lax.optimization_barrier((ffn_1, attn_1, attn_0, far))
+    attn_1 = lax.psum(attn_1, "dp")
+    attn_0 = attn_0 + swap(far, "gy")
+    ffn_1_got = to_owner(ffn_1, 1)
+    ffn_0 = over_section(ffn_0, section)
+    ffn_0, attn_1 = lax.optimization_barrier((ffn_0, attn_1))
+    ffn_0 = lax.psum(ffn_0, "dp")
+    attn_1_got = to_owner(attn_1, 1)
+    attn_0 = over_section(attn_0, section)
+    ffn_0, attn_0 = lax.optimization_barrier((ffn_0, attn_0))
+    attn_0 = lax.psum(attn_0, "dp")
+    ffn_0_got = to_owner(ffn_0, 0)
+    attn_0_got = to_owner(attn_0, 0)
+
+    in_grads = pick(section == 0, grad_0, grad_1)
+    other_grads = swap(pick(section == 0, grad_1, grad_0), "section")
 
     def by_micro(own, other):
         first = section == 0
@@ -299,49 +353,47 @@
             None, :, None
         ]
 
-    def summed(name):
-        return joined(
-            [reduce_pieces(grads[name], section, i) for i, grads in enumerate((grads_0, grads_1))],
-            section,
-        )
-
-    def shared_pieces(grads):
-        count = grads["shared"].shape[0] // 4
-        parts = [grads["shared"][j * count : (j + 1) * count] for j in range(4)]
-        index = 2 * gx + gy
-        stacked = jnp.stack(parts)
-        return [
-            lax.dynamic_index_in_dim(stacked, jnp.bitwise_xor(index, flip), 0, keepdims=False)
-            for flip in (0, 1, 2, 3)
-        ]
-
-    down = summed("down")
-    gate = summed("gate")
-    up = summed("up")
-    out = summed("out")
-    query = summed("query")
-    shared = joined(
-        [reduce_pieces(shared_pieces(g), section, i) for i, g in enumerate((grads_0, grads_1))],
-        section,
-    )
-    shared = lax.all_gather(shared, ("gx", "gy"), axis=0, tiled=True).astype(F32).T * scale
-    gain_sums = lax.psum(
-        jnp.stack([grads_0["gains"], grads_1["gains"]]), ("section", "gx", "gy", "dp")
-    )
-    gain_sums = jnp.where(section == 0, gain_sums[0], gain_sums[1]) * scale
+    def finished(own_0, got_0, own_1, got_1):
+        own, got = pick(section == 0, own_0, own_1), pick(section == 0, got_0, got_1)
+        return jnp.concatenate([pick(section == 0, own, got), pick(section == 0, got, own)])
+
+    ffn = finished(ffn_0, ffn_0_got, ffn_1, ffn_1_got)
+    attn = finished(attn_0, attn_0_got, attn_1, attn_1_got)
+    heads, hidden = w_query.shape[2] // 2, w_gate.shape[2] // 2
+    quarter = attn[2 * heads : -GAIN_ROWS]
+    quarter_beside = swap(quarter, "gy")
+    shared_half = pick(
+        gy == 0,
+        jnp.concatenate([quarter, quarter_beside]),
+        jnp.concatenate([quarter_beside, quarter]),
+    )
+    gain_sums = attn[-GAIN_ROWS : 2 - GAIN_ROWS].astype(F32) * scale
+    ffn_other = swap(ffn, "gx")
+    attn_other = swap(jnp.concatenate([attn[: 2 * heads], shared_half]), "gx")
+
+    def both_cores(mine, other):
+        low, high = pick(gx == 0, mine, other), pick(gx == 0, other, mine)
+        return jnp.concatenate([low, high]).astype(F32) * scale
+
+    gate = both_cores(ffn[:hidden], ffn_other[:hidden]).T
+    up = both_cores(ffn[hidden : 2 * hidden], ffn_other[hidden : 2 * hidden]).T
+    down = both_cores(ffn[2 * hidden :], ffn_other[2 * hidden :])
+    query = both_cores(attn[:heads], attn_other[:heads]).T
+    out = both_cores(attn[heads : 2 * heads], attn_other[heads : 2 * heads])
+    shared = both_cores(shared_half, attn_other[2 * heads :]).T
 
     return (
         by_micro(states, other_states),
         by_micro(in_grads, other_grads),
         gain_sums[:1],
-        both_cores(query, 1, scale)[None],
+        query[None],
         shared[None, :, :HD],
         shared[None, :, HD:],
-        both_cores(out, 0, scale)[None],
+        out[None],
         gain_sums[1:],
-        both_cores(gate, 1, scale)[None],
-        both_cores(up, 1, scale)[None],
-        both_cores(down, 0, scale)[None],
+        gate[None],
+        up[None],
+        down[None],
     )
 
 

time: 778 us -> 683 us (0.88); the launches traced: 768 us -> 681 us
  blocking collectives: 62.6 us -> 0 us
  starting transfers between devices: 117 us -> 62.1 us
  waiting for transfers between devices: 281 us -> 311 us
  matrix products: 158 us -> 142 us
  local copies, waits for them, and re-layouts: 38.8 us -> 47.8 us
  other arithmetic: 92.4 us -> 101 us
    psum x1 -> x4, waiting for transfers between devices: 56.9 us -> 110 us  [the longest x1 37.3 us: local(): ffn_0 = lax.psum(ffn_0, 'dp')]
    psum x1 -> x0, blocking collectives: 48 us -> none  [local(): lax.psum(jnp.stack([grads_0['gains'], grads_1['gains']]), ('section', 'gx...]
    ppermute x73 -> x44, waiting for transfers between devices: 210 us -> 173 us  [swap(): return lax.ppermute(value, axis, [(0, 1), (1, 0)])]
    ppermute x12 -> x4, starting transfers between devices: 38.4 us -> 8.05 us  [to_owner(): return lax.ppermute(value, 'section', [(1 - layer, layer)])]
    ppermute x73 -> x44, starting transfers between devices: 66.9 us -> 43.5 us  [swap(): return lax.ppermute(value, axis, [(0, 1), (1, 0)])]
    all_gather x1 -> x0, blocking collectives: 14.6 us -> none  [local(): lax.all_gather(shared, ('gx', 'gy'), axis=0, tiled=True).astype(F32)]
    dot_general x48, matrix products: 53.3 us -> 40.6 us  [mm_t(): lax.dot_general(a, b, (((1,), (1,)), ((), ())), preferred_element_type=F32)]
    another operation x32 -> x5, other arithmetic: 15.2 us -> 2.88 us  [the longest x12 5.94 us: reduce_pieces(): got = swap(jnp.stack([pieces[2], pieces[3]]), 'gx')]
  transfers between devices with their start and end apart: 90 -> 56, of which waited for: 35 -> 20; matrix products, arithmetic and copies ran while one was open for 27% -> 31% of each run, Pallas kernels for 0% -> 0%
where the time goes in v2:
time: 683 us; the launch traced here: 681 us
  waiting for transfers between devices  311 us (46%)
  matrix products  142 us (21%)
  other arithmetic  101 us (15%)
  starting transfers between devices  62.1 us (9%)
  local copies, waits for them, and re-layouts  47.8 us (7%)
  between operations  17.2 us (3%)
    ppermute x44, waiting for transfers between devices, swap(): return lax.ppermute(value, axis, [(0, 1), (1, 0)])  173 us
    dot_general x46, matrix products, t_mm(): lax.dot_general(a, b, (((0,), (0,)), ((), ())), preferred_element_type=F32)  53.9 us
    dot_general x48, matrix products, mm(): return jnp.dot(a, b, preferred_element_type=F32)  47.3 us
    ppermute x44, starting transfers between devices, swap(): return lax.ppermute(value, axis, [(0, 1), (1, 0)])  43.5 us
    dot_general x48, matrix products, mm_t(): lax.dot_general(a, b, (((1,), (1,)), ((), ())), preferred_element_type=F32)  40.6 us
    psum x1, waiting for transfers between devices, local(): ffn_0 = lax.psum(ffn_0, 'dp')  37.3 us
    unnamed x383, local copies, waits for them, and re-layouts  37 us
    psum x1, waiting for transfers between devices, local(): attn_1 = lax.psum(attn_1, 'dp')  30.3 us
  transfers between devices with their start and end apart: 56, of which 20 were waited for; matrix products, arithmetic and copies ran while one was open for 31% of the time, Pallas kernels for 0%

profile of v2, /device:TPU:0, one launch (start us, length us, event | category | flops | bytes accessed | tf_op | source)
XLA Modules:
  0.0 681.1 jit_solution(15571612552661795363)
XLA Ops:
  24.1 10.9 %collective-permute-done = f32[2,640]{1,0:T(2,128)S(1)} collective-permute-done((f32[2,640]{1,0:T(2,128)S(1)}, f32[2,640]{1,0:T(2,128)S(1)}, u32[]{:S(2)}, u32[]{:S(2)}) %collective-permute-start) | collective-permute-done | bytes 5152 | tf_op jit(solution)/shard_map/ppermute | solution.py:16
  45.0 9.9 %collective-permute-done.2 = bf16[640,256]{1,0:T(8,128)(2,1)S(1)} collective-permute-done((bf16[640,256]{1,0:T(8,128)(2,1)S(1)}, bf16[640,256]{1,0:T(8,128)(2,1)S(1)}, u32[]{:S(2)}, u32[]{:S(2)}) %collective-permute-start.2) | collective-permute-done | bytes 327712 | tf_op jit(solution)/shard_map/ppermute | solution.py:16
  69.5 22.8 %collective-permute-done.13 = bf16[1024,640]{1,0:T(8,128)(2,1)S(1)} collective-permute-done((bf16[1024,640]{1,0:T(8,128)(2,1)S(1)}, bf16[1024,640]{1,0:T(8,128)(2,1)S(1)}, u32[]{:S(2)}, u32[]{:S(2)}) %collective-permute-start.13) | collective-permute-done | bytes 1310752 | tf_op jit(solution)/shard_map/ppermute | solution.py:16
  92.3 3.8 collective-permute-start.6
  99.1 6.2 collective-permute-done.6
  121.5 12.1 %collective-permute-done.14 = bf16[640,1024]{1,0:T(8,128)(2,1)S(1)} collective-permute-done((bf16[640,1024]{1,0:T(8,128)(2,1)S(1)}, bf16[640,1024]{1,0:T(8,128)(2,1)S(1)}, u32[]{:S(2)}, u32[]{:S(2)}) %collective-permute-start.14) | collective-permute-done | bytes 1310752 | tf_op jit(solution)/shard_map/ppermute | solution.py:16
  143.3 5.9 collective-permute-done.18
  157.0 22.5 %collective-permute-done.25 = bf16[640,1024]{1,0:T(8,128)(2,1)S(1)} collective-permute-done((bf16[640,1024]{1,0:T(8,128)(2,1)S(1)}, bf16[640,1024]{1,0:T(8,128)(2,1)S(1)}, u32[]{:S(2)}, u32[]{:S(2)}) %collective-permute-start.25) | collective-permute-done | bytes 1310752 | tf_op jit(solution)/shard_map/ppermute | solution.py:16
  180.5 13.7 %fusion.510 = (f32[1,512,128]{1,2,0:T(8,128)S(1)}, f32[1,512,128]{1,2,0:T(8,128)S(1)}, bf16[512,128]{0,1:T(8,128)(2,1)S(1)}, bf16[512,128]{0,1:T(8,128)(2,1)S(1)...) fusion(f32[512,256]{0,1:T(8,128)S(1)} %fusion.705, ...), kind=kLoop, calls=%fused_computation.754 | loop fusion | flops 1769472 | bytes 3934720 | tf_op jit(solution)/shard_map/concatenate | solution.py:45
  199.7 9.9 %collective-permute-done.21 = bf16[512,512]{0,1:T(8,128)(2,1)S(1)} collective-permute-done((bf16[512,512]{0,1:T(8,128)(2,1)S(1)}, bf16[512,512]{0,1:T(8,128)(2,1)S(1)}, u32[]{:S(2)}, u32[]{:S(2)}) %collective-permute-start.21) | collective-permute-done | bytes 524320 | tf_op jit(solution)/shard_map/ppermute | solution.py:134
  249.2 3.5 multiply_convert_fusion.1
  252.7 3.6 convolution_bitcast_fusion.1
  331.8 34.5 %collective-permute-done.32 = bf16[1536,640]{1,0:T(8,128)(2,1)S(1)} collective-permute-done((bf16[1536,640]{1,0:T(8,128)(2,1)S(1)}, bf16[1536,640]{1,0:T(8,128)(2,1)S(1)}, u32[]{:S(2)}, u32[]{:S(2)}) %collective-permute-start.32) | collective-permute-done | bytes 1966112 | tf_op jit(solution)/shard_map/ppermute | solution.py:16
  368.9 15.5 %collective-permute-done.35 = bf16[672,640]{1,0:T(8,128)(2,1)S(1)} collective-permute-done((bf16[672,640]{1,0:T(8,128)(2,1)S(1)}, bf16[672,640]{1,0:T(8,128)(2,1)S(1)}, u32[]{:S(2)}, u32[]{:S(2)}) %collective-permute-start.35) | collective-permute-done | bytes 860192 | tf_op jit(solution)/shard_map/ppermute | solution.py:16
  395.5 5.3 multiply_reduce_fusion
  440.6 24.3 %collective-permute-done.39 = bf16[1536,640]{1,0:T(8,128)(2,1)} collective-permute-done((bf16[1536,640]{1,0:T(8,128)(2,1)}, bf16[1536,640]{1,0:T(8,128)(2,1)}, u32[]{:S(2)}, u32[]{:S(2)}) %collective-permute-start.39) | collective-permute-done | bytes 1966112 | tf_op jit(solution)/shard_map/ppermute | solution.py:16
  474.4 13.2 %all-reduce.7.cloned.1.call-done = bf16[768,640]{1,0:T(8,128)(2,1)} async-done(((bf16[768,640]{1,0:T(8,128)(2,1)}), bf16[768,640]{1,0:T(8,128)(2,1)}) %all-reduce.7.cloned.1.call-update) | async-done | bytes 983056 | tf_op jit(solution)/shard_map/psum | solution.py:328
  497.1 30.3 %all-reduce.9.cloned.1.call-done = bf16[336,640]{1,0:T(8,128)(2,1)} async-done(((bf16[336,640]{1,0:T(8,128)(2,1)}), bf16[336,640]{1,0:T(8,128)(2,1)}) %all-reduce.9.cloned.1.call-update) | async-done | bytes 430096 | tf_op jit(solution)/shard_map/psum | solution.py:334
  533.9 8.4 %collective-permute-done.44 = bf16[336,640]{1,0:T(8,128)(2,1)S(1)} collective-permute-done((bf16[336,640]{1,0:T(8,128)(2,1)S(1)}, bf16[336,640]{1,0:T(8,128)(2,1)S(1)}, u32[]{:S(2)}, u32[]{:S(2)}) %collective-permute-start.44) | collective-permute-done | bytes 430112 | tf_op jit(solution)/shard_map/ppermute | solution.py:16
  543.1 37.3 %all-reduce.11.cloned.1.call-done = bf16[768,640]{1,0:T(8,128)(2,1)} async-done(((bf16[768,640]{1,0:T(8,128)(2,1)}), bf16[768,640]{1,0:T(8,128)(2,1)}) %all-reduce.11.cloned.1.call-update) | async-done | bytes 983056 | tf_op jit(solution)/shard_map/psum | solution.py:339
  583.8 3.4 collective-permute-start.50
  590.6 29.1 %all-reduce.13.cloned.1.call-done = bf16[336,640]{1,0:T(8,128)(2,1)} async-done(((bf16[336,640]{1,0:T(8,128)(2,1)}), bf16[336,640]{1,0:T(8,128)(2,1)}) %all-reduce.13.cloned.1.call-update) | async-done | bytes 430096 | tf_op jit(solution)/shard_map/psum | solution.py:343
  625.8 8.8 %collective-permute-done.45 = bf16[336,640]{1,0:T(8,128)(2,1)S(1)} collective-permute-done((bf16[336,640]{1,0:T(8,128)(2,1)}, bf16[336,640]{1,0:T(8,128)(2,1)S(1)}, u32[]{:S(2)}, u32[]{:S(2)}) %collective-permute-start.45) | collective-permute-done | bytes 430112 | tf_op jit(solution)/shard_map/ppermute | solution.py:259
  643.0 3.8 collective-permute-done.38
  (751 shorter events, 325.5 us)
Async XLA Ops:
  7.2 480.4 %all-reduce.7.cloned.1.call-start = ((), (), s32[]{:S(2)}) async-start(), calls=%async_computation | async-start | bytes 1966080 | tf_op jit(solution)/shard_map/psum | solution.py:328
  18.8 43.5 %collective-permute-start.11 = (bf16[640,1024]{1,0:T(8,128)(2,1)}, bf16[640,1024]{1,0:T(8,128)(2,1)}, u32[]{:S(2)}, u32[]{:S(2)}) collective-permute-start(bf16[640,1024]{1,0:T(8,128)(2,1)} %pad_maximum_fusion.1), channel_id=1, source_target_pairs={{0,16},{16,0},{1,17},{17,1},{2,18},{18,2},{3,19},{19,3},{4,20},{20... | collective-permute-start | bytes 3932168 | tf_op jit(solution)/shard_map/ppermute | solution.py:16
  37.3 79.1 %collective-permute-start.9 = (bf16[256,640]{1,0:T(8,128)(2,1)S(1)}, bf16[256,640]{1,0:T(8,128)(2,1)S(1)}, u32[]{:S(2)}, u32[]{:S(2)}) collective-permute-start(bf16[256,640]{1,0:T(8,128)(2,1)S(1)} %get-tuple-element.163), channel_id=1, source_target_pairs={{0,8},{8,0},{1,9},{9,1},{2,10},{10,2},{3,11},{11,3},{4,12},{12,4},... | collective-permute-start | bytes 983048 | tf_op jit(solution)/shard_map/ppermute | solution.py:16
  66.0 151.1 %collective-permute-start.23 = (bf16[256,640]{1,0:T(8,128)(2,1)S(1)}, bf16[256,640]{1,0:T(8,128)(2,1)S(1)}, u32[]{:S(2)}, u32[]{:S(2)}) collective-permute-start(bf16[256,640]{1,0:T(8,128)(2,1)S(1)} %get-tuple-element.164), channel_id=1, source_target_pairs={{0,8},{8,0},{1,9},{9,1},{2,10},{10,2},{3,11},{11,3},{4,12},{12,4},... | collective-permute-start | bytes 983048 | tf_op jit(solution)/shard_map/ppermute | solution.py:16
  66.1 51.2 %collective-permute-start.10 = (bf16[256,640]{1,0:T(8,128)(2,1)S(1)}, bf16[256,640]{1,0:T(8,128)(2,1)S(1)}, u32[]{:S(2)}, u32[]{:S(2)}) collective-permute-start(bf16[256,640]{1,0:T(8,128)(2,1)S(1)} %collective-permute-done.8), channel_id=1, source_target_pairs={{0,8},{8,0},{1,9},{9,1},{2,10},{10,2},{3,11},{11,3},{4,12},{12,4},... | collective-permute-start | bytes 983048 | tf_op jit(solution)/shard_map/ppermute | solution.py:16
  66.6 151.3 %collective-permute-start.24 = (bf16[256,640]{1,0:T(8,128)(2,1)S(1)}, bf16[256,640]{1,0:T(8,128)(2,1)S(1)}, u32[]{:S(2)}, u32[]{:S(2)}) collective-permute-start(bf16[256,640]{1,0:T(8,128)(2,1)S(1)} %collective-permute-done.22), channel_id=1, source_target_pairs={{0,8},{8,0},{1,9},{9,1},{2,10},{10,2},{3,11},{11,3},{4,12},{12,4},... | collective-permute-start | bytes 983048 | tf_op jit(solution)/shard_map/ppermute | solution.py:16
  142.7 37.3 %collective-permute-start.19 = (bf16[640,256]{1,0:T(8,128)(2,1)S(1)}, bf16[640,256]{1,0:T(8,128)(2,1)S(1)}, u32[]{:S(2)}, u32[]{:S(2)}) collective-permute-start(bf16[640,256]{1,0:T(8,128)(2,1)S(1)} %get-tuple-element.149), channel_id=1, source_target_pairs={{0,8},{8,0},{1,9},{9,1},{2,10},{10,2},{3,11},{11,3},{4,12},{12,4},... | collective-permute-start | bytes 983048 | tf_op jit(solution)/shard_map/ppermute | solution.py:16
  156.4 66.7 %collective-permute-start.26 = (bf16[640,1024]{1,0:T(8,128)(2,1)S(1)}, bf16[640,1024]{1,0:T(8,128)(2,1)S(1)}, u32[]{:S(2)}, u32[]{:S(2)}) collective-permute-start(bf16[640,1024]{1,0:T(8,128)(2,1)S(1)} %get-tuple-element.89), channel_id=1, source_target_pairs={{0,8},{8,0},{1,9},{9,1},{2,10},{10,2},{3,11},{11,3},{4,12},{12,4},... | collective-permute-start | bytes 3932168 | tf_op jit(solution)/shard_map/ppermute | solution.py:16
  179.4 53.0 %collective-permute-start.28 = (bf16[640,1024]{1,0:T(8,128)(2,1)S(1)}, bf16[640,1024]{1,0:T(8,128)(2,1)S(1)}, u32[]{:S(2)}, u32[]{:S(2)}) collective-permute-start(bf16[640,1024]{1,0:T(8,128)(2,1)S(1)} %collective-permute-done.25), channel_id=1, source_target_pairs={{0,8},{8,0},{1,9},{9,1},{2,10},{10,2},{3,11},{11,3},{4,12},{12,4},... | collective-permute-start | bytes 3932168 | tf_op jit(solution)/shard_map/ppermute | solution.py:16
  270.6 46.6 %collective-permute-start.31 = (bf16[3072,640]{1,0:T(8,128)(2,1)S(1)}, bf16[3072,640]{1,0:T(8,128)(2,1)S(1)}, u32[]{:S(2)}, u32[]{:S(2)}) collective-permute-start(bf16[3072,640]{1,0:T(8,128)(2,1)S(1)} %fusion.66), channel_id=1, source_target_pairs={{0,8},{8,0},{1,9},{9,1},{2,10},{10,2},{3,11},{11,3},{4,12},{12,4},... | collective-permute-start | bytes 11796488 | tf_op jit(solution)/shard_map/ppermute | solution.py:16
  293.0 35.5 %collective-permute-start.34 = (bf16[1344,640]{1,0:T(8,128)(2,1)}, bf16[1344,640]{1,0:T(8,128)(2,1)}, u32[]{:S(2)}, u32[]{:S(2)}) collective-permute-start(bf16[1344,640]{1,0:T(8,128)(2,1)} %get-tuple-element.205), channel_id=1, source_target_pairs={{0,8},{8,0},{1,9},{9,1},{2,10},{10,2},{3,11},{11,3},{4,12},{12,4},... | collective-permute-start | bytes 5160968 | tf_op jit(solution)/shard_map/ppermute | solution.py:16
  307.6 77.7 %collective-permute-start.36 = (bf16[3072,640]{1,0:T(8,128)(2,1)}, bf16[3072,640]{1,0:T(8,128)(2,1)}, u32[]{:S(2)}, u32[]{:S(2)}) collective-permute-start(bf16[3072,640]{1,0:T(8,128)(2,1)} %fusion.54), channel_id=1, source_target_pairs={{0,8},{8,0},{1,9},{9,1},{2,10},{10,2},{3,11},{11,3},{4,12},{12,4},... | collective-permute-start | bytes 11796488 | tf_op jit(solution)/shard_map/ppermute | solution.py:16
  320.6 45.7 %collective-permute-start.32 = (bf16[1536,640]{1,0:T(8,128)(2,1)S(1)}, bf16[1536,640]{1,0:T(8,128)(2,1)S(1)}, u32[]{:S(2)}, u32[]{:S(2)}) collective-permute-start(bf16[1536,640]{1,0:T(8,128)(2,1)S(1)} %slice.658), channel_id=1, source_target_pairs={{0,4},{4,0},{1,5},{5,1},{2,6},{6,2},{3,7},{7,3},{8,12},{12,8},{9,1... | collective-permute-start | bytes 5898248 | tf_op jit(solution)/shard_map/ppermute | solution.py:16
  330.8 53.5 %collective-permute-start.35 = (bf16[672,640]{1,0:T(8,128)(2,1)S(1)}, bf16[672,640]{1,0:T(8,128)(2,1)S(1)}, u32[]{:S(2)}, u32[]{:S(2)}) collective-permute-start(bf16[672,640]{1,0:T(8,128)(2,1)S(1)} %slice.662), channel_id=1, source_target_pairs={{0,4},{4,0},{1,5},{5,1},{2,6},{6,2},{3,7},{7,3},{8,12},{12,8},{9,1... | collective-permute-start | bytes 2580488 | tf_op jit(solution)/shard_map/ppermute | solution.py:16
  411.4 53.4 %collective-permute-start.39 = (bf16[1536,640]{1,0:T(8,128)(2,1)}, bf16[1536,640]{1,0:T(8,128)(2,1)}, u32[]{:S(2)}, u32[]{:S(2)}) collective-permute-start(bf16[1536,640]{1,0:T(8,128)(2,1)} %get-tuple-element.26), channel_id=1, source_target_pairs={{0,4},{4,0},{1,5},{5,1},{2,6},{6,2},{3,7},{7,3},{8,12},{12,8},{9,1... | collective-permute-start | bytes 5898248 | tf_op jit(solution)/shard_map/ppermute | solution.py:16
  437.2 33.7 %collective-permute-start.42 = (bf16[1344,640]{1,0:T(8,128)(2,1)}, bf16[1344,640]{1,0:T(8,128)(2,1)}, u32[]{:S(2)}, u32[]{:S(2)}) collective-permute-start(bf16[1344,640]{1,0:T(8,128)(2,1)} %get-tuple-element.201), channel_id=1, source_target_pairs={{0,8},{8,0},{1,9},{9,1},{2,10},{10,2},{3,11},{11,3},{4,12},{12,4},... | collective-permute-start | bytes 5160968 | tf_op jit(solution)/shard_map/ppermute | solution.py:16
  437.2 90.2 %all-reduce.9.cloned.1.call-start = ((), (), s32[]{:S(2)}) async-start(), calls=%async_computation.1 | async-start | bytes 860160 | tf_op jit(solution)/shard_map/psum | solution.py:334
  487.6 40.2 %collective-permute-start.43 = (bf16[672,640]{1,0:T(8,128)(2,1)}, bf16[672,640]{1,0:T(8,128)(2,1)}, u32[]{:S(2)}, u32[]{:S(2)}) collective-permute-start(bf16[672,640]{1,0:T(8,128)(2,1)} %get-tuple-element.32), channel_id=1, source_target_pairs={{0,4},{4,0},{1,5},{5,1},{2,6},{6,2},{3,7},{7,3},{8,12},{12,8},{9,1... | collective-permute-start | bytes 2580488 | tf_op jit(solution)/shard_map/ppermute | solution.py:16
  491.8 88.7 %all-reduce.11.cloned.1.call-start = ((), (), s32[]{:S(2)}) async-start(), calls=%async_computation.2 | async-start | bytes 1966080 | tf_op jit(solution)/shard_map/psum | solution.py:339
  527.4 92.2 %all-reduce.13.cloned.1.call-start = ((), (), s32[]{:S(2)}) async-start(), calls=%async_computation.3 | async-start | bytes 860160 | tf_op jit(solution)/shard_map/psum | solution.py:343
  533.3 47.2 %collective-permute-start.29 = (bf16[512,640]{1,0:T(8,128)(2,1)S(1)}, bf16[512,640]{1,0:T(8,128)(2,1)S(1)}, u32[]{:S(2)}, u32[]{:S(2)}) collective-permute-start(bf16[512,640]{1,0:T(8,128)(2,1)S(1)} %get-tuple-element.247), channel_id=1, source_target_pairs={{0,16},{16,0},{1,17},{17,1},{2,18},{18,2},{3,19},{19,3},{4,20},{20... | collective-permute-start | bytes 1966088 | tf_op jit(solution)/shard_map/ppermute | solution.py:16
  583.8 52.6 %collective-permute-start.50 = (bf16[768,640]{1,0:T(8,128)(2,1)}, bf16[768,640]{1,0:T(8,128)(2,1)S(1)}, u32[]{:S(2)}, u32[]{:S(2)}) collective-permute-start(bf16[768,640]{1,0:T(8,128)(2,1)} %all-reduce.7.cloned.1.call-done), channel_id=1, source_target_pairs={{0,16},{1,17},{2,18},{3,19},{4,20},{5,21},{6,22},{7,23},{8,24},{9,... | collective-permute-start | bytes 2949128 | tf_op jit(solution)/shard_map/ppermute | solution.py:259
  587.2 38.6 %collective-permute-start.46 = (bf16[336,640]{1,0:T(8,128)(2,1)}, bf16[336,640]{1,0:T(8,128)(2,1)}, u32[]{:S(2)}, u32[]{:S(2)}) collective-permute-start(bf16[336,640]{1,0:T(8,128)(2,1)} %all-reduce.9.cloned.1.call-done), channel_id=1, source_target_pairs={{0,16},{1,17},{2,18},{3,19},{4,20},{5,21},{6,22},{7,23},{8,24},{9,... | collective-permute-start | bytes 1290248 | tf_op jit(solution)/shard_map/ppermute | solution.py:259
  589.3 48.0 %collective-permute-start.49 = (bf16[768,640]{1,0:T(8,128)(2,1)}, bf16[768,640]{1,0:T(8,128)(2,1)}, u32[]{:S(2)}, u32[]{:S(2)}) collective-permute-start(bf16[768,640]{1,0:T(8,128)(2,1)} %all-reduce.11.cloned.1.call-done), channel_id=1, source_target_pairs={{16,0},{17,1},{18,2},{19,3},{20,4},{21,5},{22,6},{23,7},{24,8},{25... | collective-permute-start | bytes 2949128 | tf_op jit(solution)/shard_map/ppermute | solution.py:259
  (219 other events, 2890.6 us)
Sparse Core Ops, SparseCore 0:
  437.4 50.2 all-reduce.6
  491.9 35.4 all-reduce.8
  530.4 50.0 all-reduce.10
  583.4 36.2 all-reduce.12

commit v3 on v2

v3 whole, which is shorter than its diff:
```python
import math

import jax
import jax.numpy as jnp
from jax import lax
from jax.experimental import pallas as pl
from jax.experimental.pallas import tpu as pltpu
from jax.sharding import PartitionSpec as P

HD = 256
WINDOW = 512
GAIN_ROWS = 32
F32 = jnp.float32
BF16 = jnp.bfloat16


def swap(value, axis):
    return lax.ppermute(value, axis, [(0, 1), (1, 0)])


def mm(a, b):
    return jnp.dot(a, b, preferred_element_type=F32)


def mm_t(a, b):
    return lax.dot_general(a, b, (((1,), (1,)), ((), ())), preferred_element_type=F32)


def t_mm(a, b):
    return lax.dot_general(a, b, (((0,), (0,)), ((), ())), preferred_element_type=F32)


def inverse_rms(value):
    return lax.rsqrt(jnp.mean(value * value, axis=-1, keepdims=True) + 1e-06)


def norm_back(value, gain, grad):
    s = inverse_rms(value)
    scaled = grad * gain
    to_value = s * scaled - value * (s * s * s) * jnp.mean(value * scaled, axis=-1, keepdims=True)
    return to_value, jnp.sum(grad * value * s, axis=0)


def rotate(value, cos, sin):
    half = value.shape[-1] // 2
    a, b = value[..., :half], value[..., half:]
    return jnp.concatenate([a * cos - b * sin, b * cos + a * sin], axis=-1)


def unrotate(value, cos, sin):
    half = value.shape[-1] // 2
    c, e = value[..., :half], value[..., half:]
    return jnp.concatenate([c * cos + e * sin, e * cos - c * sin], axis=-1)


def gelu_parts(v):
    c = math.sqrt(2.0 / math.pi)
    t = jnp.tanh(c * (v + 0.044715 * v * v * v))
    value = 0.5 * v * (1.0 + t)
    slope = 0.5 * (1.0 + t) + 0.5 * v * (1.0 - t * t) * (c * (1.0 + 3 * 0.044715 * v * v))
    return value, slope


def layout(lengths, rows):
    docs = lengths.shape[0]
    ends = jnp.cumsum(lengths)
    number = jnp.sum((rows[:, None] >= ends[None, :]).astype(jnp.int32), axis=1)
    valid = number < docs
    begin = jnp.sum(
        jnp.where(number[:, None] == jnp.arange(docs)[None, :], (ends - lengths)[None, :], 0), axis=1
    )
    place = jnp.where(valid, rows - begin, 0)
    segment = jnp.where(rows < 0, -1, jnp.where(valid, number, docs + rows))
    return segment, place, valid


def pick(flag, a, b):
    return jnp.where(flag, a, b)


def gather_weights(w_query, w_key, w_value, w_out, w_gate, w_up, w_down, section):
    gx = lax.axis_index("gx")

    def half(w, axis):
        size = w.shape[axis] // 2
        return lax.dynamic_slice_in_dim(w, gx * size, size, axis)

    def two_layers(mine, received):
        return [pick(section == layer, mine, received) for layer in range(2)]

    heads = w_query.shape[1] // 2
    first_own = jnp.concatenate([half(w_query, 1), half(w_key, 1), half(w_value, 1)], axis=1)
    out_own = half(w_out, 0)
    wide_own = jnp.concatenate([half(w_gate, 1), half(w_up, 1)], axis=1)
    down_own = half(w_down, 0)
    first_got = swap(first_own, "section")
    down_beside = swap(down_own, "gy")
    out_got = swap(out_own, "section")
    wide_got = swap(wide_own, "section")
    down_own = jnp.concatenate([down_own, down_beside])
    down_got = swap(down_own, "section")

    shared_got = first_got[:, heads:]
    shared_other = swap(shared_got, "gx")
    low, high = pick(gx == 0, shared_got, shared_other), pick(gx == 0, shared_other, shared_got)
    part = low.shape[1] // 2
    key_got = jnp.concatenate([low[:, :part], high[:, :part]], axis=1)
    value_got = jnp.concatenate([low[:, part:], high[:, part:]], axis=1)
    keys, values = two_layers(w_key, key_got), two_layers(w_value, value_got)

    queries = two_layers(first_own[:, :heads], first_got[:, :heads])
    outs = two_layers(out_own, out_got)
    wides = two_layers(wide_own, wide_got)
    downs = two_layers(down_own, down_got)
    layers = []
    for layer in range(2):
        def pairs(own):
            both = jnp.stack([own, swap(own, "gy")])
            return both, swap(both, "gx")

        down = downs[layer].reshape(2, -1, w_down.shape[1])
        layers.append(
            {
                "query": pairs(queries[layer]),
                "out": pairs(outs[layer]),
                "wide": pairs(wides[layer]),
                "down": (down, swap(down, "gx")),
                "key": keys[layer],
                "value": values[layer],
            }
        )
    return layers


def from_before(value):
    return lax.ppermute(value, ("gx", "gy"), [(0, 1), (1, 2), (2, 3)])


def to_before(value):
    return lax.ppermute(value, ("gx", "gy"), [(1, 0), (2, 1), (3, 2)])


BLOCK = 256
STEPS = 4
PARAMS = dict(
    grid=(STEPS,),
    compiler_params=pltpu.CompilerParams(
        dimension_semantics=("arbitrary",), vmem_limit_bytes=56 * 1024 * 1024
    ),
)


def all_of(shape):
    return pl.BlockSpec(shape, lambda j: (0,) * len(shape))


def step_of(shape):
    return pl.BlockSpec((1,) + shape[1:], lambda j: (j,) + (0,) * (len(shape) - 1))


def first_of(shape):
    return pl.BlockSpec((1,) + shape[1:], lambda j: (jnp.minimum(j, 1),) + (0,) * (len(shape) - 1))


def last_of(shape):
    return pl.BlockSpec(
        (1,) + shape[1:], lambda j: (jnp.maximum(j - 2, 0),) + (0,) * (len(shape) - 1)
    )


def cost(flops, bytes_accessed, transcendentals=0):
    return pl.CostEstimate(
        flops=flops, bytes_accessed=bytes_accessed, transcendentals=transcendentals
    )


def take(step, first, last, held):
    @pl.when(step < 2)
    def _():
        held[...] = first[0]

    @pl.when(step >= 2)
    def _():
        held[...] = last[0]


def put_bias(seg_q, seg_k, bias):
    rows, keys = bias.shape
    distance = (
        lax.broadcasted_iota(jnp.int32, (rows, keys), 0)
        + (keys - rows)
        - lax.broadcasted_iota(jnp.int32, (rows, keys), 1)
    )
    allowed = (distance >= 0) & (distance < WINDOW) & (seg_q[...] == seg_k[...])
    bias[...] = jnp.where(allowed, 0.0, -1e30)


def softmax(scores):
    weights = jnp.exp(scores - jnp.max(scores, axis=-1, keepdims=True))
    return weights * (1.0 / jnp.sum(weights, axis=-1, keepdims=True))


def attn_kernel(
    x_ref, gain, wq_a, wq_b, wk, wv, wo_a, wo_b, cos, sin, seg_q, seg_k,
    q_out, mixed_out, kv_out, normed_out, hidden_out, bias, wq, wo,
):
    j = pl.program_id(0)
    rows = normed_out.shape[0]
    before = x_ref.shape[0] - rows

    @pl.when(j == 0)
    def _():
        x = x_ref[...].astype(F32)
        normed = (x * inverse_rms(x) * gain[...]).astype(BF16)
        normed_out[...] = normed[before:]
        kv_out[:, :HD] = rotate(mm(normed, wk[...]), cos[...], sin[...]).astype(BF16)
        kv_out[:, HD:] = mm(normed, wv[...]).astype(BF16)
        hidden_out[...] = x[before:]
        put_bias(seg_q, seg_k, bias)

    take(j, wq_a, wq_b, wq)
    take(j, wo_a, wo_b, wo)
    q = rotate(mm(normed_out[...], wq[...]), cos[before:, :], sin[before:, :]) * HD**-0.5
    q_out[0] = q.astype(BF16)
    for at in range(0, rows, BLOCK):
        here = pl.ds(at, BLOCK)
        keys = pl.ds(at, before + BLOCK)
        scores = mm_t(q_out[0, here, :], kv_out[keys, :HD]) + bias[here, keys]
        mixed = mm(softmax(scores).astype(BF16), kv_out[keys, HD:]).astype(BF16)
        mixed_out[0, here, :] = mixed
        hidden_out[here, :] += mm(mixed, wo[...])


def attn_forward(x_all, w, place):
    cos, sin, seg_q, seg_k = place
    total, width = x_all.shape
    rows = seg_q.shape[0]
    heads = (STEPS, rows, HD)
    ops = (x_all, w["gain_attn"], *w["query"], w["key"], w["value"], *w["out"], cos, sin, seg_q, seg_k)
    pairs = {2: first_of, 3: last_of, 6: first_of, 7: last_of}
    return pl.pallas_call(
        attn_kernel,
        out_shape=(
            jax.ShapeDtypeStruct(heads, BF16),
            jax.ShapeDtypeStruct(heads, BF16),
            jax.ShapeDtypeStruct((total, 2 * HD), BF16),
            jax.ShapeDtypeStruct((rows, width), BF16),
            jax.ShapeDtypeStruct((rows, width), F32),
        ),
        in_specs=[pairs.get(i, all_of)(op.shape) for i, op in enumerate(ops)],
        out_specs=(
            step_of(heads),
            step_of(heads),
            all_of((total, 2 * HD)),
            all_of((rows, width)),
            all_of((rows, width)),
        ),
        scratch_shapes=[
            pltpu.VMEM((rows, total), F32),
            pltpu.VMEM((width, HD), BF16),
            pltpu.VMEM((HD, width), BF16),
        ],
        cost_estimate=cost(8 * 10**9, 12 * 10**6, 2 * 10**6),
        **PARAMS,
    )(*ops)


def ffn_kernel(hidden, gain, wide_a, wide_b, down_a, down_b, out, normed, total, wide, down):
    j = pl.program_id(0)
    units = down.shape[0]

    @pl.when(j == 0)
    def _():
        value = hidden[...]
        normed[...] = (value * inverse_rms(value) * gain[...]).astype(BF16)
        total[...] = value

    take(j, wide_a, wide_b, wide)
    take(j, down_a, down_b, down)
    gate = mm(normed[...], wide[:, :units])
    up = mm(normed[...], wide[:, units:])
    act = (gelu_parts(gate)[0] * up).astype(BF16)
    total[...] += mm(act, down[...])

    @pl.when(j == STEPS - 1)
    def _():
        out[...] = total[...].astype(BF16)


def ffn_forward(hidden, w):
    rows, width = hidden.shape
    ops = (hidden, w["gain_ff"], *w["wide"], *w["down"])
    units = w["down"][0].shape[1]
    pairs = {2: first_of, 3: last_of, 4: first_of, 5: last_of}
    return pl.pallas_call(
        ffn_kernel,
        out_shape=jax.ShapeDtypeStruct((rows, width), BF16),
        in_specs=[pairs.get(i, all_of)(op.shape) for i, op in enumerate(ops)],
        out_specs=all_of((rows, width)),
        scratch_shapes=[
            pltpu.VMEM((rows, width), BF16),
            pltpu.VMEM((rows, width), F32),
            pltpu.VMEM((width, 2 * units), BF16),
            pltpu.VMEM((units, width), BF16),
        ],
        cost_estimate=cost(8 * 10**9, 12 * 10**6, 10**6),
        **PARAMS,
    )(*ops)


def ffn_back_kernel(
    dy, hidden, gain, wide_a, wide_b, down_a, down_b,
    near, far, d_hidden, d_gain, normed, total, wide, down,
):
    j = pl.program_id(0)
    units = down.shape[0]

    @pl.when(j == 0)
    def _():
        value = hidden[...]
        normed[...] = (value * inverse_rms(value) * gain[...]).astype(BF16)
        total[...] = jnp.zeros_like(total)

    take(j, wide_a, wide_b, wide)
    take(j, down_a, down_b, down)
    gate = mm(normed[...], wide[:, :units])
    up = mm(normed[...], wide[:, units:])
    d_act = mm_t(dy[...], down[...])
    value, slope = gelu_parts(gate)
    act = (value * up).astype(BF16)
    d_gate = (d_act * up * slope).astype(BF16)
    d_up = (d_act * value).astype(BF16)
    total[...] += mm_t(d_gate, wide[:, :units]) + mm_t(d_up, wide[:, units:])
    parts = [t_mm(d_gate, normed[...]), t_mm(d_up, normed[...]), t_mm(act, dy[...])]

    def put(out):
        for i, part in enumerate(parts):
            out[0, pl.ds(i * units, units), :] = part.astype(BF16)

    pl.when(j < 2)(lambda: put(near))
    pl.when(j >= 2)(lambda: put(far))

    @pl.when(j == STEPS - 1)
    def _():
        to_hidden, to_gain = norm_back(hidden[...], gain[...], total[...])
        d_hidden[...] = dy[...].astype(F32) + to_hidden
        d_gain[...] = to_gain[None]


def ffn_back(dy, hidden, w):
    rows, width = hidden.shape
    ops = (dy, hidden, w["gain_ff"], *w["wide"], *w["down"])
    units = w["down"][0].shape[1]
    pairs = {3: first_of, 4: last_of, 5: first_of, 6: last_of}
    packed = (2, 3 * units, width)
    return pl.pallas_call(
        ffn_back_kernel,
        out_shape=(
            jax.ShapeDtypeStruct(packed, BF16),
            jax.ShapeDtypeStruct(packed, BF16),
            jax.ShapeDtypeStruct((rows, width), F32),
            jax.ShapeDtypeStruct((1, width), F32),
        ),
        in_specs=[pairs.get(i, all_of)(op.shape) for i, op in enumerate(ops)],
        out_specs=(first_of(packed), last_of(packed), all_of((rows, width)), all_of((1, width))),
        scratch_shapes=[
            pltpu.VMEM((rows, width), BF16),
            pltpu.VMEM((rows, width), F32),
            pltpu.VMEM((width, 2 * units), BF16),
            pltpu.VMEM((units, width), BF16),
        ],
        cost_estimate=cost(16 * 10**9, 24 * 10**6, 10**6),
        **PARAMS,
    )(*ops)


def attn_back_kernel(
    d_hidden, q, mixed, kv, wo_a, wo_b, cos, sin, seg_q, seg_k,
    d_out, d_q, d_kv, bias, wo, grad,
):
    j = pl.program_id(0)
    rows = grad.shape[0]
    before = kv.shape[0] - rows

    @pl.when(j == 0)
    def _():
        grad[...] = d_hidden[...].astype(BF16)
        d_kv[...] = jnp.zeros_like(d_kv)
        put_bias(seg_q, seg_k, bias)

    take(j, wo_a, wo_b, wo)
    d_out[0] = t_mm(mixed[0], grad[...]).astype(BF16)
    for at in range(0, rows, BLOCK):
        here = pl.ds(at, BLOCK)
        keys = pl.ds(at, before + BLOCK)
        q_here = q[0, here, :]
        d_mixed = mm_t(grad[here, :], wo[...]).astype(BF16)
        probs = softmax(mm_t(q_here, kv[keys, :HD]) + bias[here, keys])
        d_probs = mm_t(d_mixed, kv[keys, HD:])
        inner = jnp.sum(probs * d_probs, axis=-1, keepdims=True)
        d_scores = (probs * (d_probs - inner)).astype(BF16)
        back = unrotate(mm(d_scores, kv[keys, :HD]), cos[here, :], sin[here, :]) * HD**-0.5
        d_q[0, here, :] = back.astype(BF16)
        d_kv[keys, :HD] += t_mm(d_scores, q_here)
        d_kv[keys, HD:] += t_mm(probs.astype(BF16), d_mixed)


def attn_back(d_hidden, q, mixed, kv, w, place):
    cos, sin, seg_q, seg_k = place
    rows, width = d_hidden.shape
    total = kv.shape[0]
    cos, sin = cos[total - rows :], sin[total - rows :]
    ops = (d_hidden, q, mixed, kv, *w["out"], cos, sin, seg_q, seg_k)
    pairs = {1: step_of, 2: step_of, 4: first_of, 5: last_of}
    outs = (STEPS, HD, width)
    return pl.pallas_call(
        attn_back_kernel,
        out_shape=(
            jax.ShapeDtypeStruct(outs, BF16),
            jax.ShapeDtypeStruct(q.shape, BF16),
            jax.ShapeDtypeStruct((total, 2 * HD), F32),
        ),
        in_specs=[pairs.get(i, all_of)(op.shape) for i, op in enumerate(ops)],
        out_specs=(step_of(outs), step_of(q.shape), all_of((total, 2 * HD))),
        scratch_shapes=[
            pltpu.VMEM((rows, total), F32),
            pltpu.VMEM((HD, width), BF16),
            pltpu.VMEM((rows, width), BF16),
        ],
        cost_estimate=cost(10 * 10**9, 12 * 10**6, 2 * 10**6),
        **PARAMS,
    )(*ops)


def query_back_kernel(d_q, normed, wq_a, wq_b, d_query, d_normed, wq):
    j = pl.program_id(0)
    take(j, wq_a, wq_b, wq)
    d_query[0] = t_mm(d_q[0], normed[...]).astype(BF16)
    term = mm_t(d_q[0], wq[...])

    @pl.when(j == 0)
    def _():
        d_normed[...] = term

    @pl.when(j > 0)
    def _():
        d_normed[...] += term


def query_back(d_q, normed, w):
    rows, width = normed.shape
    ops = (d_q, normed, *w["query"])
    outs = (STEPS, HD, width)
    pairs = {0: step_of, 2: first_of, 3: last_of}
    return pl.pallas_call(
        query_back_kernel,
        out_shape=(jax.ShapeDtypeStruct(outs, BF16), jax.ShapeDtypeStruct((rows, width), F32)),
        in_specs=[pairs.get(i, all_of)(op.shape) for i, op in enumerate(ops)],
        out_specs=(step_of(outs), all_of((rows, width))),
        scratch_shapes=[pltpu.VMEM((width, HD), BF16)],
        cost_estimate=cost(2 * 10**9, 6 * 10**6),
        **PARAMS,
    )(*ops)


def input_back_kernel(
    d_kv, behind, normed, wk, wv, d_normed, x_ref, gain, d_hidden, cos, sin, d_x, d_shared, d_gain
):
    total = d_kv[...] + behind[...].astype(F32)
    d_k = unrotate(total[:, :HD], cos[...], sin[...]).astype(BF16)
    d_v = total[:, HD:].astype(BF16)
    d_shared[:HD, :] = t_mm(d_k, normed[...]).astype(BF16)
    d_shared[HD:, :] = t_mm(d_v, normed[...]).astype(BF16)
    grad = d_normed[...] + mm_t(d_k, wk[...]) + mm_t(d_v, wv[...])
    to_x, to_gain = norm_back(x_ref[...].astype(F32), gain[...], grad)
    d_x[...] = (d_hidden[...] + to_x).astype(BF16)
    d_gain[...] = to_gain[None]


def input_back(d_kv, behind, normed, d_normed, x, d_hidden, w, place):
    cos, sin = place[:2]
    rows, width = normed.shape
    before = cos.shape[0] - rows
    ops = (
        d_kv[before:], behind, normed, w["key"], w["value"], d_normed, x, w["gain_attn"], d_hidden,
        cos[before:], sin[before:],
    )
    return pl.pallas_call(
        input_back_kernel,
        out_shape=(
            jax.ShapeDtypeStruct((rows, width), BF16),
            jax.ShapeDtypeStruct((2 * HD, width), BF16),
            jax.ShapeDtypeStruct((1, width), F32),
        ),
        compiler_params=pltpu.CompilerParams(vmem_limit_bytes=56 * 1024 * 1024),
        cost_estimate=cost(10**9, 8 * 10**6),
    )(*ops)


def pack_attn(d_query, d_out, d_shared, d_gain_attn, d_gain_ff, order):
    gains = jnp.concatenate([d_gain_attn, d_gain_ff])
    gains = jnp.pad(gains, ((0, GAIN_ROWS - 2), (0, 0))).astype(BF16)
    count = d_shared.shape[0] // STEPS
    pieces = []
    for j in range(STEPS):
        quarter = lax.dynamic_slice_in_dim(d_shared, (order ^ j) * count, count, 0)
        pieces.append(jnp.concatenate([d_query[j], d_out[j], quarter, gains]))
    return jnp.stack(pieces[:2]), jnp.stack(pieces[2:])


def over_cores(near, far):
    kept = near + swap(far, "gx")
    return kept[0], kept[1]


def over_section(total, section):
    half = total.shape[0] // 2
    low, high = total[:half], total[half:]
    return pick(section == 0, low, high) + swap(pick(section == 0, high, low), "section")


def to_owner(value, layer):
    return lax.ppermute(value, "section", [(1 - layer, layer)])


def local(
    x_input,
    doc_lengths,
    cotangent,
    gain_attn,
    w_query,
    w_key,
    w_value,
    w_out,
    gain_ff,
    w_gate,
    w_up,
    w_down,
):
    section = lax.axis_index("section")
    gx, gy = lax.axis_index("gx"), lax.axis_index("gy")
    own_rows = x_input.shape[2]
    scale = 1.0 / lax.axis_size("dp")

    weights = gather_weights(
        w_query[0], w_key[0], w_value[0], w_out[0], w_gate[0], w_up[0], w_down[0], section
    )
    gains = jnp.concatenate([gain_attn, gain_ff])
    other_gains = swap(gains, "section")
    for layer in range(2):
        here = pick(section == layer, gains, other_gains)
        weights[layer]["gain_attn"], weights[layer]["gain_ff"] = here[:1], here[1:]

    def mine(value):
        return lax.dynamic_index_in_dim(value[:, 0], section, 0, keepdims=False)

    x = mine(x_input)
    x_all = jnp.concatenate([from_before(x), x])
    start = (gx * lax.axis_size("gy") + gy) * own_rows
    rows = start - WINDOW + jnp.arange(WINDOW + own_rows, dtype=jnp.int32)
    segment, where_in, valid = layout(mine(doc_lengths), rows)
    frequency = jnp.exp(jnp.arange(HD // 2, dtype=F32) * (-2.0 * math.log(10000.0) / HD))
    angles = where_in.astype(F32)[:, None] * frequency[None, :]
    place = (jnp.cos(angles), jnp.sin(angles), segment[WINDOW:, None], segment[None, :])

    q_0, mixed_0, kv_0, normed_0, hidden_0 = attn_forward(x_all, weights[0], place)
    out_0 = ffn_forward(hidden_0, weights[0])
    out_all = jnp.concatenate([from_before(out_0), out_0])
    q_1, mixed_1, kv_1, normed_1, hidden_1 = attn_forward(out_all, weights[1], place)
    out_1 = ffn_forward(hidden_1, weights[1])
    states = pick(section == 0, out_0, out_1)
    other_states = swap(pick(section == 0, out_1, out_0), "section")

    order = 2 * gx + gy
    barrier = lax.optimization_barrier
    dy = jnp.where(valid[WINDOW:, None], mine(cotangent), 0)

    near, far, d_hidden, gain_ff = ffn_back(dy, hidden_1, weights[1])
    ffn_1, ffn_far_1 = over_cores(near, far)
    d_out, d_q, d_kv = attn_back(d_hidden, q_1, mixed_1, kv_1, weights[1], place)
    d_q, d_kv, ffn_1, ffn_far_1 = barrier((d_q, d_kv, ffn_1, ffn_far_1))
    ffn_got = swap(ffn_far_1, "gy")
    behind = to_before(d_kv[:WINDOW].astype(BF16))
    d_query, d_normed = query_back(d_q, normed_1, weights[1])
    grad_1, d_shared, gain_attn_grad = input_back(
        d_kv, behind, normed_1, d_normed, out_0, d_hidden, weights[1], place
    )
    attn_1, attn_far_1 = over_cores(
        *pack_attn(d_query, d_out, d_shared, gain_attn_grad, gain_ff, order)
    )

    near, far, d_hidden, gain_ff = ffn_back(grad_1, hidden_0, weights[0])
    d_hidden, near, far, ffn_got, attn_1, attn_far_1 = barrier(
        (d_hidden, near, far, ffn_got, attn_1, attn_far_1)
    )
    ffn_1 = over_section(ffn_1 + ffn_got, section)
    attn_1 = attn_1 + swap(attn_far_1, "gy")
    ffn_0, ffn_far_0 = over_cores(near, far)
    d_out, d_q, d_kv = attn_back(d_hidden, q_0, mixed_0, kv_0, weights[0], place)
    d_q, d_kv, attn_1, ffn_0, ffn_far_0 = barrier((d_q, d_kv, attn_1, ffn_0, ffn_far_0))
    ffn_0 = ffn_0 + swap(ffn_far_0, "gy")
    behind = to_before(d_kv[:WINDOW].astype(BF16))
    d_query, d_normed = query_back(d_q, normed_0, weights[0])
    grad_0, d_shared, gain_attn_grad = input_back(
        d_kv, behind, normed_0, d_normed, x, d_hidden, weights[0], place
    )
    attn_1 = over_section(attn_1, section)
    grad_0, ffn_1, attn_1 = barrier((grad_0, ffn_1, attn_1))
    layer_1 = lax.psum(jnp.concatenate([ffn_1, attn_1]), "dp")
    attn_0, far = over_cores(*pack_attn(d_query, d_out, d_shared, gain_attn_grad, gain_ff, order))
    attn_0 = attn_0 + swap(far, "gy")
    ffn_0 = over_section(ffn_0, section)
    attn_0 = over_section(attn_0, section)
    layer_1, ffn_0, attn_0 = barrier((layer_1, ffn_0, attn_0))
    layer_1_got = to_owner(layer_1, 1)
    layer_0 = lax.psum(jnp.concatenate([ffn_0, attn_0]), "dp")
    layer_0_got = to_owner(layer_0, 0)
    split = ffn_0.shape[0]

    in_grads = pick(section == 0, grad_0, grad_1)
    other_grads = swap(pick(section == 0, grad_1, grad_0), "section")

    def by_micro(own, other):
        first = section == 0
        return jnp.stack([jnp.where(first, own, other), jnp.where(first, other, own)])[
            None, :, None
        ]

    def finished(own_0, got_0, own_1, got_1):
        own, got = pick(section == 0, own_0, own_1), pick(section == 0, got_0, got_1)
        return jnp.concatenate([pick(section == 0, own, got), pick(section == 0, got, own)])

    def part(lo, hi):
        return finished(
            layer_0[lo:hi], layer_0_got[lo:hi], layer_1[lo:hi], layer_1_got[lo:hi]
        )

    ffn, attn = part(0, split), part(split, None)
    heads, hidden = w_query.shape[2] // 2, w_gate.shape[2] // 2
    quarter = attn[2 * heads : -GAIN_ROWS]
    quarter_beside = swap(quarter, "gy")
    shared_half = pick(
        gy == 0,
        jnp.concatenate([quarter, quarter_beside]),
        jnp.concatenate([quarter_beside, quarter]),
    )
    gain_sums = attn[-GAIN_ROWS : 2 - GAIN_ROWS].astype(F32) * scale
    ffn_other = swap(ffn, "gx")
    attn_other = swap(jnp.concatenate([attn[: 2 * heads], shared_half]), "gx")

    def both_cores(mine, other):
        low, high = pick(gx == 0, mine, other), pick(gx == 0, other, mine)
        return jnp.concatenate([low, high]).astype(F32) * scale

    gate = both_cores(ffn[:hidden], ffn_other[:hidden]).T
    up = both_cores(ffn[hidden : 2 * hidden], ffn_other[hidden : 2 * hidden]).T
    down = both_cores(ffn[2 * hidden :], ffn_other[2 * hidden :])
    query = both_cores(attn[:heads], attn_other[:heads]).T
    out = both_cores(attn[heads : 2 * heads], attn_other[heads : 2 * heads])
    shared = both_cores(shared_half, attn_other[2 * heads :]).T

    return (
        by_micro(states, other_states),
        by_micro(in_grads, other_grads),
        gain_sums[:1],
        query[None],
        shared[None, :, :HD],
        shared[None, :, HD:],
        out[None],
        gain_sums[1:],
        gate[None],
        up[None],
        down[None],
    )


def solution(mesh):
    rows = P(None, "dp", ("gx", "gy"), None)
    columns = P("section", None, "gy")
    depth = P("section", "gy", None)
    whole = P("section", None, None)
    gain = P("section", None)
    by_layer = P("section", None, "dp", ("gx", "gy"), None)
    return jax.shard_map(
        local,
        mesh=mesh,
        in_specs=(
            rows,
            P(None, "dp", None),
            rows,
            gain,
            columns,
            whole,
            whole,
            depth,
            gain,
            columns,
            columns,
            depth,
        ),
        out_specs=(
            by_layer,
            by_layer,
            gain,
            columns,
            whole,
            whole,
            depth,
            gain,
            columns,
            columns,
            depth,
        ),
        check_vma=False,
    )
```

time: 683 us -> 667 us (0.977); the launches traced: 681 us -> 658 us
  Pallas kernels: 0 us -> 144 us
  matrix products: 142 us -> 0 us
  waiting for transfers between devices: 311 us -> 343 us
  other arithmetic: 101 us -> 77.2 us
  starting transfers between devices: 62.1 us -> 38.5 us
  local copies, waits for them, and re-layouts: 47.8 us -> 38.9 us
    pallas_call x0 -> x12, Pallas kernels: none -> 144 us  [the longest x2 44.6 us: ffn_back(): pl.pallas_call(ffn_back_kernel, out_shape=(jax.ShapeDtypeStruct(packed, B...]
    dot_general x142 -> x0, matrix products: 142 us -> none  [the longest x46 53.9 us: t_mm(): lax.dot_general(a, b, (((0,), (0,)), ((), ())), preferred_element_type=F32)]
    ppermute x44 -> x38, waiting for transfers between devices: 173 us -> 235 us  [swap(): return lax.ppermute(value, axis, [(0, 1), (1, 0)])]
    psum x4 -> x2, waiting for transfers between devices: 110 us -> 86.1 us  [the longest x1 50.6 us: local(): layer_0 = lax.psum(jnp.concatenate([ffn_0, attn_0]), 'dp')]
    unnamed x383 -> x87, local copies, waits for them, and re-layouts: 37 us -> 14.2 us
    ppermute x44 -> x38, starting transfers between devices: 43.5 us -> 23.5 us  [swap(): return lax.ppermute(value, axis, [(0, 1), (1, 0)])]
    concatenate x8 -> x6, other arithmetic: 18.7 us -> 4.79 us  [the longest x1 1.21 us: local(): layer_1 = lax.psum(jnp.concatenate([ffn_1, attn_1]), 'dp')]
    convert_element_type x19 -> x1, other arithmetic: 13.5 us -> 0.01 us  [local(): angles = where_in.astype(F32)[:, None] * frequency[None, :]]
  transfers between devices with their start and end apart: 56 -> 46, of which waited for: 20 -> 21; matrix products, arithmetic and copies ran while one was open for 31% -> 11% of each run, Pallas kernels for 0% -> 17%
where the time goes in v3:
time: 667 us; the launch traced here: 658 us
  waiting for transfers between devices  343 us (51%)
  Pallas kernels  144 us (22%)
  other arithmetic  77.2 us (12%)
  local copies, waits for them, and re-layouts  38.9 us (6%)
  starting transfers between devices  38.5 us (6%)
  between operations  15.3 us (2%)
    ppermute x38, waiting for transfers between devices, swap(): return lax.ppermute(value, axis, [(0, 1), (1, 0)])  235 us
    psum x1, waiting for transfers between devices, local(): layer_0 = lax.psum(jnp.concatenate([ffn_0, attn_0]), 'dp')  50.6 us
    pallas_call x2, Pallas kernels, ffn_back(): pl.pallas_call(ffn_back_kernel, out_shape=(jax.ShapeDtypeStruct(packed, B...  44.6 us
    psum x1, waiting for transfers between devices, local(): layer_1 = lax.psum(jnp.concatenate([ffn_1, attn_1]), 'dp')  35.5 us
    pallas_call x2, Pallas kernels, attn_back(): pl.pallas_call(attn_back_kernel, out_shape=(jax.ShapeDtypeStruct(outs, BF...  28.9 us
    pallas_call x2, Pallas kernels, attn_forward(): pl.pallas_call(attn_kernel, out_shape=(jax.ShapeDtypeStruct(heads, BF16),...  28.3 us
    ppermute x38, starting transfers between devices, swap(): return lax.ppermute(value, axis, [(0, 1), (1, 0)])  23.5 us
    pallas_call x2, Pallas kernels, ffn_forward(): pl.pallas_call(ffn_kernel, out_shape=jax.ShapeDtypeStruct((rows, width),...  20.1 us
  transfers between devices with their start and end apart: 46, of which 21 were waited for; matrix products, arithmetic and copies ran while one was open for 11% of the time, Pallas kernels for 17%

profile of v3, /device:TPU:0, one launch (start us, length us, event | category | flops | bytes accessed | tf_op | source)
XLA Modules:
  0.0 657.6 jit_solution(5875563964409687414)
XLA Ops:
  22.7 29.1 %collective-permute-done.9 = bf16[640,1024]{1,0:T(8,128)(2,1)} collective-permute-done((bf16[640,1024]{1,0:T(8,128)(2,1)S(1)}, bf16[640,1024]{1,0:T(8,128)(2,1)}, u32[]{:S(2)}, u32[]{:S(2)}) %collective-permute-start.9) | collective-permute-done | bytes 1310752 | tf_op jit(solution)/shard_map/ppermute | solution.py:18
  68.5 18.1 %collective-permute-done.10 = bf16[640,1024]{1,0:T(8,128)(2,1)} collective-permute-done((bf16[640,1024]{1,0:T(8,128)(2,1)}, bf16[640,1024]{1,0:T(8,128)(2,1)}, u32[]{:S(2)}, u32[]{:S(2)}) %collective-permute-start.10) | collective-permute-done | bytes 1310752 | tf_op jit(solution)/shard_map/ppermute | solution.py:18
  90.1 13.0 %collective-permute-done.7 = bf16[256,640]{1,0:T(8,128)(2,1)S(1)} collective-permute-done((bf16[256,640]{1,0:T(8,128)(2,1)S(1)}, bf16[256,640]{1,0:T(8,128)(2,1)S(1)}, u32[]{:S(2)}, u32[]{:S(2)}) %collective-permute-start.7) | collective-permute-done | bytes 327712 | tf_op jit(solution)/shard_map/ppermute | solution.py:18
  108.6 7.2 %collective-permute-done.3 = bf16[640,256]{1,0:T(8,128)(2,1)S(1)} collective-permute-done((bf16[640,256]{1,0:T(8,128)(2,1)S(1)}, bf16[640,256]{1,0:T(8,128)(2,1)S(1)}, u32[]{:S(2)}, u32[]{:S(2)}) %collective-permute-start.3) | collective-permute-done | bytes 327712 | tf_op jit(solution)/shard_map/ppermute | solution.py:18
  121.0 22.6 %collective-permute-done.20 = bf16[640,1024]{1,0:T(8,128)(2,1)S(1)} collective-permute-done((bf16[640,1024]{1,0:T(8,128)(2,1)S(1)}, bf16[640,1024]{1,0:T(8,128)(2,1)S(1)}, u32[]{:S(2)}, u32[]{:S(2)}) %collective-permute-start.20) | collective-permute-done | bytes 1310752 | tf_op jit(solution)/shard_map/ppermute | solution.py:18
  147.1 14.1 %shard_map.203 = (bf16[4,512,256]{2,1,0:T(8,128)(2,1)}, bf16[4,512,256]{2,1,0:T(8,128)(2,1)}, bf16[1024,512]{1,0:T(8,128)(2,1)}, bf16[512,640]{1,0:T(8,128)(2,1)}, f32[512,640]{1,0:T(8,128)}) custom-call(bf16[1024,640]{1,0:T(8,128)(2,1)} %pad_maximum_fusion.15.x_ref, f32[1,640]{1,0:T(1,128)} %get-tuple-element.245.gain, bf16[2,640,256]{2,1,0:T(8,128)(2,1)} %copy-done.24, ...), custom_call_target="tpu_custom_call" | custom-call | flops 8000000000 | bytes 12000000 | tf_op jit(solution)/shard_map/pallas_call | solution.py:241
  161.3 10.0 %shard_map.204.x_ref = bf16[512,640]{1,0:T(8,128)(2,1)} custom-call(f32[512,640]{1,0:T(8,128)} %get-tuple-element.66.hidden, f32[1,640]{1,0:T(1,128)} %get-tuple-element.244.gain, bf16[2,640,1024]{2,1,0:T(8,128)(2,1)} %pad_maximum_fusion.wide_a, bf16[2,640,1024]{2,1,0:T(8,128)(2,1)} %collective-permute-done.11.wide_b, bf16[2,512,640]{2,1,0:T(8,128)(2,1)} %bitcast.21.down_a, ...), custom_call_target="tpu_custom_call" | custom-call | flops 8000000000 | bytes 12000000 | tf_op jit(solution)/shard_map/pallas_call | solution.py:295
  178.8 11.0 %collective-permute-done.15 = bf16[512,640]{1,0:T(8,128)(2,1)S(1)} collective-permute-done((bf16[512,640]{1,0:T(8,128)(2,1)}, bf16[512,640]{1,0:T(8,128)(2,1)S(1)}, u32[]{:S(2)}, u32[]{:S(2)}) %collective-permute-start.15) | collective-permute-done | bytes 655392 | tf_op jit(solution)/shard_map/ppermute | solution.py:136
  192.7 14.1 %shard_map.205 = (bf16[4,512,256]{2,1,0:T(8,128)(2,1)}, bf16[4,512,256]{2,1,0:T(8,128)(2,1)}, bf16[1024,512]{1,0:T(8,128)(2,1)}, bf16[512,640]{1,0:T(8,128)(2,1)}, f32[512,640]{1,0:T(8,128)}) custom-call(bf16[1024,640]{1,0:T(8,128)(2,1)} %pad_maximum_fusion.18.x_ref, f32[1,640]{1,0:T(1,128)} %get-tuple-element.243.gain, bf16[2,640,256]{2,1,0:T(8,128)(2,1)} %copy-done.26, ...), custom_call_target="tpu_custom_call" | custom-call | flops 8000000000 | bytes 12000000 | tf_op jit(solution)/shard_map/pallas_call | solution.py:241
  206.9 22.3 %shard_map.207 = (bf16[2,1536,640]{2,1,0:T(8,128)(2,1)}, bf16[2,1536,640]{2,1,0:T(8,128)(2,1)}, f32[512,640]{1,0:T(8,128)}, f32[1,640]{1,0:T(1,128)}) custom-call(bf16[512,640]{1,0:T(8,128)(2,1)} %bitcast_select_fusion.dy, f32[512,640]{1,0:T(8,128)} %get-tuple-element.67.hidden, f32[1,640]{1,0:T(1,128)} %get-tuple-element.242.gain, ...), custom_call_target="tpu_custom_call" | custom-call | flops 16000000000 | bytes 24000000 | tf_op jit(solution)/shard_map/pallas_call | solution.py:356
  230.8 14.6 %shard_map.208 = (bf16[4,256,640]{2,1,0:T(8,128)(2,1)}, bf16[4,512,256]{2,1,0:T(8,128)(2,1)}, f32[1024,512]{1,0:T(8,128)}) custom-call(f32[512,640]{1,0:T(8,128)} %get-tuple-element.68.d_hidden, bf16[4,512,256]{2,1,0:T(8,128)(2,1)} %get-tuple-element.69.q, bf16[4,512,256]{2,1,0:T(8,128)(2,1)} %get-tuple-element.70.mixed, ...), custom_call_target="tpu_custom_call" | custom-call | flops 10000000000 | bytes 12000000 | tf_op jit(solution)/shard_map/pallas_call | solution.py:416
  280.1 22.2 %shard_map.211 = (bf16[2,1536,640]{2,1,0:T(8,128)(2,1)}, bf16[2,1536,640]{2,1,0:T(8,128)(2,1)}, f32[512,640]{1,0:T(8,128)}, f32[1,640]{1,0:T(1,128)}) custom-call(bf16[512,640]{1,0:T(8,128)(2,1)} %get-tuple-element.80.dy, f32[512,640]{1,0:T(8,128)} %get-tuple-element.66.hidden, f32[1,640]{1,0:T(1,128)} %get-tuple-element.244.gain, ...), custom_call_target="tpu_custom_call" | custom-call | flops 16000000000 | bytes 24000000 | tf_op jit(solution)/shard_map/pallas_call | solution.py:356
  304.3 21.3 %collective-permute-done.26 = bf16[1536,640]{1,0:T(8,128)(2,1)S(1)} collective-permute-done((bf16[1536,640]{1,0:T(8,128)(2,1)}, bf16[1536,640]{1,0:T(8,128)(2,1)S(1)}, u32[]{:S(2)}, u32[]{:S(2)}) %collective-permute-start.26) | collective-permute-done | bytes 1966112 | tf_op jit(solution)/shard_map/ppermute | solution.py:18
  325.9 14.3 %shard_map.212 = (bf16[4,256,640]{2,1,0:T(8,128)(2,1)}, bf16[4,512,256]{2,1,0:T(8,128)(2,1)}, f32[1024,512]{1,0:T(8,128)}) custom-call(f32[512,640]{1,0:T(8,128)} %get-tuple-element.90.d_hidden, bf16[4,512,256]{2,1,0:T(8,128)(2,1)} %get-tuple-element.91.q, bf16[4,512,256]{2,1,0:T(8,128)(2,1)} %get-tuple-element.92.mixed, ...), custom_call_target="tpu_custom_call" | custom-call | flops 10000000000 | bytes 12000000 | tf_op jit(solution)/shard_map/pallas_call | solution.py:416
  340.2 6.9 %collective-permute-done.28 = bf16[672,640]{1,0:T(8,128)(2,1)S(1)} collective-permute-done((bf16[672,640]{1,0:T(8,128)(2,1)S(1)}, bf16[672,640]{1,0:T(8,128)(2,1)S(1)}, u32[]{:S(2)}, u32[]{:S(2)}) %collective-permute-start.28) | collective-permute-done | bytes 860192 | tf_op jit(solution)/shard_map/ppermute | solution.py:18
  383.2 22.9 %collective-permute-done.31 = bf16[768,640]{1,0:T(8,128)(2,1)S(1)} collective-permute-done((bf16[768,640]{1,0:T(8,128)(2,1)S(1)}, bf16[768,640]{1,0:T(8,128)(2,1)S(1)}, u32[]{:S(2)}, u32[]{:S(2)}) %collective-permute-start.31) | collective-permute-done | bytes 983072 | tf_op jit(solution)/shard_map/ppermute | solution.py:18
  408.2 9.7 %collective-permute-done.32 = bf16[336,640]{1,0:T(8,128)(2,1)S(1)} collective-permute-done((bf16[336,640]{1,0:T(8,128)(2,1)S(1)}, bf16[336,640]{1,0:T(8,128)(2,1)S(1)}, u32[]{:S(2)}, u32[]{:S(2)}) %collective-permute-start.32) | collective-permute-done | bytes 430112 | tf_op jit(solution)/shard_map/ppermute | solution.py:18
  418.0 10.9 %collective-permute-done.34 = bf16[1536,640]{1,0:T(8,128)(2,1)S(1)} collective-permute-done((bf16[1536,640]{1,0:T(8,128)(2,1)S(1)}, bf16[1536,640]{1,0:T(8,128)(2,1)S(1)}, u32[]{:S(2)}, u32[]{:S(2)}) %collective-permute-start.34) | collective-permute-done | bytes 1966112 | tf_op jit(solution)/shard_map/ppermute | solution.py:18
  431.6 14.3 %collective-permute-done.37 = bf16[672,640]{1,0:T(8,128)(2,1)} collective-permute-done((bf16[672,640]{1,0:T(8,128)(2,1)}, bf16[672,640]{1,0:T(8,128)(2,1)}, u32[]{:S(2)}, u32[]{:S(2)}) %collective-permute-start.37) | collective-permute-done | bytes 860192 | tf_op jit(solution)/shard_map/ppermute | solution.py:18
  453.9 6.2 collective-permute-done.38
  460.2 35.5 %all-reduce.5.cloned.1.call-done = bf16[1104,640]{1,0:T(8,128)(2,1)} async-done(((bf16[1104,640]{1,0:T(8,128)(2,1)}), bf16[1104,640]{1,0:T(8,128)(2,1)}) %all-reduce.5.cloned.1.call-update) | async-done | bytes 1413136 | tf_op jit(solution)/shard_map/psum | solution.py:609
  496.9 10.1 %shard_map.206 = bf16[512,640]{1,0:T(8,128)(2,1)} custom-call(f32[512,640]{1,0:T(8,128)} %get-tuple-element.67.hidden, f32[1,640]{1,0:T(1,128)} %get-tuple-element.242.gain, bf16[2,640,1024]{2,1,0:T(8,128)(2,1)} %copy-done.8, bf16[2,640,1024]{2,1,0:T(8,128)(2,1)} %collective-permute-done.21.wide_b, bf16[2,512,640]{2,1,0:T(8,128)(2,1)} %bitcast.164, ...), custom_call_target="tpu_custom_call" | custom-call | flops 8000000000 | bytes 12000000 | tf_op jit(solution)/shard_map/pallas_call | solution.py:295
  511.6 50.6 %all-reduce.7.cloned.1.call-done = bf16[1104,640]{1,0:T(8,128)(2,1)} async-done(((bf16[1104,640]{1,0:T(8,128)(2,1)}), bf16[1104,640]{1,0:T(8,128)(2,1)}) %all-reduce.7.cloned.1.call-update) | async-done | bytes 1413136 | tf_op jit(solution)/shard_map/psum | solution.py:616
  567.7 43.3 %collective-permute-done.23 = bf16[512,640]{1,0:T(8,128)(2,1)} collective-permute-done((bf16[512,640]{1,0:T(8,128)(2,1)S(1)}, bf16[512,640]{1,0:T(8,128)(2,1)}, u32[]{:S(2)}, u32[]{:S(2)}) %collective-permute-start.23) | collective-permute-done | bytes 655392 | tf_op jit(solution)/shard_map/ppermute | solution.py:18
  (282 shorter events, 197.9 us)
Async XLA Ops:
  7.2 488.5 %all-reduce.5.cloned.1.call-start = ((), (), s32[]{:S(2)}) async-start(), calls=%async_computation | async-start | bytes 2826240 | tf_op jit(solution)/shard_map/psum | solution.py:609
  8.1 53.0 %collective-permute-start.1 = (f32[2,640]{1,0:T(2,128)S(1)}, f32[2,640]{1,0:T(2,128)S(1)}, u32[]{:S(2)}, u32[]{:S(2)}) collective-permute-start(f32[2,640]{1,0:T(2,128)S(1)} %pad_maximum_fusion.28), channel_id=1, source_target_pairs={{0,16},{16,0},{1,17},{17,1},{2,18},{18,2},{3,19},{19,3},{4,20},{20... | collective-permute-start | bytes 15368 | tf_op jit(solution)/shard_map/ppermute | solution.py:18
  12.8 50.7 %collective-permute-start.6 = (bf16[256,640]{1,0:T(8,128)(2,1)}, bf16[256,640]{1,0:T(8,128)(2,1)}, u32[]{:S(2)}, u32[]{:S(2)}) collective-permute-start(bf16[256,640]{1,0:T(8,128)(2,1)} %dynamic-slice_bitcast_fusion.4), channel_id=1, source_target_pairs={{0,16},{16,0},{1,17},{17,1},{2,18},{18,2},{3,19},{19,3},{4,20},{20... | collective-permute-start | bytes 983048 | tf_op jit(solution)/shard_map/ppermute | solution.py:18
  12.9 53.7 %collective-permute-start.12 = (bf16[512,640]{1,0:T(8,128)(2,1)S(1)}, bf16[512,640]{1,0:T(8,128)(2,1)}, u32[]{:S(2)}, u32[]{:S(2)}) collective-permute-start(bf16[512,640]{1,0:T(8,128)(2,1)S(1)} %dynamic-slice_bitcast_fusion), channel_id=1, source_target_pairs={{0,4},{4,0},{1,5},{5,1},{2,6},{6,2},{3,7},{7,3},{8,12},{12,8},{9,1... | collective-permute-start | bytes 1966088 | tf_op jit(solution)/shard_map/ppermute | solution.py:18
  16.4 35.4 %collective-permute-start.9 = (bf16[640,1024]{1,0:T(8,128)(2,1)S(1)}, bf16[640,1024]{1,0:T(8,128)(2,1)}, u32[]{:S(2)}, u32[]{:S(2)}) collective-permute-start(bf16[640,1024]{1,0:T(8,128)(2,1)S(1)} %pad_maximum_fusion.16), channel_id=1, source_target_pairs={{0,16},{16,0},{1,17},{17,1},{2,18},{18,2},{3,19},{19,3},{4,20},{20... | collective-permute-start | bytes 3932168 | tf_op jit(solution)/shard_map/ppermute | solution.py:18
  21.8 43.7 %collective-permute-start.2 = (bf16[640,512]{1,0:T(8,128)(2,1)}, bf16[640,512]{1,0:T(8,128)(2,1)}, u32[]{:S(2)}, u32[]{:S(2)}) collective-permute-start(bf16[640,512]{1,0:T(8,128)(2,1)} %pad_maximum_fusion.20), channel_id=1, source_target_pairs={{0,16},{16,0},{1,17},{17,1},{2,18},{18,2},{3,19},{19,3},{4,20},{20... | collective-permute-start | bytes 1966088 | tf_op jit(solution)/shard_map/ppermute | solution.py:18
  54.9 31.7 %collective-permute-start.10 = (bf16[640,1024]{1,0:T(8,128)(2,1)}, bf16[640,1024]{1,0:T(8,128)(2,1)}, u32[]{:S(2)}, u32[]{:S(2)}) collective-permute-start(bf16[640,1024]{1,0:T(8,128)(2,1)} %get-tuple-element.173), channel_id=1, source_target_pairs={{0,4},{4,0},{1,5},{5,1},{2,6},{6,2},{3,7},{7,3},{8,12},{12,8},{9,1... | collective-permute-start | bytes 3932168 | tf_op jit(solution)/shard_map/ppermute | solution.py:18
  61.1 46.2 %collective-permute-start = (bf16[512,640]{1,0:T(8,128)(2,1)S(1)}, bf16[512,640]{1,0:T(8,128)(2,1)S(1)}, u32[]{:S(2)}, u32[]{:S(2)}) collective-permute-start(bf16[512,640]{1,0:T(8,128)(2,1)S(1)} %dynamic-slice_bitcast_fusion.3.x_ref), channel_id=1, source_target_pairs={{0,4},{4,8},{8,12},{1,5},{5,9},{9,13},{2,6},{6,10},{10,14},{3,7},{... | collective-permute-start | bytes 1966088 | tf_op jit(solution)/shard_map/ppermute | solution.py:136
  65.5 37.6 %collective-permute-start.7 = (bf16[256,640]{1,0:T(8,128)(2,1)S(1)}, bf16[256,640]{1,0:T(8,128)(2,1)S(1)}, u32[]{:S(2)}, u32[]{:S(2)}) collective-permute-start(bf16[256,640]{1,0:T(8,128)(2,1)S(1)} %get-tuple-element.219), channel_id=1, source_target_pairs={{0,4},{4,0},{1,5},{5,1},{2,6},{6,2},{3,7},{7,3},{8,12},{12,8},{9,1... | collective-permute-start | bytes 983048 | tf_op jit(solution)/shard_map/ppermute | solution.py:18
  66.5 36.7 %collective-permute-start.5 = (bf16[640,256]{1,0:T(8,128)(2,1)S(1)}, bf16[640,256]{1,0:T(8,128)(2,1)S(1)}, u32[]{:S(2)}, u32[]{:S(2)}) collective-permute-start(bf16[640,256]{1,0:T(8,128)(2,1)S(1)} %slice.314), channel_id=1, source_target_pairs={{0,8},{8,0},{1,9},{9,1},{2,10},{10,2},{3,11},{11,3},{4,12},{12,4},... | collective-permute-start | bytes 983048 | tf_op jit(solution)/shard_map/ppermute | solution.py:18
  67.8 48.1 %collective-permute-start.13 = (bf16[1024,640]{1,0:T(8,128)(2,1)S(1)}, bf16[1024,640]{1,0:T(8,128)(2,1)S(1)}, u32[]{:S(2)}, u32[]{:S(2)}) collective-permute-start(bf16[1024,640]{1,0:T(8,128)(2,1)S(1)} %pad_maximum_fusion.17), channel_id=1, source_target_pairs={{0,16},{16,0},{1,17},{17,1},{2,18},{18,2},{3,19},{19,3},{4,20},{20... | collective-permute-start | bytes 3932168 | tf_op jit(solution)/shard_map/ppermute | solution.py:18
  90.1 71.2 %collective-permute-start.11 = (bf16[2,640,1024]{2,1,0:T(8,128)(2,1)}, bf16[2,640,1024]{2,1,0:T(8,128)(2,1)}, u32[]{:S(2)}, u32[]{:S(2)}) collective-permute-start(bf16[2,640,1024]{2,1,0:T(8,128)(2,1)} %pad_maximum_fusion.wide_a), channel_id=1, source_target_pairs={{0,8},{8,0},{1,9},{9,1},{2,10},{10,2},{3,11},{11,3},{4,12},{12,4},... | collective-permute-start | bytes 7864328 | tf_op jit(solution)/shard_map/ppermute | solution.py:18
  103.2 42.4 %collective-permute-start.8 = (bf16[2,256,640]{2,1,0:T(8,128)(2,1)S(1)}, bf16[2,256,640]{2,1,0:T(8,128)(2,1)S(1)}, u32[]{:S(2)}, u32[]{:S(2)}) collective-permute-start(bf16[2,256,640]{2,1,0:T(8,128)(2,1)S(1)} %pad_maximum_fusion.22.wo_a), channel_id=1, source_target_pairs={{0,8},{8,0},{1,9},{9,1},{2,10},{10,2},{3,11},{11,3},{4,12},{12,4},... | collective-permute-start | bytes 1966088 | tf_op jit(solution)/shard_map/ppermute | solution.py:18
  107.3 36.3 %collective-permute-start.20 = (bf16[640,1024]{1,0:T(8,128)(2,1)S(1)}, bf16[640,1024]{1,0:T(8,128)(2,1)S(1)}, u32[]{:S(2)}, u32[]{:S(2)}) collective-permute-start(bf16[640,1024]{1,0:T(8,128)(2,1)S(1)} %get-tuple-element.172), channel_id=1, source_target_pairs={{0,4},{4,0},{1,5},{5,1},{2,6},{6,2},{3,7},{7,3},{8,12},{12,8},{9,1... | collective-permute-start | bytes 3932168 | tf_op jit(solution)/shard_map/ppermute | solution.py:18
  119.4 41.9 %collective-permute-start.14 = (bf16[2,512,640]{2,1,0:T(8,128)(2,1)}, bf16[2,512,640]{2,1,0:T(8,128)(2,1)}, u32[]{:S(2)}, u32[]{:S(2)}) collective-permute-start(bf16[2,512,640]{2,1,0:T(8,128)(2,1)} %bitcast.21.down_a), channel_id=1, source_target_pairs={{0,8},{8,0},{1,9},{9,1},{2,10},{10,2},{3,11},{11,3},{4,12},{12,4},... | collective-permute-start | bytes 3932168 | tf_op jit(solution)/shard_map/ppermute | solution.py:18
  143.6 31.5 %collective-permute-start.18 = (bf16[256,640]{1,0:T(8,128)(2,1)}, bf16[256,640]{1,0:T(8,128)(2,1)S(1)}, u32[]{:S(2)}, u32[]{:S(2)}) collective-permute-start(bf16[256,640]{1,0:T(8,128)(2,1)} %get-tuple-element.218), channel_id=1, source_target_pairs={{0,4},{4,0},{1,5},{5,1},{2,6},{6,2},{3,7},{7,3},{8,12},{12,8},{9,1... | collective-permute-start | bytes 983048 | tf_op jit(solution)/shard_map/ppermute | solution.py:18
  147.1 59.7 %collective-permute-start.21 = (bf16[2,640,1024]{2,1,0:T(8,128)(2,1)S(1)}, bf16[2,640,1024]{2,1,0:T(8,128)(2,1)}, u32[]{:S(2)}, u32[]{:S(2)}) collective-permute-start(bf16[2,640,1024]{2,1,0:T(8,128)(2,1)S(1)} %pad_maximum_fusion.1.wide_a), channel_id=1, source_target_pairs={{0,8},{8,0},{1,9},{9,1},{2,10},{10,2},{3,11},{11,3},{4,12},{12,4},... | collective-permute-start | bytes 7864328 | tf_op jit(solution)/shard_map/ppermute | solution.py:18
  280.1 45.4 %collective-permute-start.26 = (bf16[1536,640]{1,0:T(8,128)(2,1)}, bf16[1536,640]{1,0:T(8,128)(2,1)S(1)}, u32[]{:S(2)}, u32[]{:S(2)}) collective-permute-start(bf16[1536,640]{1,0:T(8,128)(2,1)} %get-tuple-element.84), channel_id=1, source_target_pairs={{0,4},{4,0},{1,5},{5,1},{2,6},{6,2},{3,7},{7,3},{8,12},{12,8},{9,1... | collective-permute-start | bytes 5898248 | tf_op jit(solution)/shard_map/ppermute | solution.py:18
  383.1 45.8 %collective-permute-start.34 = (bf16[1536,640]{1,0:T(8,128)(2,1)S(1)}, bf16[1536,640]{1,0:T(8,128)(2,1)S(1)}, u32[]{:S(2)}, u32[]{:S(2)}) collective-permute-start(bf16[1536,640]{1,0:T(8,128)(2,1)S(1)} %copy-done.12), channel_id=1, source_target_pairs={{0,4},{4,0},{1,5},{5,1},{2,6},{6,2},{3,7},{7,3},{8,12},{12,8},{9,1... | collective-permute-start | bytes 5898248 | tf_op jit(solution)/shard_map/ppermute | solution.py:18
  408.2 37.7 %collective-permute-start.37 = (bf16[672,640]{1,0:T(8,128)(2,1)}, bf16[672,640]{1,0:T(8,128)(2,1)}, u32[]{:S(2)}, u32[]{:S(2)}) collective-permute-start(bf16[672,640]{1,0:T(8,128)(2,1)} %slice_bitcast_fusion.4), channel_id=1, source_target_pairs={{0,4},{4,0},{1,5},{5,1},{2,6},{6,2},{3,7},{7,3},{8,12},{12,8},{9,1... | collective-permute-start | bytes 2580488 | tf_op jit(solution)/shard_map/ppermute | solution.py:18
  431.5 130.8 %all-reduce.7.cloned.1.call-start = ((), (), s32[]{:S(2)}) async-start(), calls=%async_computation.1 | async-start | bytes 2826240 | tf_op jit(solution)/shard_map/psum | solution.py:616
  507.1 105.4 %collective-permute-start.40 = (bf16[1104,640]{1,0:T(8,128)(2,1)}, bf16[1104,640]{1,0:T(8,128)(2,1)}, u32[]{:S(2)}, u32[]{:S(2)}) collective-permute-start(bf16[1104,640]{1,0:T(8,128)(2,1)} %all-reduce.5.cloned.1.call-done), channel_id=1, source_target_pairs={{0,16},{1,17},{2,18},{3,19},{4,20},{5,21},{6,22},{7,23},{8,24},{9,... | collective-permute-start | bytes 4239368 | tf_op jit(solution)/shard_map/ppermute | solution.py:523
  562.3 50.1 %collective-permute-start.39 = (bf16[1104,640]{1,0:T(8,128)(2,1)}, bf16[1104,640]{1,0:T(8,128)(2,1)}, u32[]{:S(2)}, u32[]{:S(2)}) collective-permute-start(bf16[1104,640]{1,0:T(8,128)(2,1)} %all-reduce.7.cloned.1.call-done), channel_id=1, source_target_pairs={{16,0},{17,1},{18,2},{19,3},{20,4},{21,5},{22,6},{23,7},{24,8},{25... | collective-permute-start | bytes 4239368 | tf_op jit(solution)/shard_map/ppermute | solution.py:523
  565.0 46.0 %collective-permute-start.23 = (bf16[512,640]{1,0:T(8,128)(2,1)S(1)}, bf16[512,640]{1,0:T(8,128)(2,1)}, u32[]{:S(2)}, u32[]{:S(2)}) collective-permute-start(bf16[512,640]{1,0:T(8,128)(2,1)S(1)} %broadcast_select_fusion.14), channel_id=1, source_target_pairs={{0,16},{16,0},{1,17},{17,1},{2,18},{18,2},{3,19},{19,3},{4,20},{20... | collective-permute-start | bytes 1966088 | tf_op jit(solution)/shard_map/ppermute | solution.py:18
  (63 other events, 1050.1 us)
Sparse Core Ops, SparseCore 0:
  431.6 64.0 all-reduce.4
  498.7 63.5 all-reduce.6

commit v4 on v3

--- a/solution.py
+++ b/solution.py
@@ -1,3 +1,4 @@
+import functools
 import math
 
 import jax
@@ -78,8 +79,9 @@
     return jnp.where(flag, a, b)
 
 
-def gather_weights(w_query, w_key, w_value, w_out, w_gate, w_up, w_down, section):
+def gather_weights(x, w_query, w_key, w_value, w_out, w_gate, w_up, w_down, section):
     gx = lax.axis_index("gx")
+    barrier = lax.optimization_barrier
 
     def half(w, axis):
         size = w.shape[axis] // 2
@@ -88,48 +90,87 @@
     def two_layers(mine, received):
         return [pick(section == layer, mine, received) for layer in range(2)]
 
+    def over_gx(own, beside):
+        both = jnp.stack([own, beside])
+        return both, swap(both, "gx")
+
     heads = w_query.shape[1] // 2
     first_own = jnp.concatenate([half(w_query, 1), half(w_key, 1), half(w_value, 1)], axis=1)
-    out_own = half(w_out, 0)
-    wide_own = jnp.concatenate([half(w_gate, 1), half(w_up, 1)], axis=1)
-    down_own = half(w_down, 0)
+    out_own, gate_own, up_own, down_own = half(w_out, 0), half(w_gate, 1), half(w_up, 1), half(w_down, 0)
     first_got = swap(first_own, "section")
+    x_before = from_before(x)
+    out_got = swap(out_own, "section")
     down_beside = swap(down_own, "gy")
-    out_got = swap(out_own, "section")
-    wide_got = swap(wide_own, "section")
-    down_own = jnp.concatenate([down_own, down_beside])
-    down_got = swap(down_own, "section")
-
+    first_got, gate_own = barrier((first_got, gate_own))
+
+    queries = two_layers(first_own[:, :heads], first_got[:, :heads])
+    query_beside = swap(queries[0], "gy")
+    gate_got = swap(gate_own, "section")
     shared_got = first_got[:, heads:]
     shared_other = swap(shared_got, "gx")
+    out_got, up_own = barrier((out_got, up_own))
+
+    outs = two_layers(out_own, out_got)
+    out_beside = swap(outs[0], "gy")
+    up_got = swap(up_own, "section")
     low, high = pick(gx == 0, shared_got, shared_other), pick(gx == 0, shared_other, shared_got)
     part = low.shape[1] // 2
     key_got = jnp.concatenate([low[:, :part], high[:, :part]], axis=1)
     value_got = jnp.concatenate([low[:, part:], high[:, part:]], axis=1)
     keys, values = two_layers(w_key, key_got), two_layers(w_value, value_got)
-
-    queries = two_layers(first_own[:, :heads], first_got[:, :heads])
-    outs = two_layers(out_own, out_got)
-    wides = two_layers(wide_own, wide_got)
-    downs = two_layers(down_own, down_got)
-    layers = []
-    for layer in range(2):
-        def pairs(own):
-            both = jnp.stack([own, swap(own, "gy")])
-            return both, swap(both, "gx")
-
-        down = downs[layer].reshape(2, -1, w_down.shape[1])
-        layers.append(
-            {
-                "query": pairs(queries[layer]),
-                "out": pairs(outs[layer]),
-                "wide": pairs(wides[layer]),
-                "down": (down, swap(down, "gx")),
-                "key": keys[layer],
-                "value": values[layer],
+    down_pair = jnp.stack([down_own, down_beside])
+    gate_got, down_pair, keys, values = barrier((gate_got, down_pair, keys, values))
+
+    gates = two_layers(gate_own, gate_got)
+    gate_beside = swap(gates[0], "gy")
+    down_got = swap(down_pair, "section")
+    query_beside, out_beside, x_before, up_got = barrier((query_beside, out_beside, x_before, up_got))
+    ups = two_layers(up_own, up_got)
+    up_beside = swap(ups[0], "gy")
+    later = queries[1], outs[1]
+    later_besides = [swap(value, "gy") for value in later]
+    first = {
+        "query": over_gx(queries[0], query_beside),
+        "out": over_gx(outs[0], out_beside),
+        "key": keys[0],
+        "value": values[0],
+    }
+
+    def finish(kernel_out):
+        kernel_out, gate_here, up_here, arrived, gate_1 = barrier(
+            (kernel_out, gate_beside, up_beside, later_besides, gates[1])
+        )
+        gate_1_beside = swap(gate_1, "gy")
+        downs = two_layers(down_pair, down_got)
+        first.update(
+            gate=over_gx(gates[0], gate_here),
+            up=over_gx(ups[0], up_here),
+            down=(downs[0], swap(downs[0], "gx")),
+        )
+
+        def second(kernel_out):
+            kernel_out, gate_1_here, up_1, down_1 = barrier(
+                (kernel_out, gate_1_beside, ups[1], downs[1])
+            )
+            rows_before = from_before(kernel_out)
+            gate_pairs = over_gx(gate_1, gate_1_here)
+            down_pairs = down_1, swap(down_1, "gx")
+            query_pairs, out_pairs = over_gx(later[0], arrived[0]), over_gx(later[1], arrived[1])
+            rows_before, up_1 = barrier((rows_before, up_1))
+            layer = {
+                "query": query_pairs,
+                "out": out_pairs,
+                "gate": gate_pairs,
+                "up": (up_1, swap(up_1, "gy")),
+                "down": down_pairs,
+                "key": keys[1],
+                "value": values[1],
             }
-        )
-    return layers
+            return kernel_out, rows_before, layer
+
+        return kernel_out, second
+
+    return first, x_before, finish
 
 
 def from_before(value):
@@ -168,10 +209,7 @@
     )
 
 
-def cost(flops, bytes_accessed, transcendentals=0):
-    return pl.CostEstimate(
-        flops=flops, bytes_accessed=bytes_accessed, transcendentals=transcendentals
-    )
+SMALL = pl.CostEstimate(flops=1000, bytes_accessed=1000, transcendentals=0)
 
 
 def take(step, first, last, held):
@@ -260,14 +298,16 @@
             pltpu.VMEM((width, HD), BF16),
             pltpu.VMEM((HD, width), BF16),
         ],
-        cost_estimate=cost(8 * 10**9, 12 * 10**6, 2 * 10**6),
+        cost_estimate=SMALL,
         **PARAMS,
     )(*ops)
 
 
-def ffn_kernel(hidden, gain, wide_a, wide_b, down_a, down_b, out, normed, total, wide, down):
+def ffn_kernel(
+    hidden, gain, gate_a, gate_b, up_a, up_b, down_a, down_b,
+    out, normed, total, w_gate, w_up, down,
+):
     j = pl.program_id(0)
-    units = down.shape[0]
 
     @pl.when(j == 0)
     def _():
@@ -275,10 +315,11 @@
         normed[...] = (value * inverse_rms(value) * gain[...]).astype(BF16)
         total[...] = value
 
-    take(j, wide_a, wide_b, wide)
+    take(j, gate_a, gate_b, w_gate)
+    take(j, up_a, up_b, w_up)
     take(j, down_a, down_b, down)
-    gate = mm(normed[...], wide[:, :units])
-    up = mm(normed[...], wide[:, units:])
+    gate = mm(normed[...], w_gate[...])
+    up = mm(normed[...], w_up[...])
     act = (gelu_parts(gate)[0] * up).astype(BF16)
     total[...] += mm(act, down[...])
 
@@ -289,9 +330,9 @@
 
 def ffn_forward(hidden, w):
     rows, width = hidden.shape
-    ops = (hidden, w["gain_ff"], *w["wide"], *w["down"])
+    ops = (hidden, w["gain_ff"], *w["gate"], *w["up"], *w["down"])
     units = w["down"][0].shape[1]
-    pairs = {2: first_of, 3: last_of, 4: first_of, 5: last_of}
+    pairs = {i: (first_of, last_of)[i % 2] for i in range(2, 8)}
     return pl.pallas_call(
         ffn_kernel,
         out_shape=jax.ShapeDtypeStruct((rows, width), BF16),
@@ -300,77 +341,67 @@
         scratch_shapes=[
             pltpu.VMEM((rows, width), BF16),
             pltpu.VMEM((rows, width), F32),
-            pltpu.VMEM((width, 2 * units), BF16),
+            pltpu.VMEM((width, units), BF16),
+            pltpu.VMEM((width, units), BF16),
             pltpu.VMEM((units, width), BF16),
         ],
-        cost_estimate=cost(8 * 10**9, 12 * 10**6, 10**6),
+        cost_estimate=SMALL,
         **PARAMS,
     )(*ops)
 
 
-def ffn_back_kernel(
-    dy, hidden, gain, wide_a, wide_b, down_a, down_b,
-    near, far, d_hidden, d_gain, normed, total, wide, down,
-):
+def ffn_back_kernel(last, dy, hidden, gain, before, gate, up, down, out, *rest):
+    total, normed = rest[-2:]
     j = pl.program_id(0)
-    units = down.shape[0]
+    units = down.shape[1]
 
     @pl.when(j == 0)
     def _():
         value = hidden[...]
         normed[...] = (value * inverse_rms(value) * gain[...]).astype(BF16)
-        total[...] = jnp.zeros_like(total)
-
-    take(j, wide_a, wide_b, wide)
-    take(j, down_a, down_b, down)
-    gate = mm(normed[...], wide[:, :units])
-    up = mm(normed[...], wide[:, units:])
-    d_act = mm_t(dy[...], down[...])
-    value, slope = gelu_parts(gate)
-    act = (value * up).astype(BF16)
-    d_gate = (d_act * up * slope).astype(BF16)
+        total[...] = before[...] if last else jnp.zeros_like(total)
+
+    gate_value = mm(normed[...], gate[0])
+    up_value = mm(normed[...], up[0])
+    d_act = mm_t(dy[...], down[0])
+    value, slope = gelu_parts(gate_value)
+    act = (value * up_value).astype(BF16)
+    d_gate = (d_act * up_value * slope).astype(BF16)
     d_up = (d_act * value).astype(BF16)
-    total[...] += mm_t(d_gate, wide[:, :units]) + mm_t(d_up, wide[:, units:])
-    parts = [t_mm(d_gate, normed[...]), t_mm(d_up, normed[...]), t_mm(act, dy[...])]
-
-    def put(out):
-        for i, part in enumerate(parts):
-            out[0, pl.ds(i * units, units), :] = part.astype(BF16)
-
-    pl.when(j < 2)(lambda: put(near))
-    pl.when(j >= 2)(lambda: put(far))
-
-    @pl.when(j == STEPS - 1)
-    def _():
-        to_hidden, to_gain = norm_back(hidden[...], gain[...], total[...])
-        d_hidden[...] = dy[...].astype(F32) + to_hidden
-        d_gain[...] = to_gain[None]
-
-
-def ffn_back(dy, hidden, w):
+    total[...] += mm_t(d_gate, gate[0]) + mm_t(d_up, up[0])
+    for i, part in enumerate((t_mm(d_gate, normed[...]), t_mm(d_up, normed[...]), t_mm(act, dy[...]))):
+        out[0, pl.ds(i * units, units), :] = part.astype(BF16)
+
+    @pl.when(j == pl.num_programs(0) - 1)
+    def _():
+        if last:
+            d_hidden, d_gain = rest[:2]
+            to_hidden, to_gain = norm_back(hidden[...], gain[...], total[...])
+            d_hidden[...] = dy[...].astype(F32) + to_hidden
+            d_gain[...] = to_gain[None]
+        else:
+            rest[0][...] = total[...]
+
+
+def ffn_back(dy, hidden, w, pair, before=None):
     rows, width = hidden.shape
-    ops = (dy, hidden, w["gain_ff"], *w["wide"], *w["down"])
-    units = w["down"][0].shape[1]
-    pairs = {3: first_of, 4: last_of, 5: first_of, 6: last_of}
-    packed = (2, 3 * units, width)
+    last = before is not None
+    ops = (dy, hidden, w["gain_ff"], before if last else jnp.zeros((8, 128), F32))
+    ops += (w["gate"][pair], w["up"][pair], w["down"][pair])
+    packed = (2, 3 * w["down"][pair].shape[1], width)
+    shapes = [(rows, width), (1, width)] if last else [(rows, width)]
     return pl.pallas_call(
-        ffn_back_kernel,
-        out_shape=(
-            jax.ShapeDtypeStruct(packed, BF16),
-            jax.ShapeDtypeStruct(packed, BF16),
-            jax.ShapeDtypeStruct((rows, width), F32),
-            jax.ShapeDtypeStruct((1, width), F32),
+        functools.partial(ffn_back_kernel, last),
+        grid=(2,),
+        out_shape=[jax.ShapeDtypeStruct(packed, BF16)]
+        + [jax.ShapeDtypeStruct(shape, F32) for shape in shapes],
+        in_specs=[all_of(op.shape) for op in ops[:4]] + [step_of(op.shape) for op in ops[4:]],
+        out_specs=[step_of(packed)] + [all_of(shape) for shape in shapes],
+        scratch_shapes=[pltpu.VMEM((rows, width), F32), pltpu.VMEM((rows, width), BF16)],
+        compiler_params=pltpu.CompilerParams(
+            dimension_semantics=("arbitrary",), vmem_limit_bytes=56 * 1024 * 1024
         ),
-        in_specs=[pairs.get(i, all_of)(op.shape) for i, op in enumerate(ops)],
-        out_specs=(first_of(packed), last_of(packed), all_of((rows, width)), all_of((1, width))),
-        scratch_shapes=[
-            pltpu.VMEM((rows, width), BF16),
-            pltpu.VMEM((rows, width), F32),
-            pltpu.VMEM((width, 2 * units), BF16),
-            pltpu.VMEM((units, width), BF16),
-        ],
-        cost_estimate=cost(16 * 10**9, 24 * 10**6, 10**6),
-        **PARAMS,
+        cost_estimate=SMALL,
     )(*ops)
 
 
@@ -427,7 +458,7 @@
             pltpu.VMEM((HD, width), BF16),
             pltpu.VMEM((rows, width), BF16),
         ],
-        cost_estimate=cost(10 * 10**9, 12 * 10**6, 2 * 10**6),
+        cost_estimate=SMALL,
         **PARAMS,
     )(*ops)
 
@@ -458,7 +489,7 @@
         in_specs=[pairs.get(i, all_of)(op.shape) for i, op in enumerate(ops)],
         out_specs=(step_of(outs), all_of((rows, width))),
         scratch_shapes=[pltpu.VMEM((width, HD), BF16)],
-        cost_estimate=cost(2 * 10**9, 6 * 10**6),
+        cost_estimate=SMALL,
         **PARAMS,
     )(*ops)
 
@@ -493,7 +524,7 @@
             jax.ShapeDtypeStruct((1, width), F32),
         ),
         compiler_params=pltpu.CompilerParams(vmem_limit_bytes=56 * 1024 * 1024),
-        cost_estimate=cost(10**9, 8 * 10**6),
+        cost_estimate=SMALL,
     )(*ops)
 
 
@@ -508,15 +539,82 @@
     return jnp.stack(pieces[:2]), jnp.stack(pieces[2:])
 
 
-def over_cores(near, far):
-    kept = near + swap(far, "gx")
-    return kept[0], kept[1]
-
-
-def over_section(total, section):
-    half = total.shape[0] // 2
-    low, high = total[:half], total[half:]
-    return pick(section == 0, low, high) + swap(pick(section == 0, high, low), "section")
+def finish_part(scale, source, at, size):
+    return source[at : at + size, :].astype(F32) * scale
+
+
+def for_core(core, put, mine, other):
+    @pl.when(core[0] == 0)
+    def _():
+        put(0, *mine)
+        put(1, *other)
+
+    @pl.when(core[0] != 0)
+    def _():
+        put(0, *other)
+        put(1, *mine)
+
+
+def finish_ffn_kernel(scale, core, *refs):
+    gate, up, down = refs[4:]
+    units = gate.shape[1] // 2
+    part = functools.partial(finish_part, scale)
+
+    def put(core, low, high):
+        at = core * units
+        gate[:, at : at + units // 2] = part(low, 0, units // 2).T
+        gate[:, at + units // 2 : at + units] = part(high, 0, units // 2).T
+        up[:, at : at + units] = part(low, units // 2, units).T
+        down[at : at + units, :] = part(high, units // 2, units)
+
+    for_core(core, put, refs[:2], refs[2:4])
+
+
+def finish_attn_kernel(scale, core, *refs):
+    shared = refs[4]
+    query, key, value, out = refs[5:]
+    heads = query.shape[1] // 2
+    part = functools.partial(finish_part, scale)
+
+    def put(core, low, high):
+        some, at = low.shape[0] - heads, core * heads
+        query[:, at : at + heads] = part(low, 0, heads).T
+        out[at : at + some, :] = part(low, heads, some)
+        out[at + some : at + heads, :] = part(high, 0, heads - some)
+
+    for_core(core, put, refs[:2], refs[2:4])
+    key[...] = part(shared, 0, HD).T
+    value[...] = part(shared, HD, HD).T
+
+
+def finish(kernel, shapes, core, scale, *ops):
+    vmem = pl.BlockSpec(memory_space=pltpu.VMEM)
+    return pl.pallas_call(
+        functools.partial(kernel, scale),
+        out_shape=[jax.ShapeDtypeStruct(shape, F32) for shape in shapes],
+        in_specs=[pl.BlockSpec(memory_space=pltpu.SMEM)] + [vmem] * len(ops),
+        out_specs=[vmem] * len(shapes),
+        compiler_params=pltpu.CompilerParams(vmem_limit_bytes=56 * 1024 * 1024),
+        cost_estimate=SMALL,
+    )(core.reshape(1), *ops)
+
+
+def finish_ffn(mine, other, core, scale, units):
+    width = mine[0].shape[1]
+    shapes = [(width, units), (width, units), (units, width)]
+    return finish(finish_ffn_kernel, shapes, core, scale, *mine, *other)
+
+
+def finish_attn(mine, other, shared, core, scale, heads):
+    width = shared.shape[1]
+    shapes = [(width, heads), (width, HD), (width, HD), (heads, width)]
+    return finish(finish_attn_kernel, shapes, core, scale, *mine, *other, shared)
+
+
+def halves(total, section, axis):
+    half = total.shape[axis] // 2
+    low, high = (lax.slice_in_dim(total, i * half, (i + 1) * half, axis=axis) for i in range(2))
+    return pick(section == 0, low, high), pick(section == 0, high, low)
 
 
 def to_owner(value, layer):
@@ -542,20 +640,19 @@
     own_rows = x_input.shape[2]
     scale = 1.0 / lax.axis_size("dp")
 
-    weights = gather_weights(
-        w_query[0], w_key[0], w_value[0], w_out[0], w_gate[0], w_up[0], w_down[0], section
+    def mine(value):
+        return lax.dynamic_index_in_dim(value[:, 0], section, 0, keepdims=False)
+
+    x = mine(x_input)
+    first, x_before, finish_weights = gather_weights(
+        x, w_query[0], w_key[0], w_value[0], w_out[0], w_gate[0], w_up[0], w_down[0], section
     )
     gains = jnp.concatenate([gain_attn, gain_ff])
     other_gains = swap(gains, "section")
-    for layer in range(2):
-        here = pick(section == layer, gains, other_gains)
-        weights[layer]["gain_attn"], weights[layer]["gain_ff"] = here[:1], here[1:]
-
-    def mine(value):
-        return lax.dynamic_index_in_dim(value[:, 0], section, 0, keepdims=False)
-
-    x = mine(x_input)
-    x_all = jnp.concatenate([from_before(x), x])
+    gains = [pick(section == layer, gains, other_gains) for layer in range(2)]
+    first.update(gain_attn=gains[0][:1], gain_ff=gains[0][1:])
+
+    x_all = jnp.concatenate([x_before, x])
     start = (gx * lax.axis_size("gy") + gy) * own_rows
     rows = start - WINDOW + jnp.arange(WINDOW + own_rows, dtype=jnp.int32)
     segment, where_in, valid = layout(mine(doc_lengths), rows)
@@ -563,62 +660,116 @@
     angles = where_in.astype(F32)[:, None] * frequency[None, :]
     place = (jnp.cos(angles), jnp.sin(angles), segment[WINDOW:, None], segment[None, :])
 
-    q_0, mixed_0, kv_0, normed_0, hidden_0 = attn_forward(x_all, weights[0], place)
-    out_0 = ffn_forward(hidden_0, weights[0])
-    out_all = jnp.concatenate([from_before(out_0), out_0])
-    q_1, mixed_1, kv_1, normed_1, hidden_1 = attn_forward(out_all, weights[1], place)
-    out_1 = ffn_forward(hidden_1, weights[1])
-    states = pick(section == 0, out_0, out_1)
-    other_states = swap(pick(section == 0, out_1, out_0), "section")
+    q_0, mixed_0, kv_0, normed_0, hidden_0 = attn_forward(x_all, first, place)
+    hidden_0, second = finish_weights(hidden_0)
+    out_0 = ffn_forward(hidden_0, first)
+    out_0, rows_before, second = second(out_0)
+    second.update(gain_attn=gains[1][:1], gain_ff=gains[1][1:])
+    out_all = jnp.concatenate([rows_before, out_0])
+    slot = lambda *values: lax.optimization_barrier(values)
+    q_1, mixed_1, kv_1, normed_1, hidden_1 = attn_forward(out_all, second, place)
+    out_0_other = lax.ppermute(out_0, "section", [(1, 0)])
+    hidden_1, out_0_other, up_1 = slot(hidden_1, out_0_other, second["up"])
+    up_1 = jnp.stack(up_1)
+    second.update(up=(up_1, swap(up_1, "gx")))
 
     order = 2 * gx + gy
-    barrier = lax.optimization_barrier
     dy = jnp.where(valid[WINDOW:, None], mine(cotangent), 0)
-
-    near, far, d_hidden, gain_ff = ffn_back(dy, hidden_1, weights[1])
-    ffn_1, ffn_far_1 = over_cores(near, far)
-    d_out, d_q, d_kv = attn_back(d_hidden, q_1, mixed_1, kv_1, weights[1], place)
-    d_q, d_kv, ffn_1, ffn_far_1 = barrier((d_q, d_kv, ffn_1, ffn_far_1))
-    ffn_got = swap(ffn_far_1, "gy")
-    behind = to_before(d_kv[:WINDOW].astype(BF16))
-    d_query, d_normed = query_back(d_q, normed_1, weights[1])
+    turn = w_gate.shape[2] // 2
+
+    def ffn_parts(near, got):
+        a_near, a_far = (near[i, :turn] + got[i, :turn] for i in range(2))
+        return a_near, a_far, near[:, turn:] + got[:, turn:]
+
+    far, before = ffn_back(dy, hidden_1, second, 1)
+    before, far = slot(before, far)
+    got = swap(far, "gx")
+    near, d_hidden, gain_ff = ffn_back(dy, hidden_1, second, 0, before)
+    near, d_hidden, gain_ff, got = slot(near, d_hidden, gain_ff, got)
+    a_near, a_far, b = ffn_parts(near, got)
+    b_keep, b_send = halves(b, section, 1)
+    a_got = swap(a_far, "gy")
+    b_got = swap(b_send, "section")
+    out_1 = ffn_forward(hidden_1, second)
+    d_out, d_q, d_kv = attn_back(d_hidden, q_1, mixed_1, kv_1, second, place)
+    d_q, d_kv, out_1, a_got, b_got = slot(d_q, d_kv, out_1, a_got, b_got)
+    sent = d_kv[:WINDOW].astype(BF16)
+    a_keep, a_send = halves(a_near + a_got, section, 0)
+    b = b_keep + b_got
+    behind = to_before(sent)
+    a_got = swap(a_send, "section")
+    d_query, d_normed = query_back(d_q, normed_1, second)
+    d_normed, behind, b, a_got = slot(d_normed, behind, b, a_got)
+    b_far = swap(b[1], "gy")
     grad_1, d_shared, gain_attn_grad = input_back(
-        d_kv, behind, normed_1, d_normed, out_0, d_hidden, weights[1], place
-    )
-    attn_1, attn_far_1 = over_cores(
-        *pack_attn(d_query, d_out, d_shared, gain_attn_grad, gain_ff, order)
-    )
-
-    near, far, d_hidden, gain_ff = ffn_back(grad_1, hidden_0, weights[0])
-    d_hidden, near, far, ffn_got, attn_1, attn_far_1 = barrier(
-        (d_hidden, near, far, ffn_got, attn_1, attn_far_1)
-    )
-    ffn_1 = over_section(ffn_1 + ffn_got, section)
-    attn_1 = attn_1 + swap(attn_far_1, "gy")
-    ffn_0, ffn_far_0 = over_cores(near, far)
-    d_out, d_q, d_kv = attn_back(d_hidden, q_0, mixed_0, kv_0, weights[0], place)
-    d_q, d_kv, attn_1, ffn_0, ffn_far_0 = barrier((d_q, d_kv, attn_1, ffn_0, ffn_far_0))
-    ffn_0 = ffn_0 + swap(ffn_far_0, "gy")
-    behind = to_before(d_kv[:WINDOW].astype(BF16))
-    d_query, d_normed = query_back(d_q, normed_0, weights[0])
+        d_kv, behind, normed_1, d_normed, out_0, d_hidden, second, place
+    )
+    near, far = pack_attn(d_query, d_out, d_shared, gain_attn_grad, gain_ff, order)
+    got = swap(far, "gx")
+    grad_1, near, got = slot(grad_1, near, got)
+
+    c_keep_1, c_send_1 = halves(near + got, section, 1)
+    c_send_a, c_send_b = c_send_1[0], c_send_1[1]
+    c_got_a = swap(c_send_a, "section")
+    far, before = ffn_back(grad_1, hidden_0, first, 1)
+    before, far, b_far, c_got_a = slot(before, far, b_far, c_got_a)
+    ffn_1 = jnp.concatenate([a_keep + a_got, b[0] + b_far])
+    got = swap(far, "gx")
+    c_got_b = swap(c_send_b, "section")
+    near, d_hidden, gain_ff = ffn_back(grad_1, hidden_0, first, 0, before)
+    near, d_hidden, gain_ff, got, c_got_b = slot(near, d_hidden, gain_ff, got, c_got_b)
+    a_near, a_far, b = ffn_parts(near, got)
+    b_keep, b_send = halves(b, section, 1)
+    b_got = swap(b_send, "section")
+    a_got = swap(a_far, "gy")
+    d_out, d_q, d_kv = attn_back(d_hidden, q_0, mixed_0, kv_0, first, place)
+    c_1 = [c_keep_1[0] + c_got_a, c_keep_1[1] + c_got_b]
+    d_q, d_kv, a_got = slot(d_q, d_kv, a_got)
+    sent = d_kv[:WINDOW].astype(BF16)
+    a_keep, a_send = halves(a_near + a_got, section, 0)
+    behind = to_before(sent)
+    a_got = swap(a_send, "section")
+    d_query, d_normed = query_back(d_q, normed_0, first)
+    d_normed, behind, b_got, a_got = slot(d_normed, behind, b_got, a_got)
+    b = b_keep + b_got
+    b_far = swap(b[1], "gy")
     grad_0, d_shared, gain_attn_grad = input_back(
-        d_kv, behind, normed_0, d_normed, x, d_hidden, weights[0], place
-    )
-    attn_1 = over_section(attn_1, section)
-    grad_0, ffn_1, attn_1 = barrier((grad_0, ffn_1, attn_1))
-    layer_1 = lax.psum(jnp.concatenate([ffn_1, attn_1]), "dp")
-    attn_0, far = over_cores(*pack_attn(d_query, d_out, d_shared, gain_attn_grad, gain_ff, order))
-    attn_0 = attn_0 + swap(far, "gy")
-    ffn_0 = over_section(ffn_0, section)
-    attn_0 = over_section(attn_0, section)
-    layer_1, ffn_0, attn_0 = barrier((layer_1, ffn_0, attn_0))
-    layer_1_got = to_owner(layer_1, 1)
-    layer_0 = lax.psum(jnp.concatenate([ffn_0, attn_0]), "dp")
-    layer_0_got = to_owner(layer_0, 0)
-    split = ffn_0.shape[0]
-
-    in_grads = pick(section == 0, grad_0, grad_1)
-    other_grads = swap(pick(section == 0, grad_1, grad_0), "section")
+        d_kv, behind, normed_0, d_normed, x, d_hidden, first, place
+    )
+    near, far = pack_attn(d_query, d_out, d_shared, gain_attn_grad, gain_ff, order)
+    got = swap(far, "gx")
+    near, got, b_far = slot(near, got, b_far)
+    count = ffn_1.shape[0]
+    ffn = lax.psum(jnp.concatenate([ffn_1, a_keep + a_got, b[0] + b_far]), "dp")
+    c_keep, c_send = halves(near + got, section, 1)
+    c_got = swap(c_send, "section")
+    c_far_1 = swap(c_1[1], "gy")
+    c_keep, c_got, c_far_1 = slot(c_keep, c_got, c_far_1)
+    c = c_keep + c_got
+    c_far = swap(c[1], "gy")
+    grad_other = swap(pick(section == 0, grad_1, grad_0), "section")
+    out_1_other = lax.ppermute(out_1, "section", [(0, 1)])
+    ffn, c_far, grad_other, out_1_other = slot(ffn, c_far, grad_other, out_1_other)
+    attn = jnp.concatenate([c_1[0] + c_far_1, c[0] + c_far])
+    half = ffn.shape[0] // 2
+    sent = pick(section == 0, ffn[:half], ffn[half:])
+    ffn_got = swap(sent, "section")
+    attn = lax.psum(attn, "dp")
+    attn, ffn_got = slot(attn, ffn_got)
+
+    def two_halves(both, got):
+        half = both.shape[0] // 2
+        mine = pick(section == 0, both[half:], both[:half])
+        return pick(section == 0, mine, got), pick(section == 0, got, mine)
+
+    half = attn.shape[0] // 2
+    attn_got = swap(pick(section == 0, attn[:half], attn[half:]), "section")
+    ffn_mine = two_halves(ffn, ffn_got)
+    gate, up, down = finish_ffn(
+        ffn_mine, [swap(value, "gx") for value in ffn_mine], gx, scale, w_gate.shape[2]
+    )
+    states, in_grads = pick(section == 0, out_0, out_1), pick(section == 0, grad_0, grad_1)
+    other_states = pick(section == 0, out_0_other, out_1_other)
 
     def by_micro(own, other):
         first = section == 0
@@ -626,46 +777,32 @@
             None, :, None
         ]
 
-    def finished(own_0, got_0, own_1, got_1):
-        own, got = pick(section == 0, own_0, own_1), pick(section == 0, got_0, got_1)
-        return jnp.concatenate([pick(section == 0, own, got), pick(section == 0, got, own)])
-
-    def part(lo, hi):
-        return finished(
-            layer_0[lo:hi], layer_0_got[lo:hi], layer_1[lo:hi], layer_1_got[lo:hi]
-        )
-
-    ffn, attn = part(0, split), part(split, None)
-    heads, hidden = w_query.shape[2] // 2, w_gate.shape[2] // 2
-    quarter = attn[2 * heads : -GAIN_ROWS]
-    quarter_beside = swap(quarter, "gy")
-    shared_half = pick(
-        gy == 0,
-        jnp.concatenate([quarter, quarter_beside]),
-        jnp.concatenate([quarter_beside, quarter]),
-    )
-    gain_sums = attn[-GAIN_ROWS : 2 - GAIN_ROWS].astype(F32) * scale
-    ffn_other = swap(ffn, "gx")
-    attn_other = swap(jnp.concatenate([attn[: 2 * heads], shared_half]), "gx")
-
-    def both_cores(mine, other):
-        low, high = pick(gx == 0, mine, other), pick(gx == 0, other, mine)
-        return jnp.concatenate([low, high]).astype(F32) * scale
-
-    gate = both_cores(ffn[:hidden], ffn_other[:hidden]).T
-    up = both_cores(ffn[hidden : 2 * hidden], ffn_other[hidden : 2 * hidden]).T
-    down = both_cores(ffn[2 * hidden :], ffn_other[2 * hidden :])
-    query = both_cores(attn[:heads], attn_other[:heads]).T
-    out = both_cores(attn[heads : 2 * heads], attn_other[heads : 2 * heads])
-    shared = both_cores(shared_half, attn_other[2 * heads :]).T
+    states, in_grads = by_micro(states, other_states), by_micro(in_grads, grad_other)
+    attn_got, gate, up, down, states, in_grads = slot(attn_got, gate, up, down, states, in_grads)
+    attn_low, high = two_halves(attn, attn_got)
+    attn_others = swap(attn_low, "gx"), swap(high, "gx")
+    count = d_shared.shape[0] // STEPS
+    quarter = high[-GAIN_ROWS - count : -GAIN_ROWS]
+    gain_sums = high[-GAIN_ROWS : 2 - GAIN_ROWS].astype(F32) * scale
+    beside = swap(quarter, "gy")
+    both = pick(
+        gy == 0, jnp.concatenate([quarter, beside]), jnp.concatenate([beside, quarter])
+    )
+    both_other = swap(both, "gx")
+    shared = pick(
+        gx == 0, jnp.concatenate([both, both_other]), jnp.concatenate([both_other, both])
+    )
+    query, key, value, out = finish_attn(
+        (attn_low, high), attn_others, shared, gx, scale, w_query.shape[2]
+    )
 
     return (
-        by_micro(states, other_states),
-        by_micro(in_grads, other_grads),
+        states,
+        in_grads,
         gain_sums[:1],
         query[None],
-        shared[None, :, :HD],
-        shared[None, :, HD:],
+        key[None],
+        value[None],
         out[None],
         gain_sums[1:],
         gate[None],

time: 667 us -> 553 us (0.83)
  waiting for transfers between devices: 343 us -> 203 us
  starting transfers between devices: 38.5 us -> 55 us
  Pallas kernels: 144 us -> 160 us
    ppermute x38 -> x52, waiting for transfers between devices: 235 us -> 99.3 us  [swap(): return lax.ppermute(value, axis, [(0, 1), (1, 0)])]
    ppermute x38 -> x52, starting transfers between devices: 23.5 us -> 41.3 us  [swap(): return lax.ppermute(value, axis, [(0, 1), (1, 0)])]
    pallas_call x2 -> x6, Pallas kernels: 44.6 us -> 60.5 us  [the longest x4 49.6 us: ffn_back(): pl.pallas_call(functools.partial(ffn_back_kernel, last), grid=(2,), out_s...]
    ppermute x2, waiting for transfers between devices: 0.01 us -> 9.76 us  [the longest x1 9.76 us: local(): out_1_other = lax.ppermute(out_1, 'section', [(0, 1)])]
    ppermute x2, waiting for transfers between devices: 11.3 us -> 3.18 us  [to_before(): return lax.ppermute(value, ('gx', 'gy'), [(1, 0), (2, 1), (3, 2)])]
    psum x2, waiting for transfers between devices: 86.1 us -> 78.8 us  [the longest x1 44.7 us: local(): attn = lax.psum(attn, 'dp')]
    add x12 -> x18, other arithmetic: 13.9 us -> 19 us  [the longest x2 5.47 us: ffn_parts(): return (a_near, a_far, near[:, turn:] + got[:, turn:])]
    unnamed x87 -> x170, local copies, waits for them, and re-layouts: 14.2 us -> 12.1 us
  transfers between devices with their start and end apart: 46 -> 60, of which waited for: 21 -> 24; matrix products, arithmetic and copies ran while one was open for 11% -> 13% of each run, Pallas kernels for 17% -> 25%
where the time goes in v4:
time: 553 us; the launch traced here: 544 us
  waiting for transfers between devices  203 us (37%)
  Pallas kernels  160 us (29%)
  other arithmetic  71.7 us (13%)
  starting transfers between devices  55 us (10%)
  local copies, waits for them, and re-layouts  38.1 us (7%)
  between operations  15.7 us (3%)
    ppermute x52, waiting for transfers between devices, swap(): return lax.ppermute(value, axis, [(0, 1), (1, 0)])  99.3 us
    pallas_call x4, Pallas kernels, ffn_back(): pl.pallas_call(functools.partial(ffn_back_kernel, last), grid=(2,), out_s...  49.6 us
    psum x1, waiting for transfers between devices, local(): attn = lax.psum(attn, 'dp')  44.7 us
    ppermute x52, starting transfers between devices, swap(): return lax.ppermute(value, axis, [(0, 1), (1, 0)])  41.3 us
    psum x1, waiting for transfers between devices, local(): ffn = lax.psum(jnp.concatenate([ffn_1, a_keep + a_got, b[0] + b_far]), 'dp')  34.1 us
    pallas_call x2, Pallas kernels, attn_forward(): pl.pallas_call(attn_kernel, out_shape=(jax.ShapeDtypeStruct(heads, BF16),...  28.4 us
    pallas_call x2, Pallas kernels, attn_back(): pl.pallas_call(attn_back_kernel, out_shape=(jax.ShapeDtypeStruct(outs, BF...  28.2 us
    pallas_call x2, Pallas kernels, ffn_forward(): pl.pallas_call(ffn_kernel, out_shape=jax.ShapeDtypeStruct((rows, width),...  20.2 us
  transfers between devices with their start and end apart: 60, of which 24 were waited for; matrix products, arithmetic and copies ran while one was open for 13% of the time, Pallas kernels for 25%

profile of v4, /device:TPU:0, one launch (start us, length us, event | category | flops | bytes accessed | tf_op | source)
XLA Modules:
  0.0 543.8 jit_solution(14026497368689317361)
XLA Ops:
  27.5 8.4 %collective-permute-done = bf16[640,512]{1,0:T(8,128)(2,1)S(1)} collective-permute-done((bf16[640,512]{1,0:T(8,128)(2,1)}, bf16[640,512]{1,0:T(8,128)(2,1)S(1)}, u32[]{:S(2)}, u32[]{:S(2)}) %collective-permute-start) | collective-permute-done | bytes 655392 | tf_op jit(solution)/shard_map/ppermute | solution.py:19
  60.9 8.2 %collective-permute-done.8 = bf16[640,512]{1,0:T(8,128)(2,1)S(1)} collective-permute-done((bf16[640,512]{1,0:T(8,128)(2,1)}, bf16[640,512]{1,0:T(8,128)(2,1)S(1)}, u32[]{:S(2)}, u32[]{:S(2)}) %collective-permute-start.8) | collective-permute-done | bytes 655392 | tf_op jit(solution)/shard_map/ppermute | solution.py:19
  79.8 14.1 %shard_map.203 = (bf16[4,512,256]{2,1,0:T(8,128)(2,1)}, bf16[4,512,256]{2,1,0:T(8,128)(2,1)}, bf16[1024,512]{1,0:T(8,128)(2,1)}, bf16[512,640]{1,0:T(8,128)(2,1)}, f32[512,640]{1,0:T(8,128)}) custom-call(bf16[1024,640]{1,0:T(8,128)(2,1)} %pad_maximum_fusion.13.x_ref, f32[1,640]{1,0:T(1,128)} %get-tuple-element.371.gain, bf16[2,640,256]{2,1,0:T(8,128)(2,1)} %copy-done.14, ...), custom_call_target="tpu_custom_call" | custom-call | flops 1000 | bytes 1000 | tf_op jit(solution)/shard_map/pallas_call | solution.py:279
  112.5 10.1 %shard_map.204.x_ref = bf16[512,640]{1,0:T(8,128)(2,1)} custom-call(f32[512,640]{1,0:T(8,128)} %get-tuple-element.148.hidden, f32[1,640]{1,0:T(1,128)} %get-tuple-element.370.gain, bf16[2,640,512]{2,1,0:T(8,128)(2,1)} %copy-done.3, bf16[2,640,512]{2,1,0:T(8,128)(2,1)} %copy-done.21, bf16[2,640,512]{2,1,0:T(8,128)(2,1)} %copy-done.2, ...), custom_call_target="tpu_custom_call" | custom-call | flops 1000 | bytes 1000 | tf_op jit(solution)/shard_map/pallas_call | solution.py:336
  131.4 11.9 %collective-permute-done.21 = bf16[512,640]{1,0:T(8,128)(2,1)S(1)} collective-permute-done((bf16[512,640]{1,0:T(8,128)(2,1)}, bf16[512,640]{1,0:T(8,128)(2,1)S(1)}, u32[]{:S(2)}, u32[]{:S(2)}) %collective-permute-start.21) | collective-permute-done | bytes 655392 | tf_op jit(solution)/shard_map/ppermute | solution.py:177
  150.4 14.3 %shard_map.205 = (bf16[4,512,256]{2,1,0:T(8,128)(2,1)}, bf16[4,512,256]{2,1,0:T(8,128)(2,1)}, bf16[1024,512]{1,0:T(8,128)(2,1)}, bf16[512,640]{1,0:T(8,128)(2,1)}, f32[512,640]{1,0:T(8,128)}) custom-call(bf16[1024,640]{1,0:T(8,128)(2,1)} %pad_maximum_fusion.17.x_ref, f32[1,640]{1,0:T(1,128)} %get-tuple-element.369.gain, bf16[2,640,256]{2,1,0:T(8,128)(2,1)} %copy-done.15, ...), custom_call_target="tpu_custom_call" | custom-call | flops 1000 | bytes 1000 | tf_op jit(solution)/shard_map/pallas_call | solution.py:279
  171.0 11.8 %shard_map.206 = (bf16[2,1536,640]{2,1,0:T(8,128)(2,1)}, f32[512,640]{1,0:T(8,128)}) custom-call(bf16[512,640]{1,0:T(8,128)(2,1)} %bitcast_select_fusion.dy, f32[512,640]{1,0:T(8,128)} %get-tuple-element.162.hidden, f32[1,640]{1,0:T(1,128)} %get-tuple-element.368.gain, f32[8,128]{1,0:T(8,128)} %broadcast_2_before.2.before, bf16[2,640,512]{2,1,0:T(8,128)(2,1)} %copy-done.23, ...), custom_call_target="tpu_custom_call" | custom-call | flops 1000 | bytes 1000 | tf_op jit(solution)/shard_map/pallas_call | solution.py:393
  183.0 13.2 %shard_map.207 = (bf16[2,1536,640]{2,1,0:T(8,128)(2,1)}, f32[512,640]{1,0:T(8,128)}, f32[1,640]{1,0:T(1,128)}) custom-call(bf16[512,640]{1,0:T(8,128)(2,1)} %bitcast_select_fusion.dy, f32[512,640]{1,0:T(8,128)} %get-tuple-element.162.hidden, f32[1,640]{1,0:T(1,128)} %get-tuple-element.368.gain, f32[512,640]{1,0:T(8,128)} %get-tuple-element.169.before, ...), custom_call_target="tpu_custom_call" | custom-call | flops 1000 | bytes 1000 | tf_op jit(solution)/shard_map/pallas_call | solution.py:393
  206.4 10.0 %shard_map.209 = bf16[512,640]{1,0:T(8,128)(2,1)} custom-call(f32[512,640]{1,0:T(8,128)} %get-tuple-element.162.hidden, f32[1,640]{1,0:T(1,128)} %get-tuple-element.368.gain, bf16[2,640,512]{2,1,0:T(8,128)(2,1)} %copy-done.6, bf16[2,640,512]{2,1,0:T(8,128)(2,1)} %copy-done.23, bf16[2,640,512]{2,1,0:T(8,128)(2,1)} %copy-done.7, ...), custom_call_target="tpu_custom_call" | custom-call | flops 1000 | bytes 1000 | tf_op jit(solution)/shard_map/pallas_call | solution.py:336
  216.4 14.1 %shard_map.208 = (bf16[4,256,640]{2,1,0:T(8,128)(2,1)}, bf16[4,512,256]{2,1,0:T(8,128)(2,1)}, f32[1024,512]{1,0:T(8,128)}) custom-call(f32[512,640]{1,0:T(8,128)} %get-tuple-element.174.d_hidden, bf16[4,512,256]{2,1,0:T(8,128)(2,1)} %get-tuple-element.175.q, bf16[4,512,256]{2,1,0:T(8,128)(2,1)} %get-tuple-element.176.mixed, ...), custom_call_target="tpu_custom_call" | custom-call | flops 1000 | bytes 1000 | tf_op jit(solution)/shard_map/pallas_call | solution.py:447
  238.4 6.2 %shard_map.210 = (bf16[4,256,640]{2,1,0:T(8,128)(2,1)}, f32[512,640]{1,0:T(8,128)}) custom-call(bf16[4,512,256]{2,1,0:T(8,128)(2,1)} %get-tuple-element.183.d_q, bf16[512,640]{1,0:T(8,128)(2,1)} %get-tuple-element.184.normed, bf16[2,640,256]{2,1,0:T(8,128)(2,1)} %copy-done.15, bf16[2,640,256]{2,1,0:T(8,128)(2,1)} %copy-done.37), custom_call_target="tpu_custom_call" | custom-call | flops 1000 | bytes 1000 | tf_op jit(solution)/shard_map/pallas_call | solution.py:486
  270.7 11.7 %shard_map.212 = (bf16[2,1536,640]{2,1,0:T(8,128)(2,1)}, f32[512,640]{1,0:T(8,128)}) custom-call(bf16[512,640]{1,0:T(8,128)(2,1)} %get-tuple-element.198.dy, f32[512,640]{1,0:T(8,128)} %get-tuple-element.148.hidden, f32[1,640]{1,0:T(1,128)} %get-tuple-element.370.gain, f32[8,128]{1,0:T(8,128)} %broadcast_2_before.2.before, bf16[2,640,512]{2,1,0:T(8,128)(2,1)} %copy-done.21, ...), custom_call_target="tpu_custom_call" | custom-call | flops 1000 | bytes 1000 | tf_op jit(solution)/shard_map/pallas_call | solution.py:393
  283.5 12.9 %shard_map.213 = (bf16[2,1536,640]{2,1,0:T(8,128)(2,1)}, f32[512,640]{1,0:T(8,128)}, f32[1,640]{1,0:T(1,128)}) custom-call(bf16[512,640]{1,0:T(8,128)(2,1)} %get-tuple-element.198.dy, f32[512,640]{1,0:T(8,128)} %get-tuple-element.148.hidden, f32[1,640]{1,0:T(1,128)} %get-tuple-element.370.gain, f32[512,640]{1,0:T(8,128)} %get-tuple-element.203.before, ...), custom_call_target="tpu_custom_call" | custom-call | flops 1000 | bytes 1000 | tf_op jit(solution)/shard_map/pallas_call | solution.py:393
  302.9 14.1 %shard_map.214 = (bf16[4,256,640]{2,1,0:T(8,128)(2,1)}, bf16[4,512,256]{2,1,0:T(8,128)(2,1)}, f32[1024,512]{1,0:T(8,128)}) custom-call(f32[512,640]{1,0:T(8,128)} %get-tuple-element.208.d_hidden, bf16[4,512,256]{2,1,0:T(8,128)(2,1)} %get-tuple-element.209.q, bf16[4,512,256]{2,1,0:T(8,128)(2,1)} %get-tuple-element.210.mixed, ...), custom_call_target="tpu_custom_call" | custom-call | flops 1000 | bytes 1000 | tf_op jit(solution)/shard_map/pallas_call | solution.py:447
  323.4 6.5 %shard_map.215 = (bf16[4,256,640]{2,1,0:T(8,128)(2,1)}, f32[512,640]{1,0:T(8,128)}) custom-call(bf16[4,512,256]{2,1,0:T(8,128)(2,1)} %get-tuple-element.216.d_q, bf16[512,640]{1,0:T(8,128)(2,1)} %get-tuple-element.217.normed, bf16[2,640,256]{2,1,0:T(8,128)(2,1)} %copy-done.14, bf16[2,640,256]{2,1,0:T(8,128)(2,1)} %collective-permute-done.7.wq_b), custom_call_target="tpu_custom_call" | custom-call | flops 1000 | bytes 1000 | tf_op jit(solution)/shard_map/pallas_call | solution.py:486
  331.7 8.2 %collective-permute-done.42 = bf16[256,640]{1,0:T(8,128)(2,1)S(1)} collective-permute-done((bf16[256,640]{1,0:T(8,128)(2,1)S(1)}, bf16[256,640]{1,0:T(8,128)(2,1)S(1)}, u32[]{:S(2)}, u32[]{:S(2)}) %collective-permute-start.42) | collective-permute-done | bytes 327712 | tf_op jit(solution)/shard_map/ppermute | solution.py:19
  356.8 14.3 %collective-permute-done.44 = bf16[512,640]{1,0:T(8,128)(2,1)S(1)} collective-permute-done((bf16[512,640]{1,0:T(8,128)(2,1)S(1)}, bf16[512,640]{1,0:T(8,128)(2,1)S(1)}, u32[]{:S(2)}, u32[]{:S(2)}) %collective-permute-start.44) | collective-permute-done | bytes 655392 | tf_op jit(solution)/shard_map/ppermute | solution.py:19
  379.5 6.6 %collective-permute-done.46 = bf16[336,640]{1,0:T(8,128)(2,1)S(1)} collective-permute-done((bf16[336,640]{1,0:T(8,128)(2,1)S(1)}, bf16[336,640]{1,0:T(8,128)(2,1)S(1)}, u32[]{:S(2)}, u32[]{:S(2)}) %collective-permute-start.46) | collective-permute-done | bytes 430112 | tf_op jit(solution)/shard_map/ppermute | solution.py:19
  386.1 9.4 %collective-permute-done.45 = bf16[2,336,640]{2,1,0:T(8,128)(2,1)S(1)} collective-permute-done((bf16[2,336,640]{2,1,0:T(8,128)(2,1)S(1)}, bf16[2,336,640]{2,1,0:T(8,128)(2,1)S(1)}, u32[]{:S(2)}, u32[]{:S(2)}) %collective-permute-start.45) | collective-permute-done | bytes 860192 | tf_op jit(solution)/shard_map/ppermute | solution.py:19
  398.4 9.8 %collective-permute-done.49 = bf16[512,640]{1,0:T(8,128)(2,1)S(1)} collective-permute-done((bf16[512,640]{1,0:T(8,128)(2,1)S(1)}, bf16[512,640]{1,0:T(8,128)(2,1)S(1)}, u32[]{:S(2)}, u32[]{:S(2)}) %collective-permute-start.49) | collective-permute-done | bytes 655392 | tf_op jit(solution)/shard_map/ppermute | solution.py:751
  409.0 11.9 %collective-permute-done.48 = bf16[512,640]{1,0:T(8,128)(2,1)S(1)} collective-permute-done((bf16[512,640]{1,0:T(8,128)(2,1)S(1)}, bf16[512,640]{1,0:T(8,128)(2,1)S(1)}, u32[]{:S(2)}, u32[]{:S(2)}) %collective-permute-start.48) | collective-permute-done | bytes 655392 | tf_op jit(solution)/shard_map/ppermute | solution.py:19
  421.7 34.1 %all-reduce.5.cloned.1.call-done = bf16[1536,640]{1,0:T(8,128)(2,1)} async-done(((bf16[1536,640]{1,0:T(8,128)(2,1)}), bf16[1536,640]{1,0:T(8,128)(2,1)}) %all-reduce.5.cloned.1.call-update) | async-done | bytes 1966096 | tf_op jit(solution)/shard_map/psum | solution.py:743
  461.0 44.7 %all-reduce.7.cloned.1.call-done = bf16[672,640]{1,0:T(8,128)(2,1)} async-done(((bf16[672,640]{1,0:T(8,128)(2,1)}), bf16[672,640]{1,0:T(8,128)(2,1)}) %all-reduce.7.cloned.1.call-update) | async-done | bytes 860176 | tf_op jit(solution)/shard_map/psum | solution.py:757
  515.3 6.9 %shard_map.217 = (f32[640,1024]{1,0:T(8,128)}, f32[640,1024]{1,0:T(8,128)}, f32[1024,640]{1,0:T(8,128)}) custom-call(s32[1]{0:T(128)} %bitcast.71.core, bf16[768,640]{1,0:T(8,128)(2,1)} %copy-done.27, bf16[768,640]{1,0:T(8,128)(2,1)} %copy-done.26, bf16[768,640]{1,0:T(8,128)(2,1)} %copy-done.50, bf16[768,640]{1,0:T(8,128)(2,1)} %copy-done.49), custom_call_target="tpu_custom_call" | custom-call | flops 1000 | bytes 1000 | tf_op jit(solution)/shard_map/pallas_call | solution.py:592
  (402 shorter events, 214.8 us)
Async XLA Ops:
  7.2 448.6 %all-reduce.5.cloned.1.call-start = ((), (), s32[]{:S(2)}) async-start(), calls=%async_computation | async-start | bytes 3932160 | tf_op jit(solution)/shard_map/psum | solution.py:743
  13.0 26.6 %collective-permute-start.9 = (bf16[512,640]{1,0:T(8,128)(2,1)}, bf16[512,640]{1,0:T(8,128)(2,1)S(1)}, u32[]{:S(2)}, u32[]{:S(2)}) collective-permute-start(bf16[512,640]{1,0:T(8,128)(2,1)} %fusion.26), channel_id=1, source_target_pairs={{0,4},{4,0},{1,5},{5,1},{2,6},{6,2},{3,7},{7,3},{8,12},{12,8},{9,1... | collective-permute-start | bytes 1966088 | tf_op jit(solution)/shard_map/ppermute | solution.py:19
  15.6 35.8 %collective-permute-start.4 = (bf16[512,640]{1,0:T(8,128)(2,1)S(1)}, bf16[512,640]{1,0:T(8,128)(2,1)}, u32[]{:S(2)}, u32[]{:S(2)}) collective-permute-start(bf16[512,640]{1,0:T(8,128)(2,1)S(1)} %dynamic-slice_bitcast_fusion.x_ref), channel_id=1, source_target_pairs={{0,4},{4,8},{8,12},{1,5},{5,9},{9,13},{2,6},{6,10},{10,14},{3,7},{... | collective-permute-start | bytes 1966088 | tf_op jit(solution)/shard_map/ppermute | solution.py:177
  39.5 29.5 %collective-permute-start.8 = (bf16[640,512]{1,0:T(8,128)(2,1)}, bf16[640,512]{1,0:T(8,128)(2,1)S(1)}, u32[]{:S(2)}, u32[]{:S(2)}) collective-permute-start(bf16[640,512]{1,0:T(8,128)(2,1)} %dynamic-slice_bitcast_fusion.2), channel_id=1, source_target_pairs={{0,16},{16,0},{1,17},{17,1},{2,18},{18,2},{3,19},{19,3},{4,20},{20... | collective-permute-start | bytes 1966088 | tf_op jit(solution)/shard_map/ppermute | solution.py:19
  50.9 21.5 %collective-permute-start.6 = (f32[2,640]{1,0:T(2,128)S(1)}, f32[2,640]{1,0:T(2,128)S(1)}, u32[]{:S(2)}, u32[]{:S(2)}) collective-permute-start(f32[2,640]{1,0:T(2,128)S(1)} %pad_maximum_fusion.28), channel_id=1, source_target_pairs={{0,16},{16,0},{1,17},{17,1},{2,18},{18,2},{3,19},{19,3},{4,20},{20... | collective-permute-start | bytes 15368 | tf_op jit(solution)/shard_map/ppermute | solution.py:19
  57.6 44.5 %collective-permute-start.13 = (bf16[640,512]{1,0:T(8,128)(2,1)}, bf16[640,512]{1,0:T(8,128)(2,1)}, u32[]{:S(2)}, u32[]{:S(2)}) collective-permute-start(bf16[640,512]{1,0:T(8,128)(2,1)} %get-tuple-element.325), channel_id=1, source_target_pairs={{0,4},{4,0},{1,5},{5,1},{2,6},{6,2},{3,7},{7,3},{8,12},{12,8},{9,1... | collective-permute-start | bytes 1966088 | tf_op jit(solution)/shard_map/ppermute | solution.py:19
  69.1 37.3 %collective-permute-start.18 = (bf16[2,512,640]{2,1,0:T(8,128)(2,1)S(1)}, bf16[2,512,640]{2,1,0:T(8,128)(2,1)}, u32[]{:S(2)}, u32[]{:S(2)}) collective-permute-start(bf16[2,512,640]{2,1,0:T(8,128)(2,1)S(1)} %pad_maximum_fusion.14), channel_id=1, source_target_pairs={{0,16},{16,0},{1,17},{17,1},{2,18},{18,2},{3,19},{19,3},{4,20},{20... | collective-permute-start | bytes 3932168 | tf_op jit(solution)/shard_map/ppermute | solution.py:19
  72.4 29.7 %collective-permute-start.12 = (bf16[640,512]{1,0:T(8,128)(2,1)}, bf16[640,512]{1,0:T(8,128)(2,1)}, u32[]{:S(2)}, u32[]{:S(2)}) collective-permute-start(bf16[640,512]{1,0:T(8,128)(2,1)} %get-tuple-element.327), channel_id=1, source_target_pairs={{0,4},{4,0},{1,5},{5,1},{2,6},{6,2},{3,7},{7,3},{8,12},{12,8},{9,1... | collective-permute-start | bytes 1966088 | tf_op jit(solution)/shard_map/ppermute | solution.py:19
  74.9 22.4 %collective-permute-start.15 = (bf16[256,640]{1,0:T(8,128)(2,1)}, bf16[256,640]{1,0:T(8,128)(2,1)S(1)}, u32[]{:S(2)}, u32[]{:S(2)}) collective-permute-start(bf16[256,640]{1,0:T(8,128)(2,1)} %get-tuple-element.344), channel_id=1, source_target_pairs={{0,4},{4,0},{1,5},{5,1},{2,6},{6,2},{3,7},{7,3},{8,12},{12,8},{9,1... | collective-permute-start | bytes 983048 | tf_op jit(solution)/shard_map/ppermute | solution.py:19
  76.0 26.1 %collective-permute-start.14 = (bf16[640,256]{1,0:T(8,128)(2,1)}, bf16[640,256]{1,0:T(8,128)(2,1)S(1)}, u32[]{:S(2)}, u32[]{:S(2)}) collective-permute-start(bf16[640,256]{1,0:T(8,128)(2,1)} %get-tuple-element.330), channel_id=1, source_target_pairs={{0,4},{4,0},{1,5},{5,1},{2,6},{6,2},{3,7},{7,3},{8,12},{12,8},{9,1... | collective-permute-start | bytes 983048 | tf_op jit(solution)/shard_map/ppermute | solution.py:19
  129.6 20.0 %collective-permute-start.22 = (bf16[2,640,256]{2,1,0:T(8,128)(2,1)S(1)}, bf16[2,640,256]{2,1,0:T(8,128)(2,1)S(1)}, u32[]{:S(2)}, u32[]{:S(2)}) collective-permute-start(bf16[2,640,256]{2,1,0:T(8,128)(2,1)S(1)} %pad_maximum_fusion.24.wq_a), channel_id=1, source_target_pairs={{0,8},{8,0},{1,9},{9,1},{2,10},{10,2},{3,11},{11,3},{4,12},{12,4},... | collective-permute-start | bytes 1966088 | tf_op jit(solution)/shard_map/ppermute | solution.py:19
  130.1 34.6 %collective-permute-start.24 = (bf16[512,640]{1,0:T(8,128)(2,1)S(1)}, bf16[512,640]{1,0:T(8,128)(2,1)}, u32[]{:S(2)}, u32[]{:S(2)}) collective-permute-start(bf16[512,640]{1,0:T(8,128)(2,1)S(1)} %copy-done.8), channel_id=1, source_target_pairs={{16,0},{17,1},{18,2},{19,3},{20,4},{21,5},{22,6},{23,7},{24,8},{25... | collective-permute-start | bytes 1966088 | tf_op jit(solution)/shard_map/ppermute | solution.py:671
  143.4 21.4 %collective-permute-start.25 = (bf16[640,512]{1,0:T(8,128)(2,1)S(1)}, bf16[640,512]{1,0:T(8,128)(2,1)}, u32[]{:S(2)}, u32[]{:S(2)}) collective-permute-start(bf16[640,512]{1,0:T(8,128)(2,1)S(1)} %copy-done.35), channel_id=1, source_target_pairs={{0,4},{4,0},{1,5},{5,1},{2,6},{6,2},{3,7},{7,3},{8,12},{12,8},{9,1... | collective-permute-start | bytes 1966088 | tf_op jit(solution)/shard_map/ppermute | solution.py:19
  200.9 31.3 %collective-permute-start.31 = (bf16[2,512,640]{2,1,0:T(8,128)(2,1)}, bf16[2,512,640]{2,1,0:T(8,128)(2,1)}, u32[]{:S(2)}, u32[]{:S(2)}) collective-permute-start(bf16[2,512,640]{2,1,0:T(8,128)(2,1)} %broadcast_select_fusion.2), channel_id=1, source_target_pairs={{0,16},{16,0},{1,17},{17,1},{2,18},{18,2},{3,19},{19,3},{4,20},{20... | collective-permute-start | bytes 3932168 | tf_op jit(solution)/shard_map/ppermute | solution.py:19
  204.0 27.9 %collective-permute-start.30 = (bf16[512,640]{1,0:T(8,128)(2,1)}, bf16[512,640]{1,0:T(8,128)(2,1)}, u32[]{:S(2)}, u32[]{:S(2)}) collective-permute-start(bf16[512,640]{1,0:T(8,128)(2,1)} %add_bitcast_fusion.1), channel_id=1, source_target_pairs={{0,4},{4,0},{1,5},{5,1},{2,6},{6,2},{3,7},{7,3},{8,12},{12,8},{9,1... | collective-permute-start | bytes 1966088 | tf_op jit(solution)/shard_map/ppermute | solution.py:19
  301.8 38.1 %collective-permute-start.41 = (bf16[2,512,640]{2,1,0:T(8,128)(2,1)}, bf16[2,512,640]{2,1,0:T(8,128)(2,1)}, u32[]{:S(2)}, u32[]{:S(2)}) collective-permute-start(bf16[2,512,640]{2,1,0:T(8,128)(2,1)} %broadcast_select_fusion.1), channel_id=1, source_target_pairs={{0,16},{16,0},{1,17},{17,1},{2,18},{18,2},{3,19},{19,3},{4,20},{20... | collective-permute-start | bytes 3932168 | tf_op jit(solution)/shard_map/ppermute | solution.py:19
  319.4 20.5 %collective-permute-start.40 = (bf16[512,512]{1,0:T(8,128)(2,1)}, bf16[512,512]{1,0:T(8,128)(2,1)}, u32[]{:S(2)}, u32[]{:S(2)}) collective-permute-start(bf16[512,512]{1,0:T(8,128)(2,1)} %slice.455), channel_id=1, source_target_pairs={{4,0},{8,4},{12,8},{5,1},{9,5},{13,9},{6,2},{10,6},{14,10},{7,3},{... | collective-permute-start | bytes 1572872 | tf_op jit(solution)/shard_map/ppermute | solution.py:181
  351.1 20.0 %collective-permute-start.43 = (bf16[2,672,640]{2,1,0:T(8,128)(2,1)S(1)}, bf16[2,672,640]{2,1,0:T(8,128)(2,1)S(1)}, u32[]{:S(2)}, u32[]{:S(2)}) collective-permute-start(bf16[2,672,640]{2,1,0:T(8,128)(2,1)S(1)} %pad_maximum_fusion.12), channel_id=1, source_target_pairs={{0,8},{8,0},{1,9},{9,1},{2,10},{10,2},{3,11},{11,3},{4,12},{12,4},... | collective-permute-start | bytes 5160968 | tf_op jit(solution)/shard_map/ppermute | solution.py:19
  372.7 133.0 %all-reduce.7.cloned.1.call-start = ((), (), s32[]{:S(2)}) async-start(), calls=%async_computation.1 | async-start | bytes 1720320 | tf_op jit(solution)/shard_map/psum | solution.py:757
  373.4 22.1 %collective-permute-start.45 = (bf16[2,336,640]{2,1,0:T(8,128)(2,1)S(1)}, bf16[2,336,640]{2,1,0:T(8,128)(2,1)S(1)}, u32[]{:S(2)}, u32[]{:S(2)}) collective-permute-start(bf16[2,336,640]{2,1,0:T(8,128)(2,1)S(1)} %get-tuple-element.306), channel_id=1, source_target_pairs={{0,16},{16,0},{1,17},{17,1},{2,18},{18,2},{3,19},{19,3},{4,20},{20... | collective-permute-start | bytes 2580488 | tf_op jit(solution)/shard_map/ppermute | solution.py:19
  376.4 31.7 %collective-permute-start.49 = (bf16[512,640]{1,0:T(8,128)(2,1)S(1)}, bf16[512,640]{1,0:T(8,128)(2,1)S(1)}, u32[]{:S(2)}, u32[]{:S(2)}) collective-permute-start(bf16[512,640]{1,0:T(8,128)(2,1)S(1)} %copy-done.31), channel_id=1, source_target_pairs={{0,16},{1,17},{2,18},{3,19},{4,20},{5,21},{6,22},{7,23},{8,24},{9,... | collective-permute-start | bytes 1966088 | tf_op jit(solution)/shard_map/ppermute | solution.py:751
  379.4 41.5 %collective-permute-start.48 = (bf16[512,640]{1,0:T(8,128)(2,1)S(1)}, bf16[512,640]{1,0:T(8,128)(2,1)S(1)}, u32[]{:S(2)}, u32[]{:S(2)}) collective-permute-start(bf16[512,640]{1,0:T(8,128)(2,1)S(1)} %broadcast_select_fusion.15), channel_id=1, source_target_pairs={{0,16},{16,0},{1,17},{17,1},{2,18},{18,2},{3,19},{19,3},{4,20},{20... | collective-permute-start | bytes 1966088 | tf_op jit(solution)/shard_map/ppermute | solution.py:19
  395.7 26.0 %collective-permute-start.47 = (bf16[336,640]{1,0:T(8,128)(2,1)S(1)}, bf16[336,640]{1,0:T(8,128)(2,1)S(1)}, u32[]{:S(2)}, u32[]{:S(2)}) collective-permute-start(bf16[336,640]{1,0:T(8,128)(2,1)S(1)} %slice_bitcast_fusion.3), channel_id=1, source_target_pairs={{0,4},{4,0},{1,5},{5,1},{2,6},{6,2},{3,7},{7,3},{8,12},{12,8},{9,1... | collective-permute-start | bytes 1290248 | tf_op jit(solution)/shard_map/ppermute | solution.py:19
  458.5 47.2 %collective-permute-start.50 = (bf16[768,640]{1,0:T(8,128)(2,1)}, bf16[768,640]{1,0:T(8,128)(2,1)}, u32[]{:S(2)}, u32[]{:S(2)}) collective-permute-start(bf16[768,640]{1,0:T(8,128)(2,1)} %broadcast_select_fusion.7), channel_id=1, source_target_pairs={{0,16},{16,0},{1,17},{17,1},{2,18},{18,2},{3,19},{19,3},{4,20},{20... | collective-permute-start | bytes 2949128 | tf_op jit(solution)/shard_map/ppermute | solution.py:19
  (121 other events, 1099.6 us)
Sparse Core Ops, SparseCore 0:
  372.8 82.9 all-reduce.4
  461.1 44.5 all-reduce.6

commit v5 on v4

--- a/solution.py
+++ b/solution.py
@@ -153,10 +153,12 @@
                 (kernel_out, gate_1_beside, ups[1], downs[1])
             )
             rows_before = from_before(kernel_out)
-            gate_pairs = over_gx(gate_1, gate_1_here)
             down_pairs = down_1, swap(down_1, "gx")
             query_pairs, out_pairs = over_gx(later[0], arrived[0]), over_gx(later[1], arrived[1])
-            rows_before, up_1 = barrier((rows_before, up_1))
+            gate_pairs = over_gx(gate_1, gate_1_here)
+            rows_before, up_1, gate_pairs, down_pairs, query_pairs, out_pairs = barrier(
+                (rows_before, up_1, gate_pairs, down_pairs, query_pairs, out_pairs)
+            )
             layer = {
                 "query": query_pairs,
                 "out": out_pairs,
@@ -405,9 +407,19 @@
     )(*ops)
 
 
+def put_pair(step, near, far, value):
+    @pl.when(step < 2)
+    def _():
+        near[0] = value
+
+    @pl.when(step >= 2)
+    def _():
+        far[0] = value
+
+
 def attn_back_kernel(
     d_hidden, q, mixed, kv, wo_a, wo_b, cos, sin, seg_q, seg_k,
-    d_out, d_q, d_kv, bias, wo, grad,
+    near, far, d_q, sent, own, bias, wo, grad, d_kv,
 ):
     j = pl.program_id(0)
     rows = grad.shape[0]
@@ -420,9 +432,10 @@
         put_bias(seg_q, seg_k, bias)
 
     take(j, wo_a, wo_b, wo)
-    d_out[0] = t_mm(mixed[0], grad[...]).astype(BF16)
+    put_pair(j, near, far, t_mm(mixed[0], grad[...]).astype(BF16))
     for at in range(0, rows, BLOCK):
         here = pl.ds(at, BLOCK)
+        place = pl.ds(before + at, BLOCK)
         keys = pl.ds(at, before + BLOCK)
         q_here = q[0, here, :]
         d_mixed = mm_t(grad[here, :], wo[...]).astype(BF16)
@@ -430,43 +443,55 @@
         d_probs = mm_t(d_mixed, kv[keys, HD:])
         inner = jnp.sum(probs * d_probs, axis=-1, keepdims=True)
         d_scores = (probs * (d_probs - inner)).astype(BF16)
-        back = unrotate(mm(d_scores, kv[keys, :HD]), cos[here, :], sin[here, :]) * HD**-0.5
+        back = unrotate(mm(d_scores, kv[keys, :HD]), cos[place, :], sin[place, :]) * HD**-0.5
         d_q[0, here, :] = back.astype(BF16)
         d_kv[keys, :HD] += t_mm(d_scores, q_here)
         d_kv[keys, HD:] += t_mm(probs.astype(BF16), d_mixed)
 
+    @pl.when(j == STEPS - 1)
+    def _():
+        sent[...] = d_kv[:before, :].astype(BF16)
+        own[...] = d_kv[before:, :]
+
 
 def attn_back(d_hidden, q, mixed, kv, w, place):
-    cos, sin, seg_q, seg_k = place
     rows, width = d_hidden.shape
     total = kv.shape[0]
-    cos, sin = cos[total - rows :], sin[total - rows :]
-    ops = (d_hidden, q, mixed, kv, *w["out"], cos, sin, seg_q, seg_k)
+    ops = (d_hidden, q, mixed, kv, *w["out"], *place)
     pairs = {1: step_of, 2: step_of, 4: first_of, 5: last_of}
-    outs = (STEPS, HD, width)
+    outs = (2, HD, width)
     return pl.pallas_call(
         attn_back_kernel,
         out_shape=(
             jax.ShapeDtypeStruct(outs, BF16),
+            jax.ShapeDtypeStruct(outs, BF16),
             jax.ShapeDtypeStruct(q.shape, BF16),
-            jax.ShapeDtypeStruct((total, 2 * HD), F32),
+            jax.ShapeDtypeStruct((total - rows, 2 * HD), BF16),
+            jax.ShapeDtypeStruct((rows, 2 * HD), F32),
         ),
         in_specs=[pairs.get(i, all_of)(op.shape) for i, op in enumerate(ops)],
-        out_specs=(step_of(outs), step_of(q.shape), all_of((total, 2 * HD))),
+        out_specs=(
+            first_of(outs),
+            last_of(outs),
+            step_of(q.shape),
+            all_of((total - rows, 2 * HD)),
+            all_of((rows, 2 * HD)),
+        ),
         scratch_shapes=[
             pltpu.VMEM((rows, total), F32),
             pltpu.VMEM((HD, width), BF16),
             pltpu.VMEM((rows, width), BF16),
+            pltpu.VMEM((total, 2 * HD), F32),
         ],
         cost_estimate=SMALL,
         **PARAMS,
     )(*ops)
 
 
-def query_back_kernel(d_q, normed, wq_a, wq_b, d_query, d_normed, wq):
+def query_back_kernel(d_q, normed, wq_a, wq_b, near, far, d_normed, wq):
     j = pl.program_id(0)
     take(j, wq_a, wq_b, wq)
-    d_query[0] = t_mm(d_q[0], normed[...]).astype(BF16)
+    put_pair(j, near, far, t_mm(d_q[0], normed[...]).astype(BF16))
     term = mm_t(d_q[0], wq[...])
 
     @pl.when(j == 0)
@@ -481,13 +506,17 @@
 def query_back(d_q, normed, w):
     rows, width = normed.shape
     ops = (d_q, normed, *w["query"])
-    outs = (STEPS, HD, width)
+    outs = (2, HD, width)
     pairs = {0: step_of, 2: first_of, 3: last_of}
     return pl.pallas_call(
         query_back_kernel,
-        out_shape=(jax.ShapeDtypeStruct(outs, BF16), jax.ShapeDtypeStruct((rows, width), F32)),
+        out_shape=(
+            jax.ShapeDtypeStruct(outs, BF16),
+            jax.ShapeDtypeStruct(outs, BF16),
+            jax.ShapeDtypeStruct((rows, width), F32),
+        ),
         in_specs=[pairs.get(i, all_of)(op.shape) for i, op in enumerate(ops)],
-        out_specs=(step_of(outs), all_of((rows, width))),
+        out_specs=(first_of(outs), last_of(outs), all_of((rows, width))),
         scratch_shapes=[pltpu.VMEM((width, HD), BF16)],
         cost_estimate=SMALL,
         **PARAMS,
@@ -497,8 +526,9 @@
 def input_back_kernel(
     d_kv, behind, normed, wk, wv, d_normed, x_ref, gain, d_hidden, cos, sin, d_x, d_shared, d_gain
 ):
+    before = cos.shape[0] - normed.shape[0]
     total = d_kv[...] + behind[...].astype(F32)
-    d_k = unrotate(total[:, :HD], cos[...], sin[...]).astype(BF16)
+    d_k = unrotate(total[:, :HD], cos[before:, :], sin[before:, :]).astype(BF16)
     d_v = total[:, HD:].astype(BF16)
     d_shared[:HD, :] = t_mm(d_k, normed[...]).astype(BF16)
     d_shared[HD:, :] = t_mm(d_v, normed[...]).astype(BF16)
@@ -511,10 +541,8 @@
 def input_back(d_kv, behind, normed, d_normed, x, d_hidden, w, place):
     cos, sin = place[:2]
     rows, width = normed.shape
-    before = cos.shape[0] - rows
     ops = (
-        d_kv[before:], behind, normed, w["key"], w["value"], d_normed, x, w["gain_attn"], d_hidden,
-        cos[before:], sin[before:],
+        d_kv, behind, normed, w["key"], w["value"], d_normed, x, w["gain_attn"], d_hidden, cos, sin,
     )
     return pl.pallas_call(
         input_back_kernel,
@@ -528,15 +556,19 @@
     )(*ops)
 
 
-def pack_attn(d_query, d_out, d_shared, d_gain_attn, d_gain_ff, order):
+def pack_shared(d_shared, d_gain_attn, d_gain_ff, order):
     gains = jnp.concatenate([d_gain_attn, d_gain_ff])
     gains = jnp.pad(gains, ((0, GAIN_ROWS - 2), (0, 0))).astype(BF16)
     count = d_shared.shape[0] // STEPS
     pieces = []
     for j in range(STEPS):
         quarter = lax.dynamic_slice_in_dim(d_shared, (order ^ j) * count, count, 0)
-        pieces.append(jnp.concatenate([d_query[j], d_out[j], quarter, gains]))
+        pieces.append(jnp.concatenate([quarter, gains]))
     return jnp.stack(pieces[:2]), jnp.stack(pieces[2:])
+
+
+def over_cores(near, got):
+    return jnp.concatenate([a + b for a, b in zip(near, got)], axis=1)
 
 
 def finish_part(scale, source, at, size):
@@ -561,11 +593,13 @@
     part = functools.partial(finish_part, scale)
 
     def put(core, low, high):
-        at = core * units
-        gate[:, at : at + units // 2] = part(low, 0, units // 2).T
-        gate[:, at + units // 2 : at + units] = part(high, 0, units // 2).T
-        up[:, at : at + units] = part(low, units // 2, units).T
-        down[at : at + units, :] = part(high, units // 2, units)
+        at, step = core * units, units // 4
+        gate[:, at : at + 3 * step] = part(low, 0, 3 * step).T
+        gate[:, at + 3 * step : at + units] = part(high, 0, step).T
+        up[:, at : at + 2 * step] = part(high, step, 2 * step).T
+        up[:, at + 2 * step : at + units] = part(low, 3 * step, 2 * step).T
+        down[at : at + step, :] = part(low, 5 * step, step)
+        down[at + step : at + units, :] = part(high, 3 * step, 3 * step)
 
     for_core(core, put, refs[:2], refs[2:4])
 
@@ -617,8 +651,16 @@
     return pick(section == 0, low, high), pick(section == 0, high, low)
 
 
-def to_owner(value, layer):
-    return lax.ppermute(value, "section", [(1 - layer, layer)])
+def shifted(value, axis, steps):
+    count = lax.axis_size(axis)
+    return lax.ppermute(value, axis, [(i, (i + steps) % count) for i in range(count)])
+
+
+def share(value, axis, steps):
+    count = lax.axis_size(axis)
+    rows = value.shape[0] // count
+    place = lax.rem(lax.axis_index(axis) + steps, count)
+    return lax.dynamic_slice_in_dim(value, place * rows, rows, 0)
 
 
 def local(
@@ -668,14 +710,19 @@
     out_all = jnp.concatenate([rows_before, out_0])
     slot = lambda *values: lax.optimization_barrier(values)
     q_1, mixed_1, kv_1, normed_1, hidden_1 = attn_forward(out_all, second, place)
-    out_0_other = lax.ppermute(out_0, "section", [(1, 0)])
-    hidden_1, out_0_other, up_1 = slot(hidden_1, out_0_other, second["up"])
+    hidden_1, up_1 = slot(hidden_1, second["up"])
     up_1 = jnp.stack(up_1)
     second.update(up=(up_1, swap(up_1, "gx")))
 
+    def by_micro(own, other):
+        first = section == 0
+        return jnp.stack([jnp.where(first, own, other), jnp.where(first, other, own)])[
+            None, :, None
+        ]
+
     order = 2 * gx + gy
     dy = jnp.where(valid[WINDOW:, None], mine(cotangent), 0)
-    turn = w_gate.shape[2] // 2
+    turn = 3 * w_gate.shape[2] // 4
 
     def ffn_parts(near, got):
         a_near, a_far = (near[i, :turn] + got[i, :turn] for i in range(2))
@@ -691,95 +738,110 @@
     a_got = swap(a_far, "gy")
     b_got = swap(b_send, "section")
     out_1 = ffn_forward(hidden_1, second)
-    d_out, d_q, d_kv = attn_back(d_hidden, q_1, mixed_1, kv_1, second, place)
-    d_q, d_kv, out_1, a_got, b_got = slot(d_q, d_kv, out_1, a_got, b_got)
-    sent = d_kv[:WINDOW].astype(BF16)
+    out_near, out_far, d_q, sent, d_kv = attn_back(
+        d_hidden, q_1, mixed_1, kv_1, second, place
+    )
+    d_q, sent, out_1, a_got, b_got = slot(d_q, sent, out_1, a_got, b_got)
     a_keep, a_send = halves(a_near + a_got, section, 0)
     b = b_keep + b_got
     behind = to_before(sent)
     a_got = swap(a_send, "section")
-    d_query, d_normed = query_back(d_q, normed_1, second)
+    query_near, query_far, d_normed = query_back(d_q, normed_1, second)
+    query_got, out_got = swap(query_far, "gx"), swap(out_far, "gx")
     d_normed, behind, b, a_got = slot(d_normed, behind, b, a_got)
     b_far = swap(b[1], "gy")
     grad_1, d_shared, gain_attn_grad = input_back(
         d_kv, behind, normed_1, d_normed, out_0, d_hidden, second, place
     )
-    near, far = pack_attn(d_query, d_out, d_shared, gain_attn_grad, gain_ff, order)
-    got = swap(far, "gx")
+    near, far = pack_shared(d_shared, gain_attn_grad, gain_ff, order)
+    near, got = (query_near, out_near, near), (query_got, out_got, swap(far, "gx"))
     grad_1, near, got = slot(grad_1, near, got)
 
-    c_keep_1, c_send_1 = halves(near + got, section, 1)
+    c_keep_1, c_send_1 = halves(over_cores(near, got), section, 1)
     c_send_a, c_send_b = c_send_1[0], c_send_1[1]
     c_got_a = swap(c_send_a, "section")
     far, before = ffn_back(grad_1, hidden_0, first, 1)
     before, far, b_far, c_got_a = slot(before, far, b_far, c_got_a)
     ffn_1 = jnp.concatenate([a_keep + a_got, b[0] + b_far])
+    direct = lax.axis_size("dp") == 4
+    terms = [share(ffn_1, "dp", steps) for steps in range(4)] if direct else []
+    some = [shifted(terms[steps], "dp", steps) for steps in (1, 3)] if direct else []
     got = swap(far, "gx")
     c_got_b = swap(c_send_b, "section")
     near, d_hidden, gain_ff = ffn_back(grad_1, hidden_0, first, 0, before)
-    near, d_hidden, gain_ff, got, c_got_b = slot(near, d_hidden, gain_ff, got, c_got_b)
+    near, d_hidden, gain_ff, got, c_got_b, some, terms = slot(
+        near, d_hidden, gain_ff, got, c_got_b, some, terms
+    )
+    some += [shifted(terms[2], "dp", 2)] if direct else []
     a_near, a_far, b = ffn_parts(near, got)
     b_keep, b_send = halves(b, section, 1)
     b_got = swap(b_send, "section")
     a_got = swap(a_far, "gy")
-    d_out, d_q, d_kv = attn_back(d_hidden, q_0, mixed_0, kv_0, first, place)
+    out_near, out_far, d_q, sent, d_kv = attn_back(
+        d_hidden, q_0, mixed_0, kv_0, first, place
+    )
     c_1 = [c_keep_1[0] + c_got_a, c_keep_1[1] + c_got_b]
-    d_q, d_kv, a_got = slot(d_q, d_kv, a_got)
-    sent = d_kv[:WINDOW].astype(BF16)
-    a_keep, a_send = halves(a_near + a_got, section, 0)
+    d_q, sent, some = slot(d_q, sent, some)
+    if direct:
+        mine_1 = sum((value.astype(F32) for value in some), terms[0].astype(F32)).astype(BF16)
+        some = [mine_1, shifted(mine_1, "dp", 1)]
     behind = to_before(sent)
-    a_got = swap(a_send, "section")
-    d_query, d_normed = query_back(d_q, normed_0, first)
-    d_normed, behind, b_got, a_got = slot(d_normed, behind, b_got, a_got)
+    query_near, query_far, d_normed = query_back(d_q, normed_0, first)
+    query_got, out_got = swap(query_far, "gx"), swap(out_far, "gx")
+    d_normed, behind, b_got, a_got, some = slot(d_normed, behind, b_got, a_got, some)
     b = b_keep + b_got
     b_far = swap(b[1], "gy")
+    a_keep, a_send = halves(a_near + a_got, section, 0)
+    a_got = swap(a_send, "section")
+    some += [shifted(some[0], "dp", steps) for steps in (2, 3)] if direct else []
     grad_0, d_shared, gain_attn_grad = input_back(
         d_kv, behind, normed_0, d_normed, x, d_hidden, first, place
     )
-    near, far = pack_attn(d_query, d_out, d_shared, gain_attn_grad, gain_ff, order)
-    got = swap(far, "gx")
-    near, got, b_far = slot(near, got, b_far)
-    count = ffn_1.shape[0]
-    ffn = lax.psum(jnp.concatenate([ffn_1, a_keep + a_got, b[0] + b_far]), "dp")
-    c_keep, c_send = halves(near + got, section, 1)
+    grad_0, d_shared, a_got, b_far, some = slot(grad_0, d_shared, a_got, b_far, some)
+    ffn_0 = jnp.concatenate([a_keep + a_got, b[0] + b_far])
+    if direct:
+        ffn_0 = lax.psum(ffn_0, "dp")
+        found = jnp.stack(some)
+        place = lax.axis_index("dp")
+        ffn_1 = jnp.concatenate(
+            [
+                lax.dynamic_index_in_dim(found, lax.rem(place + 4 - i, 4), 0, keepdims=False)
+                for i in range(4)
+            ]
+        )
+    else:
+        ffn_1, ffn_0 = lax.psum((ffn_1, ffn_0), "dp")
+    near, far = pack_shared(d_shared, gain_attn_grad, gain_ff, order)
+    near, got = (query_near, out_near, near), (query_got, out_got, swap(far, "gx"))
+    c_keep, c_send = halves(over_cores(near, got), section, 1)
     c_got = swap(c_send, "section")
     c_far_1 = swap(c_1[1], "gy")
-    c_keep, c_got, c_far_1 = slot(c_keep, c_got, c_far_1)
+    c_keep, c_got, c_far_1, grad_0 = slot(c_keep, c_got, c_far_1, grad_0)
     c = c_keep + c_got
     c_far = swap(c[1], "gy")
-    grad_other = swap(pick(section == 0, grad_1, grad_0), "section")
-    out_1_other = lax.ppermute(out_1, "section", [(0, 1)])
-    ffn, c_far, grad_other, out_1_other = slot(ffn, c_far, grad_other, out_1_other)
+    first_rows, second_rows = (jnp.concatenate(rows) for rows in ((out_0, grad_0), (out_1, grad_1)))
+    others = swap(pick(section == 0, second_rows, first_rows), "section")
+    ffn_0, ffn_1, c_far = slot(ffn_0, ffn_1, c_far)
     attn = jnp.concatenate([c_1[0] + c_far_1, c[0] + c_far])
-    half = ffn.shape[0] // 2
-    sent = pick(section == 0, ffn[:half], ffn[half:])
+    sent = pick(section == 0, ffn_1, ffn_0)
     ffn_got = swap(sent, "section")
     attn = lax.psum(attn, "dp")
-    attn, ffn_got = slot(attn, ffn_got)
-
-    def two_halves(both, got):
-        half = both.shape[0] // 2
-        mine = pick(section == 0, both[half:], both[:half])
+    attn, ffn_got, others = slot(attn, ffn_got, others)
+
+    def two_halves(one, zero, got):
+        mine = pick(section == 0, zero, one)
         return pick(section == 0, mine, got), pick(section == 0, got, mine)
 
     half = attn.shape[0] // 2
     attn_got = swap(pick(section == 0, attn[:half], attn[half:]), "section")
-    ffn_mine = two_halves(ffn, ffn_got)
+    ffn_mine = two_halves(ffn_1, ffn_0, ffn_got)
     gate, up, down = finish_ffn(
         ffn_mine, [swap(value, "gx") for value in ffn_mine], gx, scale, w_gate.shape[2]
     )
-    states, in_grads = pick(section == 0, out_0, out_1), pick(section == 0, grad_0, grad_1)
-    other_states = pick(section == 0, out_0_other, out_1_other)
-
-    def by_micro(own, other):
-        first = section == 0
-        return jnp.stack([jnp.where(first, own, other), jnp.where(first, other, own)])[
-            None, :, None
-        ]
-
-    states, in_grads = by_micro(states, other_states), by_micro(in_grads, grad_other)
+    states = by_micro(pick(section == 0, out_0, out_1), others[:own_rows])
+    in_grads = by_micro(pick(section == 0, grad_0, grad_1), others[own_rows:])
     attn_got, gate, up, down, states, in_grads = slot(attn_got, gate, up, down, states, in_grads)
-    attn_low, high = two_halves(attn, attn_got)
+    attn_low, high = two_halves(attn[:half], attn[half:], attn_got)
     attn_others = swap(attn_low, "gx"), swap(high, "gx")
     count = d_shared.shape[0] // STEPS
     quarter = high[-GAIN_ROWS - count : -GAIN_ROWS]

time: 553 us -> 513 us (0.928)
  waiting for transfers between devices: 203 us -> 161 us
  local copies, waits for them, and re-layouts: 38.1 us -> 27.7 us
  starting transfers between devices: 55 us -> 63 us
    ppermute x52 -> x56, waiting for transfers between devices: 99.3 us -> 67.4 us  [swap(): return lax.ppermute(value, axis, [(0, 1), (1, 0)])]
    psum x1, waiting for transfers between devices: 34.1 us -> 22.6 us  [local(): ffn_0 = lax.psum(ffn_0, 'dp')]
    slice x6 -> x0, local copies, waits for them, and re-layouts: 8.85 us -> none  [the longest x2 4.4 us: local(): sent = d_kv[:WINDOW].astype(BF16)]
    another operation x11, other arithmetic: 9.96 us -> 3.41 us  [the longest x5 1.71 us: pack_shared(): return (jnp.stack(pieces[:2]), jnp.stack(pieces[2:]))]
    ppermute x52 -> x56, starting transfers between devices: 41.3 us -> 45.8 us  [swap(): return lax.ppermute(value, axis, [(0, 1), (1, 0)])]
    unnamed x170 -> x156, local copies, waits for them, and re-layouts: 12.1 us -> 11.5 us
    select_n x21 -> x20, other arithmetic: 19.6 us -> 19.8 us  [pick(): return jnp.where(flag, a, b)]
  transfers between devices with their start and end apart: 60 -> 68, of which waited for: 24 -> 25; matrix products, arithmetic and copies ran while one was open for 13% -> 14% of each run, Pallas kernels for 25% -> 30%
where the time goes in v5:
time: 513 us; the launch traced here: 503 us
  Pallas kernels  165 us (32%)
  waiting for transfers between devices  161 us (31%)
  other arithmetic  70.5 us (14%)
  starting transfers between devices  63 us (12%)
  local copies, waits for them, and re-layouts  27.7 us (5%)
  between operations  15.6 us (3%)
    ppermute x56, waiting for transfers between devices, swap(): return lax.ppermute(value, axis, [(0, 1), (1, 0)])  67.4 us
    pallas_call x4, Pallas kernels, ffn_back(): pl.pallas_call(functools.partial(ffn_back_kernel, last), grid=(2,), out_s...  49.5 us
    ppermute x56, starting transfers between devices, swap(): return lax.ppermute(value, axis, [(0, 1), (1, 0)])  45.8 us
    psum x1, waiting for transfers between devices, local(): attn = lax.psum(attn, 'dp')  45 us
    pallas_call x2, Pallas kernels, attn_back(): pl.pallas_call(attn_back_kernel, out_shape=(jax.ShapeDtypeStruct(outs, BF...  31 us
    pallas_call x2, Pallas kernels, attn_forward(): pl.pallas_call(attn_kernel, out_shape=(jax.ShapeDtypeStruct(heads, BF16),...  28.8 us
    psum x1, waiting for transfers between devices, local(): ffn_0 = lax.psum(ffn_0, 'dp')  22.6 us
    pallas_call x2, Pallas kernels, ffn_forward(): pl.pallas_call(ffn_kernel, out_shape=jax.ShapeDtypeStruct((rows, width),...  20.1 us
  transfers between devices with their start and end apart: 68, of which 25 were waited for; matrix products, arithmetic and copies ran while one was open for 14% of the time, Pallas kernels for 30%

profile of v5, /device:TPU:0, one launch (start us, length us, event | category | flops | bytes accessed | tf_op | source)
XLA Modules:
  0.0 503.2 jit_solution(1518006306539657582)
XLA Ops:
  26.8 8.2 %collective-permute-done = bf16[640,512]{1,0:T(8,128)(2,1)} collective-permute-done((bf16[640,512]{1,0:T(8,128)(2,1)}, bf16[640,512]{1,0:T(8,128)(2,1)}, u32[]{:S(2)}, u32[]{:S(2)}) %collective-permute-start) | collective-permute-done | bytes 655392 | tf_op jit(solution)/shard_map/ppermute | solution.py:19
  51.4 4.9 collective-permute-done.5
  60.9 8.8 %collective-permute-done.8 = bf16[640,512]{1,0:T(8,128)(2,1)S(1)} collective-permute-done((bf16[640,512]{1,0:T(8,128)(2,1)}, bf16[640,512]{1,0:T(8,128)(2,1)S(1)}, u32[]{:S(2)}, u32[]{:S(2)}) %collective-permute-start.8) | collective-permute-done | bytes 655392 | tf_op jit(solution)/shard_map/ppermute | solution.py:19
  80.4 14.1 %shard_map.203 = (bf16[4,512,256]{2,1,0:T(8,128)(2,1)}, bf16[4,512,256]{2,1,0:T(8,128)(2,1)}, bf16[1024,512]{1,0:T(8,128)(2,1)}, bf16[512,640]{1,0:T(8,128)(2,1)}, f32[512,640]{1,0:T(8,128)}) custom-call(bf16[1024,640]{1,0:T(8,128)(2,1)} %pad_maximum_fusion.x_ref, f32[1,640]{1,0:T(1,128)} %get-tuple-element.427.gain, bf16[2,640,256]{2,1,0:T(8,128)(2,1)} %copy-done.14, ...), custom_call_target="tpu_custom_call" | custom-call | flops 1000 | bytes 1000 | tf_op jit(solution)/shard_map/pallas_call | solution.py:281
  98.4 5.1 %collective-permute-done.14 = bf16[640,256]{1,0:T(8,128)(2,1)S(1)} collective-permute-done((bf16[640,256]{1,0:T(8,128)(2,1)}, bf16[640,256]{1,0:T(8,128)(2,1)S(1)}, u32[]{:S(2)}, u32[]{:S(2)}) %collective-permute-start.14) | collective-permute-done | bytes 327712 | tf_op jit(solution)/shard_map/ppermute | solution.py:19
  113.3 10.0 %shard_map.204.x_ref = bf16[512,640]{1,0:T(8,128)(2,1)} custom-call(f32[512,640]{1,0:T(8,128)} %get-tuple-element.179.hidden, f32[1,640]{1,0:T(1,128)} %get-tuple-element.426.gain, bf16[2,640,512]{2,1,0:T(8,128)(2,1)} %copy-done.5, bf16[2,640,512]{2,1,0:T(8,128)(2,1)} %copy-done.18, bf16[2,640,512]{2,1,0:T(8,128)(2,1)} %copy-done.4, ...), custom_call_target="tpu_custom_call" | custom-call | flops 1000 | bytes 1000 | tf_op jit(solution)/shard_map/pallas_call | solution.py:338
  133.4 11.7 %collective-permute-done.21 = bf16[512,640]{1,0:T(8,128)(2,1)S(1)} collective-permute-done((bf16[512,640]{1,0:T(8,128)(2,1)S(1)}, bf16[512,640]{1,0:T(8,128)(2,1)S(1)}, u32[]{:S(2)}, u32[]{:S(2)}) %collective-permute-start.21) | collective-permute-done | bytes 655392 | tf_op jit(solution)/shard_map/ppermute | solution.py:179
  150.4 14.6 %shard_map.205 = (bf16[4,512,256]{2,1,0:T(8,128)(2,1)}, bf16[4,512,256]{2,1,0:T(8,128)(2,1)}, bf16[1024,512]{1,0:T(8,128)(2,1)}, bf16[512,640]{1,0:T(8,128)(2,1)}, f32[512,640]{1,0:T(8,128)}) custom-call(bf16[1024,640]{1,0:T(8,128)(2,1)} %pad_maximum_fusion.5.x_ref, f32[1,640]{1,0:T(1,128)} %get-tuple-element.425.gain, bf16[2,640,256]{2,1,0:T(8,128)(2,1)} %copy-done.15, ...), custom_call_target="tpu_custom_call" | custom-call | flops 1000 | bytes 1000 | tf_op jit(solution)/shard_map/pallas_call | solution.py:281
  169.4 11.8 %shard_map.206 = (bf16[2,1536,640]{2,1,0:T(8,128)(2,1)}, f32[512,640]{1,0:T(8,128)}) custom-call(bf16[512,640]{1,0:T(8,128)(2,1)} %bitcast_select_fusion.dy, f32[512,640]{1,0:T(8,128)} %get-tuple-element.199.hidden, f32[1,640]{1,0:T(1,128)} %get-tuple-element.424.gain, f32[8,128]{1,0:T(8,128)} %broadcast_2_before.2.before, bf16[2,640,512]{2,1,0:T(8,128)(2,1)} %copy-done.20, ...), custom_call_target="tpu_custom_call" | custom-call | flops 1000 | bytes 1000 | tf_op jit(solution)/shard_map/pallas_call | solution.py:395
  181.4 12.9 %shard_map.207 = (bf16[2,1536,640]{2,1,0:T(8,128)(2,1)}, f32[512,640]{1,0:T(8,128)}, f32[1,640]{1,0:T(1,128)}) custom-call(bf16[512,640]{1,0:T(8,128)(2,1)} %bitcast_select_fusion.dy, f32[512,640]{1,0:T(8,128)} %get-tuple-element.199.hidden, f32[1,640]{1,0:T(1,128)} %get-tuple-element.424.gain, f32[512,640]{1,0:T(8,128)} %get-tuple-element.206.before, ...), custom_call_target="tpu_custom_call" | custom-call | flops 1000 | bytes 1000 | tf_op jit(solution)/shard_map/pallas_call | solution.py:395
  199.8 10.0 %shard_map.209 = bf16[512,640]{1,0:T(8,128)(2,1)} custom-call(f32[512,640]{1,0:T(8,128)} %get-tuple-element.199.hidden, f32[1,640]{1,0:T(1,128)} %get-tuple-element.424.gain, bf16[2,640,512]{2,1,0:T(8,128)(2,1)} %copy-done.8, bf16[2,640,512]{2,1,0:T(8,128)(2,1)} %copy-done.20, bf16[2,640,512]{2,1,0:T(8,128)(2,1)} %copy-done.9, ...), custom_call_target="tpu_custom_call" | custom-call | flops 1000 | bytes 1000 | tf_op jit(solution)/shard_map/pallas_call | solution.py:338
  209.8 15.5 %shard_map.208 = (bf16[2,256,640]{2,1,0:T(8,128)(2,1)}, bf16[2,256,640]{2,1,0:T(8,128)(2,1)}, bf16[4,512,256]{2,1,0:T(8,128)(2,1)}, bf16[512,512]{1,0:T(8,128)(2,1)}, f32[512,512]{1,0:T(8,128)}) custom-call(f32[512,640]{1,0:T(8,128)} %get-tuple-element.213.d_hidden, bf16[4,512,256]{2,1,0:T(8,128)(2,1)} %get-tuple-element.214.q, ...), custom_call_target="tpu_custom_call" | custom-call | flops 1000 | bytes 1000 | tf_op jit(solution)/shard_map/pallas_call | solution.py:463
  232.4 7.2 %shard_map.210 = (bf16[2,256,640]{2,1,0:T(8,128)(2,1)}, bf16[2,256,640]{2,1,0:T(8,128)(2,1)}, f32[512,640]{1,0:T(8,128)}) custom-call(bf16[4,512,256]{2,1,0:T(8,128)(2,1)} %get-tuple-element.222.d_q, bf16[512,640]{1,0:T(8,128)(2,1)} %get-tuple-element.223.normed, bf16[2,640,256]{2,1,0:T(8,128)(2,1)} %copy-done.15, bf16[2,640,256]{2,1,0:T(8,128)(2,1)} %copy-done.34), custom_call_target="tpu_custom_call" | custom-call | flops 1000 | bytes 1000 | tf_op jit(solution)/shard_map/pallas_call | solution.py:511
  243.1 5.3 %shard_map.211 = (bf16[512,640]{1,0:T(8,128)(2,1)}, bf16[512,640]{1,0:T(8,128)(2,1)}, f32[1,640]{1,0:T(1,128)}) custom-call(f32[512,512]{1,0:T(8,128)} %get-tuple-element.217.d_kv, bf16[512,512]{1,0:T(8,128)(2,1)} %collective-permute-done.31.behind, bf16[512,640]{1,0:T(8,128)(2,1)} %get-tuple-element.223.normed, bf16[640,256]{1,0:T(8,128)(2,1)} %get-tuple-element.193.wk, ...), custom_call_target="tpu_custom_call" | custom-call | flops 1000 | bytes 1000 | tf_op jit(solution)/shard_map/pallas_call | solution.py:547
  256.8 11.7 %shard_map.212 = (bf16[2,1536,640]{2,1,0:T(8,128)(2,1)}, f32[512,640]{1,0:T(8,128)}) custom-call(bf16[512,640]{1,0:T(8,128)(2,1)} %get-tuple-element.244.dy, f32[512,640]{1,0:T(8,128)} %get-tuple-element.179.hidden, f32[1,640]{1,0:T(1,128)} %get-tuple-element.426.gain, f32[8,128]{1,0:T(8,128)} %broadcast_2_before.2.before, bf16[2,640,512]{2,1,0:T(8,128)(2,1)} %copy-done.18, ...), custom_call_target="tpu_custom_call" | custom-call | flops 1000 | bytes 1000 | tf_op jit(solution)/shard_map/pallas_call | solution.py:395
  277.7 13.1 %shard_map.213 = (bf16[2,1536,640]{2,1,0:T(8,128)(2,1)}, f32[512,640]{1,0:T(8,128)}, f32[1,640]{1,0:T(1,128)}) custom-call(bf16[512,640]{1,0:T(8,128)(2,1)} %get-tuple-element.244.dy, f32[512,640]{1,0:T(8,128)} %get-tuple-element.179.hidden, f32[1,640]{1,0:T(1,128)} %get-tuple-element.426.gain, f32[512,640]{1,0:T(8,128)} %get-tuple-element.249.before, ...), custom_call_target="tpu_custom_call" | custom-call | flops 1000 | bytes 1000 | tf_op jit(solution)/shard_map/pallas_call | solution.py:395
  298.3 15.5 %shard_map.214 = (bf16[2,256,640]{2,1,0:T(8,128)(2,1)}, bf16[2,256,640]{2,1,0:T(8,128)(2,1)}, bf16[4,512,256]{2,1,0:T(8,128)(2,1)}, bf16[512,512]{1,0:T(8,128)(2,1)}, f32[512,512]{1,0:T(8,128)}) custom-call(f32[512,640]{1,0:T(8,128)} %get-tuple-element.256.d_hidden, bf16[4,512,256]{2,1,0:T(8,128)(2,1)} %get-tuple-element.257.q, ...), custom_call_target="tpu_custom_call" | custom-call | flops 1000 | bytes 1000 | tf_op jit(solution)/shard_map/pallas_call | solution.py:463
  316.9 7.2 %shard_map.215 = (bf16[2,256,640]{2,1,0:T(8,128)(2,1)}, bf16[2,256,640]{2,1,0:T(8,128)(2,1)}, f32[512,640]{1,0:T(8,128)}) custom-call(bf16[4,512,256]{2,1,0:T(8,128)(2,1)} %get-tuple-element.265.d_q, bf16[512,640]{1,0:T(8,128)(2,1)} %get-tuple-element.266.normed, bf16[2,640,256]{2,1,0:T(8,128)(2,1)} %copy-done.14, ...), custom_call_target="tpu_custom_call" | custom-call | flops 1000 | bytes 1000 | tf_op jit(solution)/shard_map/pallas_call | solution.py:511
  337.4 5.3 %shard_map.216 = (bf16[512,640]{1,0:T(8,128)(2,1)}, bf16[512,640]{1,0:T(8,128)(2,1)}, f32[1,640]{1,0:T(1,128)}) custom-call(f32[512,512]{1,0:T(8,128)} %get-tuple-element.271.d_kv, bf16[512,512]{1,0:T(8,128)(2,1)} %copy-done.58, bf16[512,640]{1,0:T(8,128)(2,1)} %get-tuple-element.266.normed, bf16[640,256]{1,0:T(8,128)(2,1)} %get-tuple-element.173.wk, ...), custom_call_target="tpu_custom_call" | custom-call | flops 1000 | bytes 1000 | tf_op jit(solution)/shard_map/pallas_call | solution.py:547
  344.0 7.7 %collective-permute-done.51 = bf16[192,640]{1,0:T(8,128)(2,1)S(1)} collective-permute-done((bf16[192,640]{1,0:T(8,128)(2,1)S(1)}, bf16[192,640]{1,0:T(8,128)(2,1)S(1)}, u32[]{:S(2)}, u32[]{:S(2)}) %collective-permute-start.51) | collective-permute-done | bytes 245792 | tf_op jit(solution)/shard_map/ppermute | solution.py:656
  369.5 15.5 %collective-permute-done.54 = bf16[2,336,640]{2,1,0:T(8,128)(2,1)} collective-permute-done((bf16[2,336,640]{2,1,0:T(8,128)(2,1)}, bf16[2,336,640]{2,1,0:T(8,128)(2,1)}, u32[]{:S(2)}, u32[]{:S(2)}) %collective-permute-start.54) | collective-permute-done | bytes 860192 | tf_op jit(solution)/shard_map/ppermute | solution.py:19
  392.3 22.6 %all-reduce.5.cloned.1.call-done = bf16[768,640]{1,0:T(8,128)(2,1)} async-done(((bf16[768,640]{1,0:T(8,128)(2,1)}), bf16[768,640]{1,0:T(8,128)(2,1)}) %all-reduce.5.cloned.1.call-update) | async-done | bytes 983056 | tf_op jit(solution)/shard_map/psum | solution.py:803
  420.8 45.0 %all-reduce.7.cloned.1.call-done = bf16[672,640]{1,0:T(8,128)(2,1)} async-done(((bf16[672,640]{1,0:T(8,128)(2,1)}), bf16[672,640]{1,0:T(8,128)(2,1)}) %all-reduce.7.cloned.1.call-update) | async-done | bytes 860176 | tf_op jit(solution)/shard_map/psum | solution.py:828
  474.8 6.9 %shard_map.217 = (f32[640,1024]{1,0:T(8,128)}, f32[640,1024]{1,0:T(8,128)}, f32[1024,640]{1,0:T(8,128)}) custom-call(s32[1]{0:T(128)} %bitcast.63.core, bf16[768,640]{1,0:T(8,128)(2,1)} %copy-done.24, bf16[768,640]{1,0:T(8,128)(2,1)} %copy-done.23, bf16[768,640]{1,0:T(8,128)(2,1)} %copy-done.45, bf16[768,640]{1,0:T(8,128)(2,1)} %copy-done.44), custom_call_target="tpu_custom_call" | custom-call | flops 1000 | bytes 1000 | tf_op jit(solution)/shard_map/pallas_call | solution.py:626
  (401 shorter events, 196.8 us)
Async XLA Ops:
  7.2 407.7 %all-reduce.5.cloned.1.call-start = ((), (), s32[]{:S(2)}) async-start(), calls=%async_computation | async-start | bytes 1966080 | tf_op jit(solution)/shard_map/psum | solution.py:803
  12.9 27.3 %collective-permute-start.9 = (bf16[512,640]{1,0:T(8,128)(2,1)}, bf16[512,640]{1,0:T(8,128)(2,1)}, u32[]{:S(2)}, u32[]{:S(2)}) collective-permute-start(bf16[512,640]{1,0:T(8,128)(2,1)} %fusion.30), channel_id=1, source_target_pairs={{0,4},{4,0},{1,5},{5,1},{2,6},{6,2},{3,7},{7,3},{8,12},{12,8},{9,1... | collective-permute-start | bytes 1966088 | tf_op jit(solution)/shard_map/ppermute | solution.py:19
  15.6 35.8 %collective-permute-start.4 = (bf16[512,640]{1,0:T(8,128)(2,1)S(1)}, bf16[512,640]{1,0:T(8,128)(2,1)}, u32[]{:S(2)}, u32[]{:S(2)}) collective-permute-start(bf16[512,640]{1,0:T(8,128)(2,1)S(1)} %dynamic-slice_bitcast_fusion.x_ref), channel_id=1, source_target_pairs={{0,4},{4,8},{8,12},{1,5},{5,9},{9,13},{2,6},{6,10},{10,14},{3,7},{... | collective-permute-start | bytes 1966088 | tf_op jit(solution)/shard_map/ppermute | solution.py:179
  40.2 29.4 %collective-permute-start.8 = (bf16[640,512]{1,0:T(8,128)(2,1)}, bf16[640,512]{1,0:T(8,128)(2,1)S(1)}, u32[]{:S(2)}, u32[]{:S(2)}) collective-permute-start(bf16[640,512]{1,0:T(8,128)(2,1)} %dynamic-slice_bitcast_fusion.2), channel_id=1, source_target_pairs={{0,16},{16,0},{1,17},{17,1},{2,18},{18,2},{3,19},{19,3},{4,20},{20... | collective-permute-start | bytes 1966088 | tf_op jit(solution)/shard_map/ppermute | solution.py:19
  50.9 22.5 %collective-permute-start.6 = (f32[2,640]{1,0:T(2,128)S(1)}, f32[2,640]{1,0:T(2,128)S(1)}, u32[]{:S(2)}, u32[]{:S(2)}) collective-permute-start(f32[2,640]{1,0:T(2,128)S(1)} %pad_maximum_fusion.33), channel_id=1, source_target_pairs={{0,16},{16,0},{1,17},{17,1},{2,18},{18,2},{3,19},{19,3},{4,20},{20... | collective-permute-start | bytes 15368 | tf_op jit(solution)/shard_map/ppermute | solution.py:19
  57.6 46.0 %collective-permute-start.13 = (bf16[640,512]{1,0:T(8,128)(2,1)}, bf16[640,512]{1,0:T(8,128)(2,1)}, u32[]{:S(2)}, u32[]{:S(2)}) collective-permute-start(bf16[640,512]{1,0:T(8,128)(2,1)} %get-tuple-element.373), channel_id=1, source_target_pairs={{0,4},{4,0},{1,5},{5,1},{2,6},{6,2},{3,7},{7,3},{8,12},{12,8},{9,1... | collective-permute-start | bytes 1966088 | tf_op jit(solution)/shard_map/ppermute | solution.py:19
  69.7 37.4 %collective-permute-start.18 = (bf16[2,512,640]{2,1,0:T(8,128)(2,1)S(1)}, bf16[2,512,640]{2,1,0:T(8,128)(2,1)}, u32[]{:S(2)}, u32[]{:S(2)}) collective-permute-start(bf16[2,512,640]{2,1,0:T(8,128)(2,1)S(1)} %pad_maximum_fusion.1), channel_id=1, source_target_pairs={{0,16},{16,0},{1,17},{17,1},{2,18},{18,2},{3,19},{19,3},{4,20},{20... | collective-permute-start | bytes 3932168 | tf_op jit(solution)/shard_map/ppermute | solution.py:19
  73.4 30.1 %collective-permute-start.12 = (bf16[640,512]{1,0:T(8,128)(2,1)}, bf16[640,512]{1,0:T(8,128)(2,1)}, u32[]{:S(2)}, u32[]{:S(2)}) collective-permute-start(bf16[640,512]{1,0:T(8,128)(2,1)} %get-tuple-element.375), channel_id=1, source_target_pairs={{0,4},{4,0},{1,5},{5,1},{2,6},{6,2},{3,7},{7,3},{8,12},{12,8},{9,1... | collective-permute-start | bytes 1966088 | tf_op jit(solution)/shard_map/ppermute | solution.py:19
  75.5 22.9 %collective-permute-start.15 = (bf16[256,640]{1,0:T(8,128)(2,1)}, bf16[256,640]{1,0:T(8,128)(2,1)S(1)}, u32[]{:S(2)}, u32[]{:S(2)}) collective-permute-start(bf16[256,640]{1,0:T(8,128)(2,1)} %get-tuple-element.400), channel_id=1, source_target_pairs={{0,4},{4,0},{1,5},{5,1},{2,6},{6,2},{3,7},{7,3},{8,12},{12,8},{9,1... | collective-permute-start | bytes 983048 | tf_op jit(solution)/shard_map/ppermute | solution.py:19
  77.1 26.4 %collective-permute-start.14 = (bf16[640,256]{1,0:T(8,128)(2,1)}, bf16[640,256]{1,0:T(8,128)(2,1)S(1)}, u32[]{:S(2)}, u32[]{:S(2)}) collective-permute-start(bf16[640,256]{1,0:T(8,128)(2,1)} %get-tuple-element.386), channel_id=1, source_target_pairs={{0,4},{4,0},{1,5},{5,1},{2,6},{6,2},{3,7},{7,3},{8,12},{12,8},{9,1... | collective-permute-start | bytes 983048 | tf_op jit(solution)/shard_map/ppermute | solution.py:19
  146.2 18.9 %collective-permute-start.26 = (bf16[640,512]{1,0:T(8,128)(2,1)S(1)}, bf16[640,512]{1,0:T(8,128)(2,1)S(1)}, u32[]{:S(2)}, u32[]{:S(2)}) collective-permute-start(bf16[640,512]{1,0:T(8,128)(2,1)S(1)} %copy-done.33), channel_id=1, source_target_pairs={{0,4},{4,0},{1,5},{5,1},{2,6},{6,2},{3,7},{7,3},{8,12},{12,8},{9,1... | collective-permute-start | bytes 1966088 | tf_op jit(solution)/shard_map/ppermute | solution.py:19
  197.4 27.9 %collective-permute-start.29 = (bf16[768,640]{1,0:T(8,128)(2,1)S(1)}, bf16[768,640]{1,0:T(8,128)(2,1)}, u32[]{:S(2)}, u32[]{:S(2)}) collective-permute-start(bf16[768,640]{1,0:T(8,128)(2,1)S(1)} %add_bitcast_fusion.1), channel_id=1, source_target_pairs={{0,4},{4,0},{1,5},{5,1},{2,6},{6,2},{3,7},{7,3},{8,12},{12,8},{9,1... | collective-permute-start | bytes 2949128 | tf_op jit(solution)/shard_map/ppermute | solution.py:19
  198.6 26.8 %collective-permute-start.30 = (bf16[2,384,640]{2,1,0:T(8,128)(2,1)}, bf16[2,384,640]{2,1,0:T(8,128)(2,1)}, u32[]{:S(2)}, u32[]{:S(2)}) collective-permute-start(bf16[2,384,640]{2,1,0:T(8,128)(2,1)} %broadcast_select_fusion.7), channel_id=1, source_target_pairs={{0,16},{16,0},{1,17},{17,1},{2,18},{18,2},{3,19},{19,3},{4,20},{20... | collective-permute-start | bytes 2949128 | tf_op jit(solution)/shard_map/ppermute | solution.py:19
  230.0 23.5 %collective-permute-start.34 = (bf16[2,256,640]{2,1,0:T(8,128)(2,1)}, bf16[2,256,640]{2,1,0:T(8,128)(2,1)S(1)}, u32[]{:S(2)}, u32[]{:S(2)}) collective-permute-start(bf16[2,256,640]{2,1,0:T(8,128)(2,1)} %get-tuple-element.237), channel_id=1, source_target_pairs={{0,8},{8,0},{1,9},{9,1},{2,10},{10,2},{3,11},{11,3},{4,12},{12,4},... | collective-permute-start | bytes 1966088 | tf_op jit(solution)/shard_map/ppermute | solution.py:19
  268.6 22.3 %collective-permute-start.38 = (bf16[2,1536,640]{2,1,0:T(8,128)(2,1)}, bf16[2,1536,640]{2,1,0:T(8,128)(2,1)}, u32[]{:S(2)}, u32[]{:S(2)}) collective-permute-start(bf16[2,1536,640]{2,1,0:T(8,128)(2,1)} %get-tuple-element.253), channel_id=1, source_target_pairs={{0,8},{8,0},{1,9},{9,1},{2,10},{10,2},{3,11},{11,3},{4,12},{12,4},... | collective-permute-start | bytes 11796488 | tf_op jit(solution)/shard_map/ppermute | solution.py:19
  269.9 20.9 %collective-permute-start.39 = (bf16[336,640]{1,0:T(8,128)(2,1)}, bf16[336,640]{1,0:T(8,128)(2,1)S(1)}, u32[]{:S(2)}, u32[]{:S(2)}) collective-permute-start(bf16[336,640]{1,0:T(8,128)(2,1)} %get-tuple-element.390), channel_id=1, source_target_pairs={{0,16},{16,0},{1,17},{17,1},{2,18},{18,2},{3,19},{19,3},{4,20},{20... | collective-permute-start | bytes 1290248 | tf_op jit(solution)/shard_map/ppermute | solution.py:19
  294.9 34.6 %collective-permute-start.47 = (bf16[768,640]{1,0:T(8,128)(2,1)S(1)}, bf16[768,640]{1,0:T(8,128)(2,1)S(1)}, u32[]{:S(2)}, u32[]{:S(2)}) collective-permute-start(bf16[768,640]{1,0:T(8,128)(2,1)S(1)} %add_bitcast_fusion), channel_id=1, source_target_pairs={{0,4},{4,0},{1,5},{5,1},{2,6},{6,2},{3,7},{7,3},{8,12},{12,8},{9,1... | collective-permute-start | bytes 2949128 | tf_op jit(solution)/shard_map/ppermute | solution.py:19
  296.6 32.9 %collective-permute-start.46 = (bf16[2,384,640]{2,1,0:T(8,128)(2,1)S(1)}, bf16[2,384,640]{2,1,0:T(8,128)(2,1)}, u32[]{:S(2)}, u32[]{:S(2)}) collective-permute-start(bf16[2,384,640]{2,1,0:T(8,128)(2,1)S(1)} %broadcast_select_fusion.6), channel_id=1, source_target_pairs={{0,16},{16,0},{1,17},{17,1},{2,18},{18,2},{3,19},{19,3},{4,20},{20... | collective-permute-start | bytes 2949128 | tf_op jit(solution)/shard_map/ppermute | solution.py:19
  337.4 21.1 %collective-permute-start.44 = (bf16[2,256,640]{2,1,0:T(8,128)(2,1)}, bf16[2,256,640]{2,1,0:T(8,128)(2,1)}, u32[]{:S(2)}, u32[]{:S(2)}) collective-permute-start(bf16[2,256,640]{2,1,0:T(8,128)(2,1)} %get-tuple-element.270), channel_id=1, source_target_pairs={{0,8},{8,0},{1,9},{9,1},{2,10},{10,2},{3,11},{11,3},{4,12},{12,4},... | collective-permute-start | bytes 1966088 | tf_op jit(solution)/shard_map/ppermute | solution.py:19
  363.4 21.6 %collective-permute-start.54 = (bf16[2,336,640]{2,1,0:T(8,128)(2,1)}, bf16[2,336,640]{2,1,0:T(8,128)(2,1)}, u32[]{:S(2)}, u32[]{:S(2)}) collective-permute-start(bf16[2,336,640]{2,1,0:T(8,128)(2,1)} %get-tuple-element.368), channel_id=1, source_target_pairs={{0,16},{16,0},{1,17},{17,1},{2,18},{18,2},{3,19},{19,3},{4,20},{20... | collective-permute-start | bytes 2580488 | tf_op jit(solution)/shard_map/ppermute | solution.py:19
  365.8 99.9 %all-reduce.7.cloned.1.call-start = ((), (), s32[]{:S(2)}) async-start(), calls=%async_computation.1 | async-start | bytes 1720320 | tf_op jit(solution)/shard_map/psum | solution.py:828
  387.2 27.7 %collective-permute-start.56 = (bf16[336,640]{1,0:T(8,128)(2,1)}, bf16[336,640]{1,0:T(8,128)(2,1)}, u32[]{:S(2)}, u32[]{:S(2)}) collective-permute-start(bf16[336,640]{1,0:T(8,128)(2,1)} %slice_bitcast_fusion.3), channel_id=1, source_target_pairs={{0,4},{4,0},{1,5},{5,1},{2,6},{6,2},{3,7},{7,3},{8,12},{12,8},{9,1... | collective-permute-start | bytes 1290248 | tf_op jit(solution)/shard_map/ppermute | solution.py:19
  389.9 75.9 %collective-permute-start.58 = (bf16[1024,640]{1,0:T(8,128)(2,1)}, bf16[1024,640]{1,0:T(8,128)(2,1)}, u32[]{:S(2)}, u32[]{:S(2)}) collective-permute-start(bf16[1024,640]{1,0:T(8,128)(2,1)} %maximum_select_fusion), channel_id=1, source_target_pairs={{0,16},{16,0},{1,17},{17,1},{2,18},{18,2},{3,19},{19,3},{4,20},{20... | collective-permute-start | bytes 3932168 | tf_op jit(solution)/shard_map/ppermute | solution.py:19
  415.9 49.8 %collective-permute-start.57 = (bf16[768,640]{1,0:T(8,128)(2,1)}, bf16[768,640]{1,0:T(8,128)(2,1)}, u32[]{:S(2)}, u32[]{:S(2)}) collective-permute-start(bf16[768,640]{1,0:T(8,128)(2,1)} %broadcast_select_fusion.5), channel_id=1, source_target_pairs={{0,16},{16,0},{1,17},{17,1},{2,18},{18,2},{3,19},{19,3},{4,20},{20... | collective-permute-start | bytes 2949128 | tf_op jit(solution)/shard_map/ppermute | solution.py:19
  (122 other events, 1036.9 us)
Sparse Core Ops, SparseCore 0:
  365.9 48.8 all-reduce.4
  420.9 44.8 all-reduce.6
